TPU v7x, 32 devices: a whole 2x2x4 slice. The times are simulated.
32 devices in a mesh: group: 2 (over x), seq: 16 (over z, y, core).
Axes of the slice: x: 2, y: 2, z: 4, core: 2. Of those that a mesh axis runs over, the one named last changes fastest.
Arguments:
- tokens: bfloat16 [256, 8192], P('group', 'seq'), parts along dimension 0, may hold values from -1700 to 1700
- gain: bfloat16 [8192], P('seq'), may hold values from 0.099609375 to 1.8984375
- w_query: bfloat16 [8192, 8192], P('seq'), may hold values from -0.0625 to 0.0625
- w_key: bfloat16 [1024, 8192], P('seq'), may hold values from -0.375 to 0.375
- w_value: bfloat16 [1024, 8192], P('seq'), may hold values from -0.0625 to 0.0625
- w_out: bfloat16 [8192, 8192], P('seq'), may hold values from -0.09375 to 0.09375
- prefix_cache: bfloat16 [2, 8192, 1024], P(None, ('group', 'seq')), parts along dimension 1, may hold values from -2700 to 2700
Outputs:
- mixed: bfloat16 [256, 8192], P('group', 'seq'), parts along dimension 0
There are 2 independent parts, one for each index of `group`. A program takes and returns all parts, laid end to end along the dimension named above; an argument that names none is the same for every part. Nothing has to cross between parts.
All inputs are finite; a program needn't handle non-finite values.
Results may differ from a plain program's by a relative error of at most 0.014.
The roundings to bfloat16 on the way count: a program that leaves them out, or rounds other values in their place, can miss the bound.
Values may be sent and summed in bfloat16 or wider, within the bound.
No kernel may reach another device: no remote copies, remote signals or barrier semaphores. Data moves between devices by JAX's collectives and lax.ppermute only.
A program may use at most 64 MiB of HBM per device.

v0:
```python
import math

import jax
import jax.numpy as jnp
from jax import lax
from jax.sharding import PartitionSpec as P

H = 64
KV = 8
DH = 128


def body(tokens, gain, w_query, w_key, w_value, w_out, prefix_cache):
    contract_dims = (((1,), (1,)), ((), ()))
    row_count = tokens.shape[0]
    whole, gain_all = (
        lax.all_gather(tokens, "seq", axis=1, tiled=True),
        lax.all_gather(gain, "seq", axis=0, tiled=True),
    )
    wide_tokens = whole.astype(jnp.float32)
    inverse = lax.rsqrt(jnp.mean(wide_tokens * wide_tokens, axis=1, keepdims=True) + 1e-05)
    normed = (wide_tokens * inverse * gain_all.astype(jnp.float32)).astype(jnp.bfloat16)
    query_part = lax.dot_general(normed, w_query, contract_dims, preferred_element_type=jnp.float32)
    key_part = lax.dot_general(normed, w_key, contract_dims, preferred_element_type=jnp.float32)
    value_part = lax.dot_general(normed, w_value, contract_dims, preferred_element_type=jnp.float32)
    query, key_own, value_own = (
        lax.all_gather(query_part.astype(jnp.bfloat16), "seq", axis=1, tiled=True),
        lax.all_gather(key_part.astype(jnp.bfloat16), "seq", axis=1, tiled=True),
        lax.all_gather(value_part.astype(jnp.bfloat16), "seq", axis=1, tiled=True),
    )
    group_size = H // KV
    score_scale = 1.0 / math.sqrt(DH)
    positions_here = prefix_cache.shape[1]
    query_heads = query.reshape(row_count, KV, group_size, DH)
    key_heads = key_own.reshape(row_count, KV, DH)
    own_scores = (
        jnp.einsum("rgjd,rgd->rgj", query_heads, key_heads, preferred_element_type=jnp.float32)
        * score_scale
    )
    prefix_keys = prefix_cache[0].reshape(positions_here, KV, DH)
    prefix_values = prefix_cache[1].reshape(positions_here, KV, DH)
    scores = (
        jnp.einsum("rgjd,pgd->grjp", query_heads, prefix_keys, preferred_element_type=jnp.float32)
        * score_scale
    )
    local_max = jnp.maximum(jnp.transpose(jnp.max(scores, axis=3), (1, 0, 2)), own_scores).reshape(
        row_count, H
    )
    row_max = lax.pmax(local_max.astype(jnp.bfloat16), "seq").astype(local_max.dtype)
    max_groups = row_max.reshape(row_count, KV, group_size)
    numer_list = []
    denom_list = []
    for head_group in range(KV):
        weights = jnp.exp(scores[head_group] - max_groups[:, head_group, :, None])
        denom_list.append(jnp.sum(weights, axis=2))
        numer_list.append(
            jnp.einsum(
                "rjp,pd->rjd",
                weights.astype(jnp.bfloat16),
                prefix_values[:, head_group],
                preferred_element_type=jnp.float32,
            )
        )
    numerator = jnp.stack(numer_list, axis=1).reshape(row_count, H, DH)
    denominator = jnp.stack(denom_list, axis=1).reshape(row_count, H)
    device = lax.axis_index("seq")
    local_heads = H // lax.axis_size("seq")
    first_head = device * local_heads
    numer_mine, denom_mine = (
        lax.psum_scatter(numerator, "seq", scatter_dimension=1, tiled=True),
        lax.psum_scatter(denominator, "seq", scatter_dimension=1, tiled=True),
    )
    max_mine = lax.dynamic_slice_in_dim(row_max, first_head, local_heads, 1)
    own_mine = lax.dynamic_slice_in_dim(
        own_scores.reshape(row_count, H), first_head, local_heads, 1
    )
    head_numbers = first_head + jnp.arange(local_heads, dtype=jnp.int32)
    select = (
        (head_numbers // group_size)[:, None] == jnp.arange(KV, dtype=jnp.int32)[None, :]
    ).astype(jnp.float32)
    value_heads = jnp.einsum(
        "rgd,hg->rhd", value_own.reshape(row_count, KV, DH).astype(jnp.float32), select
    )
    own_weight = jnp.exp(own_mine - max_mine)
    denom_all = denom_mine + own_weight
    rounded = lax.optimization_barrier(own_weight.astype(jnp.bfloat16)).astype(jnp.float32)
    numer_all = numer_mine + rounded[..., None] * value_heads
    attention = (
        (numer_all / denom_all[..., None]).astype(jnp.bfloat16).reshape(row_count, local_heads * DH)
    )
    mixed = lax.psum_scatter(
        lax.dot_general(
            w_out, attention, (((0,), (1,)), ((), ())), preferred_element_type=jnp.float32
        ),
        "seq",
        scatter_dimension=0,
        tiled=True,
    )
    return jnp.transpose(mixed).astype(jnp.bfloat16)


def solution(mesh):
    return jax.shard_map(
        body,
        mesh=mesh,
        in_specs=(
            P("group", "seq"),
            P("seq"),
            P("seq", None),
            P("seq", None),
            P("seq", None),
            P("seq", None),
            P(None, ("group", "seq"), None),
        ),
        out_specs=P("group", "seq"),
        check_vma=False,
    )
```

profile of v0, /device:TPU:0, one launch (start us, length us, event | category | flops | bytes accessed | tf_op | source)
XLA Modules:
  0.0 366.6 jit_solution(5957612537099877847)
XLA Ops:
  8.0 23.1 %all-gather = bf16[16,1,512]{2,1,0:T(2,128)(2,1)S(1)} all-gather(bf16[1,1,512]{2,1,0:T(2,128)(2,1)S(1)} %reshape.80), channel_id=1, replica_groups=mesh['group'=2,'seq'=16] {'seq'}, dimensions={0}, use_global_device_ids=true | all-gather | bytes 17408 | tf_op jit(solution)/shard_map/all_gather | solution.py:18
  31.2 22.3 %all-gather.4.cloned.1.call-done = bf16[128,8192]{1,0:T(8,128)(2,1)} async-done(((bf16[128,512]{1,0:T(8,128)(2,1)}), bf16[128,8192]{1,0:T(8,128)(2,1)}) %all-gather.4.cloned.1.call-update) | async-done | bytes 2097168 | tf_op jit(solution)/shard_map/all_gather | solution.py:17
  53.4 2.1 fusion
  55.5 7.7 %convolution_convert_fusion = bf16[128,512]{1,0:T(8,128)(2,1)} fusion(bf16[512,8192]{1,0:T(8,128)(2,1)} %param.9, bf16[128,8192]{1,0:T(8,128)(2,1)} %all-gather.4.cloned.1.call-done, f32[8192]{0:T(1024)S(1)} %bitcast.248, f32[128]{0:T(128)S(1)} %add_rsqrt_fusion), kind=kOutput, calls=%fused_computation.30 | convolution fusion | flops 1078001664 | bytes 10650112 | tf_op jit(solution)/shard_map/dot_general | solution.py:23
  63.8 2.5 convolution_convert_fusion.2
  66.3 20.1 %all_gather.18 = bf16[128,1024]{0,1:T(8,128)(2,1)S(1)} all-gather(bf16[128,64]{0,1:T(8,128)(2,1)S(1)} %convolution_convert_fusion.2), channel_id=1, replica_groups=mesh['group'=2,'seq'=16] {'seq'}, dimensions={1}, use_global_device_ids=true | all-gather | bytes 278528 | tf_op jit(solution)/shard_map/all_gather | solution.py:28
  86.6 17.5 %all-gather.6.cloned.1.call-done = bf16[128,8192]{1,0:T(8,128)(2,1)} async-done(((bf16[128,512]{1,0:T(8,128)(2,1)}), bf16[128,8192]{1,0:T(8,128)(2,1)}) %all-gather.6.cloned.1.call-update) | async-done | bytes 2097168 | tf_op jit(solution)/shard_map/all_gather | solution.py:27
  104.1 2.2 copy.65
  106.3 6.3 %fusion.69 = (bf16[8,128,8]{1,2,0:T(8,128)(2,1)S(1)}, f32[8,128,8,256]{3,1,2,0:T(8,128)}) fusion(bf16[256,8,128,1]{0,2,3,1:T(8,128)(2,1)S(1)} %bitcast.243, bf16[128,8,8,128]{3,2,1,0:T(8,128)(2,1)S(1)} %bitcast.232), kind=kOutput, calls=%fused_computation.126 | convolution fusion | flops 541057024 | bytes 11026432 | tf_op jit(solution)/shard_map/rgjd,pgd->grjp/dot_general | solution.py:43
  114.0 59.7 %pmax.7 = bf16[128,64]{0,1:T(8,128)(2,1)S(1)} all-reduce(bf16[128,64]{0,1:T(8,128)(2,1)S(1)} %fusion.59), channel_id=1, replica_groups=mesh['group'=2,'seq'=16] {'seq'}, use_global_device_ids=true, to_apply=%region_2.0 | all-reduce | flops 8192 | bytes 32768 | tf_op jit(solution)/shard_map/pmax | solution.py:49
  173.7 2.4 fusion.11
  176.1 2.5 fusion.10
  178.6 2.4 fusion.9
  180.9 2.4 fusion.8
  183.3 2.4 fusion.7
  185.7 2.5 fusion.6
  188.2 2.4 fusion.5
  190.6 2.4 fusion.4
  194.3 2.6 convolution_convert_fusion.1
  197.0 17.8 %all_gather.19 = bf16[128,1024]{0,1:T(8,128)(2,1)S(1)} all-gather(bf16[128,64]{0,1:T(8,128)(2,1)S(1)} %convolution_convert_fusion.1), channel_id=1, replica_groups=mesh['group'=2,'seq'=16] {'seq'}, dimensions={1}, use_global_device_ids=true | all-gather | bytes 278528 | tf_op jit(solution)/shard_map/all_gather | solution.py:29
  215.0 4.6 %fusion.17 = (f32[128,8]{0,1:T(8,128)S(1)}, f32[128,8]{0,1:T(8,128)S(1)}, f32[128,8]{0,1:T(8,128)S(1)}, f32[128,8]{0,1:T(8,128)S(1)}, f32[128,8]{0,1:T(8,128)S(1...) fusion(f32[8,128,8,256]{3,1,2,0:T(8,128)} %get-tuple-element.28, ...), kind=kLoop, calls=%fused_computation.35 | loop fusion | flops 4186112 | bytes 8454144 | tf_op jit(solution)/shard_map/reduce_sum | solution.py:55
  219.7 60.7 %all-reduce = f32[128,64]{0,1:T(8,128)S(1)} all-reduce(f32[128,64]{0,1:T(8,128)S(1)} %bitcast.247), channel_id=3, replica_groups=mesh['group'=2,'seq'=16] {'seq'}, use_global_device_ids=true, to_apply=%region_12.0.clone | all-reduce | flops 8192 | bytes 65536
  282.0 6.6 %convolution_bitcast_fusion = f32[8192,128]{0,1:T(8,128)} fusion(bf16[512,8192]{1,0:T(8,128)(2,1)} %param.12, bf16[16,8,4,128]{3,2,1,0:T(4,128)(2,1)S(1)} %bitcast.246), kind=kOutput, calls=%fused_computation | convolution fusion | flops 1073741824 | bytes 12713984 | tf_op jit(solution)/shard_map/dot_general | solution.py:92
  288.6 69.8 %reduce-scatter.5.cloned.1.call-done = f32[512,128]{0,1:T(8,128)} async-done(((f32[8192,128]{0,1:T(8,128)}), f32[512,128]{0,1:T(8,128)}) %reduce-scatter.5.cloned.1.call-update) | async-done | bytes 262160 | tf_op jit(solution)/shard_map/reduce_scatter | solution.py:91
  (46 shorter events, 7.8 us)
Async XLA Ops:
  6.5 57.3 %copy-start = (bf16[64,8192]{1,0:T(8,128)(2,1)S(1)}, bf16[64,8192]{1,0:T(8,128)(2,1)}, u32[]{:S(2)}) copy-start(bf16[64,8192]{1,0:T(8,128)(2,1)} %param.10) | copy-start | bytes 3145732
  6.5 46.9 %all-gather.4.cloned.1.call-start = ((), (), s32[]{:S(2)}) async-start(), calls=%async_computation.2 | async-start | bytes 2228224 | tf_op jit(solution)/shard_map/all_gather | solution.py:17
  7.3 96.9 %all-gather.6.cloned.1.call-start = ((), (), s32[]{:S(2)}) async-start(), calls=%async_computation.3 | async-start | bytes 2228224 | tf_op jit(solution)/shard_map/all_gather | solution.py:27
  55.5 7.8 %copy-start.1 = (bf16[2,256,1024]{2,1,0:T(8,128)(2,1)S(1)}, bf16[2,256,1024]{2,1,0:T(8,128)(2,1)}, u32[]{:S(2)}) copy-start(bf16[2,256,1024]{2,1,0:T(8,128)(2,1)} %param.13) | copy-start | bytes 3145732
  63.3 217.3 %reduce-scatter.3.cloned.1.call-start = ((), (), s32[]{:S(2)}) async-start(), calls=%async_computation.4 | async-start | bytes 4456448 | tf_op jit(solution)/shard_map/reduce_scatter | solution.py:70
  185.7 7.3 %copy-start.3 = (u32[32]{0:T(128)S(1)}, u32[32]{0:T(128)}, u32[]{:S(2)}) copy-start(u32[32]{0:T(128)} %constant.40) | copy-start | bytes 388
  185.7 8.6 %copy-start.2 = (bf16[64,8192]{1,0:T(8,128)(2,1)S(1)}, bf16[64,8192]{1,0:T(8,128)(2,1)}, u32[]{:S(2)}) copy-start(bf16[64,8192]{1,0:T(8,128)(2,1)} %param.11) | copy-start | bytes 3145732
  193.0 165.4 %reduce-scatter.5.cloned.1.call-start = ((), (), s32[]{:S(2)}) async-start(), calls=%async_computation.5 | async-start | bytes 4456448 | tf_op jit(solution)/shard_map/reduce_scatter | solution.py:91
Sparse Core Ops, SparseCore 0:
  9.5 43.8 all-gather.3
  63.4 40.7 all-gather.5
  193.1 70.3 reduce-scatter.2
  288.7 69.6 reduce-scatter.4
where the time goes:
time: 367 us
  blocking collectives  181 us (49%)
  waiting for transfers between devices  110 us (30%)
  matrix products  46.3 us (13%)
  between operations  14 us (4%)
  other arithmetic  9.59 us (3%)
  local copies, waits for them, and re-layouts  4.79 us (1%)
    reduce_scatter x1, waiting for transfers between devices, body(): lax.psum_scatter(lax.dot_general(w_out, attention, (((0,), (1,)), ((), ()...  69.8 us
    unnamed x1, blocking collectives  60.7 us
    pmax x1, blocking collectives, body(): lax.pmax(local_max.astype(jnp.bfloat16), 'seq').astype(local_max.dtype)  59.7 us
    all_gather x1, blocking collectives, body(): lax.all_gather(gain, 'seq', axis=0, tiled=True)  23.1 us
    all_gather x1, waiting for transfers between devices, body(): lax.all_gather(tokens, 'seq', axis=1, tiled=True)  22.3 us
    all_gather x1, blocking collectives, body(): lax.all_gather(key_part.astype(jnp.bfloat16), 'seq', axis=1, tiled=True)  20.1 us
    dot_general x8, matrix products, body(): jnp.einsum('rjp,pd->rjd', weights.astype(jnp.bfloat16), prefix_values[:,...  19.3 us
    all_gather x1, blocking collectives, body(): lax.all_gather(value_part.astype(jnp.bfloat16), 'seq', axis=1, tiled=True)  17.8 us
  transfers between devices with their start and end apart: 4, of which 3 were waited for; matrix products, arithmetic and copies ran while one was open for 3% of the time, Pallas kernels for 0%

commit v1 on v0

v1 whole, which is shorter than its diff:
```python
import functools
import math

import jax
import jax.numpy as jnp
from jax import lax
from jax.experimental import pallas as pl
from jax.experimental.pallas import tpu as pltpu
from jax.sharding import PartitionSpec as P

H = 64
KV = 8
DH = 128
EPS = 1e-05
PAD = 16
MIB = 1 << 20
TRANS_B = (((1,), (1,)), ((), ()))


def vmem_specs(count):
    return [pl.BlockSpec(memory_space=pltpu.VMEM)] * count


def project_kernel(count, rows, owner_ref, *refs):
    blocks, (w_query, w_key, w_value, query_ref, own_ref) = refs[:count], refs[count:]
    width = blocks[0].shape[1]
    total = jnp.zeros((rows, 1), jnp.float32)
    for block in blocks:
        wide = block[:rows, :].astype(jnp.float32)
        total += jnp.sum(wide * wide, axis=1, keepdims=True)
    inverse = lax.rsqrt(total / (width * count) + EPS)
    query = jnp.zeros(query_ref.shape, jnp.float32)
    key = jnp.zeros((rows, w_key.shape[0]), jnp.float32)
    value = jnp.zeros((rows, w_key.shape[0]), jnp.float32)
    for number, block in enumerate(blocks):
        gain = block[rows : rows + PAD, :].astype(jnp.float32)[0:1, :]
        wide = block[:rows, :].astype(jnp.float32)
        normed = (wide * inverse * gain).astype(jnp.bfloat16)
        columns = pl.ds(pl.multiple_of(owner_ref[number] * width, width), width)
        query += lax.dot_general(normed, w_query[:, columns], TRANS_B, preferred_element_type=jnp.float32)
        key += lax.dot_general(normed, w_key[:, columns], TRANS_B, preferred_element_type=jnp.float32)
        value += lax.dot_general(normed, w_value[:, columns], TRANS_B, preferred_element_type=jnp.float32)
    query_ref[...] = query.astype(jnp.bfloat16)
    own_ref[...] = jnp.concatenate([key, value], axis=1).astype(jnp.bfloat16)


def project(owners, blocks, w_query, w_key, w_value, rows):
    count = len(blocks)
    return pl.pallas_call(
        functools.partial(project_kernel, count, rows),
        out_shape=(
            jax.ShapeDtypeStruct((rows, w_query.shape[0]), jnp.bfloat16),
            jax.ShapeDtypeStruct((rows, 2 * w_key.shape[0]), jnp.bfloat16),
        ),
        in_specs=[pl.BlockSpec(memory_space=pltpu.SMEM)] + vmem_specs(count + 3),
        out_specs=tuple(vmem_specs(2)),
        compiler_params=pltpu.CompilerParams(vmem_limit_bytes=48 * MIB),
        name="project",
    )(owners, *blocks, w_query, w_key, w_value)


def attend_kernel(count, heads, *refs):
    caches, (query_ref, own_key, own_value, out_ref, query_all, scores) = refs[:count], refs[count:]
    rows = query_ref.shape[0]
    scale = 1.0 / math.sqrt(DH)
    for head in range(heads):
        query_all[head * rows : (head + 1) * rows, :] = query_ref[:, head * DH : (head + 1) * DH]
    query = query_all[...]
    keys_own = jnp.concatenate([own_key[...].astype(jnp.float32)] * heads, axis=0)
    values_own = jnp.concatenate([own_value[...].astype(jnp.float32)] * heads, axis=0)
    own = jnp.sum(query.astype(jnp.float32) * keys_own, axis=1, keepdims=True) * scale
    step = caches[0].shape[1]
    best = None
    for number, cache in enumerate(caches):
        part = lax.dot_general(query, cache[0], TRANS_B, preferred_element_type=jnp.float32)
        scores[:, number * step : (number + 1) * step] = part
        for lane in range(0, step, 128):
            piece = part[:, lane : lane + 128]
            best = piece if best is None else jnp.maximum(best, piece)
    top = jnp.maximum(jnp.max(best, axis=1, keepdims=True) * scale, own)
    total = jnp.zeros((heads * rows, 128), jnp.float32)
    numerator = jnp.zeros((heads * rows, DH), jnp.float32)
    for number, cache in enumerate(caches):
        weights = jnp.exp(scores[:, number * step : (number + 1) * step] * scale - top)
        for lane in range(0, step, 128):
            total += weights[:, lane : lane + 128]
        numerator += jnp.dot(weights.astype(jnp.bfloat16), cache[1], preferred_element_type=jnp.float32)
    own_weight = jnp.exp(own - top)
    denominator = jnp.sum(total, axis=1, keepdims=True) + own_weight
    rounded = own_weight.astype(jnp.bfloat16).astype(jnp.float32)
    result = ((numerator + rounded * values_own) / denominator).astype(jnp.bfloat16)
    for head in range(heads):
        out_ref[:, head * DH : (head + 1) * DH] = result[head * rows : (head + 1) * rows, :]


def attend(caches, query, own_key, own_value):
    count, rows = len(caches), query.shape[0]
    heads = query.shape[1] // DH
    positions = count * caches[0].shape[1]
    return pl.pallas_call(
        functools.partial(attend_kernel, count, heads),
        out_shape=jax.ShapeDtypeStruct(query.shape, jnp.bfloat16),
        in_specs=vmem_specs(count + 3),
        out_specs=pl.BlockSpec(memory_space=pltpu.VMEM),
        scratch_shapes=[
            pltpu.VMEM((heads * rows, DH), jnp.bfloat16),
            pltpu.VMEM((heads * rows, positions), jnp.float32),
        ],
        compiler_params=pltpu.CompilerParams(vmem_limit_bytes=48 * MIB),
        name="attend",
    )(*caches, query, own_key, own_value)


def body(tokens, gain, w_query, w_key, w_value, w_out, prefix_cache, size):
    chips = size // 2
    outer = chips // 2
    cycle = [2 * a for a in range(outer)] + [2 * a + 1 for a in reversed(range(outer))]
    place_of = {chip: place for place, chip in enumerate(cycle)}
    places = jnp.array([place_of[chip] for chip in range(chips)], jnp.int32)
    cycle_array = jnp.array(cycle, jnp.int32)
    device = lax.axis_index("seq")
    chip, core = device // 2, device % 2
    place = places[chip]

    def around(value, step):
        pairs = [
            (2 * cycle[p] + k, 2 * cycle[(p + step) % chips] + k) for p in range(chips) for k in (0, 1)
        ]
        return lax.ppermute(value, "seq", pairs)

    def swap(value, bit):
        return lax.ppermute(value, "seq", [(i, i ^ bit) for i in range(size)])

    rows = tokens.shape[0]
    width = tokens.shape[1]

    positions = prefix_cache.shape[1]
    heads_here = jnp.repeat(prefix_cache.reshape(2, positions, KV, DH), chips // KV, axis=2) if chips > KV else prefix_cache.reshape(2, positions, KV, DH)
    by_chip = heads_here.reshape(2, positions, outer, 2, DH)
    inner = chip % 2
    to_keep = lax.dynamic_index_in_dim(by_chip, inner, 3, keepdims=False)
    to_send = lax.dynamic_index_in_dim(by_chip, 1 - inner, 3, keepdims=False)
    from_side = swap(to_send, 2)
    caches = []
    for step in range(outer):
        target = (chip // 2) ^ step
        for source in (to_keep, from_side):
            part = lax.dynamic_index_in_dim(source, target, 2, keepdims=False)
            part = swap(part, 4 * step) if step else part
            caches += [part, swap(part, 1)]

    block = jnp.concatenate([tokens, jnp.broadcast_to(gain[None, :], (PAD, width))], axis=0)
    blocks, owners = [], []

    def take(value, offset):
        owner = cycle_array[(place + offset) % chips]
        blocks.extend([value, swap(value, 1)])
        owners.extend([2 * owner + core, 2 * owner + 1 - core])

    take(block, 0)
    right = left = block
    for step in range(1, chips // 2 + 1):
        right = around(right, 1)
        take(right, chips - step)
        if step < chips // 2:
            left = around(left, -1)
            take(left, step)
    owners = jnp.stack(owners).astype(jnp.int32)
    query, own = project(owners, blocks, w_query, w_key, w_value, rows)

    local_heads = H // size
    sharers = size // KV
    half = own.shape[1] // 2
    own_parts = [own] if sharers == 1 else None
    if sharers == 2:
        other = swap(own, 1)
        first = jnp.where(core == 0, own, other)
        second = jnp.where(core == 0, other, own)
        own_parts = [first, second]
    elif own_parts is None:
        gathered = lax.all_gather(own, "seq", axis=0, axis_index_groups=[list(range(g * sharers, (g + 1) * sharers)) for g in range(KV)])
        own_parts = [gathered[i] for i in range(sharers)]
    own_key = jnp.concatenate([part[:, :half] for part in own_parts], axis=1)
    own_value = jnp.concatenate([part[:, half:] for part in own_parts], axis=1)
    attention = attend(caches, query, own_key, own_value)

    features = w_out.shape[1] // size
    partial = jnp.dot(attention, w_out, preferred_element_type=jnp.float32)
    partial = partial.astype(jnp.bfloat16).reshape(rows, chips, 2, features)
    mine = lax.dynamic_index_in_dim(partial, core, 2, keepdims=False)
    others = lax.dynamic_index_in_dim(partial, 1 - core, 2, keepdims=False)
    summed = mine.astype(jnp.float32) + swap(others, 1).astype(jnp.float32)

    def for_place(offset):
        target = cycle_array[(place + offset) % chips]
        return lax.dynamic_index_in_dim(summed, target, 1, keepdims=False)

    right = left = None
    for step in reversed(range(1, chips // 2 + 1)):
        term = for_place(step)
        right = term if right is None else right.astype(jnp.float32) + term
        right = around(right.astype(jnp.bfloat16), 1)
        if step < chips // 2:
            term = for_place(chips - step)
            left = term if left is None else left.astype(jnp.float32) + term
            left = around(left.astype(jnp.bfloat16), -1)
    return (for_place(0) + right.astype(jnp.float32) + left.astype(jnp.float32)).astype(jnp.bfloat16)


def solution(mesh):
    return jax.shard_map(
        functools.partial(body, size=mesh.shape["seq"]),
        mesh=mesh,
        in_specs=(
            P("group", "seq"),
            P("seq"),
            P("seq", None),
            P("seq", None),
            P("seq", None),
            P("seq", None),
            P(None, ("group", "seq"), None),
        ),
        out_specs=P("group", "seq"),
        check_vma=False,
    )
```

time: 367 us -> 140 us (0.38)
  blocking collectives: 181 us -> 0 us
  waiting for transfers between devices: 110 us -> 29.7 us
  matrix products: 46.3 us -> 2.62 us
  starting transfers between devices: 0.12 us -> 30.8 us
  local copies, waits for them, and re-layouts: 4.79 us -> 28.3 us
  Pallas kernels: 0 us -> 13.2 us
  between operations: 14 us -> 27 us
    reduce_scatter x2 -> x0, waiting for transfers between devices: 69.8 us -> none  [the longest x1 69.8 us: body(): lax.psum_scatter(lax.dot_general(w_out, attention, (((0,), (1,)), ((), ()...]
    all_gather x3 -> x0, blocking collectives: 61.1 us -> none  [the longest x1 23.1 us: body(): lax.all_gather(gain, 'seq', axis=0, tiled=True)]
    unnamed x1 -> x0, blocking collectives: 60.7 us -> none
    pmax x1 -> x0, blocking collectives: 59.7 us -> none  [body(): lax.pmax(local_max.astype(jnp.bfloat16), 'seq').astype(local_max.dtype)]
    dot_general x14 -> x1, matrix products: 46.3 us -> 2.62 us  [body(): partial = jnp.dot(attention, w_out, preferred_element_type=jnp.float32)]
    all_gather x2 -> x0, waiting for transfers between devices: 39.8 us -> none  [the longest x1 22.3 us: body(): lax.all_gather(tokens, 'seq', axis=1, tiled=True)]
    ppermute x0 -> x39, starting transfers between devices: none -> 30.8 us  [the longest x14 16.4 us: around(): return lax.ppermute(value, 'seq', pairs)]
    ppermute x0 -> x39, waiting for transfers between devices: none -> 29.7 us  [the longest x14 19.9 us: around(): return lax.ppermute(value, 'seq', pairs)]
  transfers between devices with their start and end apart: 4 -> 39, of which waited for: 3 -> 12; matrix products, arithmetic and copies ran while one was open for 3% -> 10% of each run, Pallas kernels for 0% -> 6%
where the time goes in v1:
time: 140 us; the launch traced here: 139 us
  starting transfers between devices  30.8 us (22%)
  waiting for transfers between devices  29.7 us (21%)
  local copies, waits for them, and re-layouts  28.3 us (20%)
  between operations  27 us (19%)
  Pallas kernels  13.2 us (9%)
  other arithmetic  7.14 us (5%)
  matrix products  2.62 us (2%)
    ppermute x14, waiting for transfers between devices, around(): return lax.ppermute(value, 'seq', pairs)  19.9 us
    ppermute x14, starting transfers between devices, around(): return lax.ppermute(value, 'seq', pairs)  16.4 us
    ppermute x25, starting transfers between devices, swap(): return lax.ppermute(value, 'seq', [(i, i ^ bit) for i in range(size)])  14.4 us
    ppermute x25, waiting for transfers between devices, swap(): return lax.ppermute(value, 'seq', [(i, i ^ bit) for i in range(size)])  9.87 us
    pallas_call x1, Pallas kernels, project(): pl.pallas_call(functools.partial(project_kernel, count, rows), out_shape=...  8.35 us
    unnamed x26, local copies, waits for them, and re-layouts  6.24 us
    dynamic_slice x1, local copies, waits for them, and re-layouts, body(): mine = lax.dynamic_index_in_dim(partial, core, 2, keepdims=False)  5.81 us
    pallas_call x1, Pallas kernels, attend(): pl.pallas_call(functools.partial(attend_kernel, count, heads), out_shape=...  4.84 us
  transfers between devices with their start and end apart: 39, of which 12 were waited for; matrix products, arithmetic and copies ran while one was open for 10% of the time, Pallas kernels for 6%

profile of v1, /device:TPU:0, one launch (start us, length us, event | category | flops | bytes accessed | tf_op | source)
XLA Modules:
  0.0 138.8 jit_solution(17094438637536022433)
XLA Ops:
  1.6 3.1 %collective-permute-start.16 = (bf16[144,512]{1,0:T(8,128)(2,1)S(1)}, bf16[144,512]{1,0:T(8,128)(2,1)S(1)}, u32[]{:S(2)}, u32[]{:S(2)}) collective-permute-start(bf16[144,512]{1,0:T(8,128)(2,1)S(1)} %pad_maximum_fusion.refs_0_), channel_id=1, source_target_pairs={{0,4},{1,5},{4,8},{5,9},{8,12},{9,13},{12,14},{13,15},{14,10},{15,... | collective-permute-start | bytes 442376 | tf_op jit(solution)/shard_map/ppermute | solution.py:129
  4.7 1.8 %reshape_reshape.3 = bf16[2,256,4,2,128]{4,3,2,1,0:T(2,128)(2,1)S(1)} reshape(bf16[2,256,1024]{2,1,0:T(8,128)(2,1)} %param.15) | data formatting | bytes 2097152 | tf_op jit(solution)/shard_map/reshape;reshape | solution.py:139
  6.5 1.9 %constant_dynamic-slice_fusion.2 = (bf16[2,256,1,1,128]{4,3,2,1,0:T(2,128)(2,1)}, bf16[2,256,1,1,128]{4,3,2,1,0:T(2,128)(2,1)S(1)}, bf16[2,256,1,1,128]{4,3,2,1,0:T(2,128)(2,1)S(1)}, bf16[2,256,1,1,128]{4,3,2,1,0:T(2,128)(2,1)}) fusion(bf16[2,256,4,2,128]{4,3,2,1,0:T(2,128)(2,1)S(1)} %reshape_reshape.3, s32[]{:T(128)S(6)} %select_n.195, s32[]{:T(128)S(6)} %select_n.188, ...), kind=kLoop, calls=%fused_computation.37 | loop fusion | bytes 1048596 | tf_op jit(solution)/shard_map/jit(dynamic_index_in_dim)/dynamic_slice | solution.py:148
  8.4 2.1 %collective-permute-start.3 = (bf16[2,256,128]{2,1,0:T(8,128)(2,1)S(1)}, bf16[2,256,128]{2,1,0:T(8,128)(2,1)}, u32[]{:S(2)}, u32[]{:S(2)}) collective-permute-start(bf16[2,256,128]{2,1,0:T(8,128)(2,1)S(1)} %bitcast.92), channel_id=1, source_target_pairs={{0,4},{1,5},{2,6},{3,7},{4,0},{5,1},{6,2},{7,3},{8,12},{9,13},{10,... | collective-permute-start | bytes 393224 | tf_op jit(solution)/shard_map/ppermute | solution.py:132
  10.5 2.7 %collective-permute-start.7 = (bf16[2,256,128]{2,1,0:T(8,128)(2,1)S(1)}, bf16[2,256,128]{2,1,0:T(8,128)(2,1)}, u32[]{:S(2)}, u32[]{:S(2)}) collective-permute-start(bf16[2,256,128]{2,1,0:T(8,128)(2,1)S(1)} %bitcast.91), channel_id=1, source_target_pairs={{0,8},{1,9},{2,10},{3,11},{4,12},{5,13},{6,14},{7,15},{8,0},{9,1},... | collective-permute-start | bytes 393224 | tf_op jit(solution)/shard_map/ppermute | solution.py:132
  13.7 2.4 %constant_dynamic-slice_fusion.5 = bf16[2,256,4,1,128]{4,3,2,1,0:T(2,128)(2,1)S(1)} fusion(bf16[2,256,4,2,128]{4,3,2,1,0:T(2,128)(2,1)} %copy-done.5, s32[]{:T(128)S(6)} %select_n.189), kind=kLoop, calls=%fused_computation.40 | loop fusion | bytes 1048580 | tf_op jit(solution)/shard_map/jit(dynamic_index_in_dim)/dynamic_slice | solution.py:142
  19.3 2.3 %collective-permute-start.24 = (bf16[144,512]{1,0:T(8,128)(2,1)S(1)}, bf16[144,512]{1,0:T(8,128)(2,1)S(1)}, u32[]{:S(2)}, u32[]{:S(2)}) collective-permute-start(bf16[144,512]{1,0:T(8,128)(2,1)S(1)} %collective-permute-done.20.refs_6_), channel_id=1, source_target_pairs={{0,4},{1,5},{4,8},{5,9},{8,12},{9,13},{12,14},{13,15},{14,10},{15,... | collective-permute-start | bytes 442376 | tf_op jit(solution)/shard_map/ppermute | solution.py:129
  21.6 10.2 %collective-permute-done.22.refs_8_ = bf16[144,512]{1,0:T(8,128)(2,1)S(1)} collective-permute-done((bf16[144,512]{1,0:T(8,128)(2,1)S(1)}, bf16[144,512]{1,0:T(8,128)(2,1)S(1)}, u32[]{:S(2)}, u32[]{:S(2)}) %collective-permute-start.22) | collective-permute-done | bytes 147488 | tf_op jit(solution)/shard_map/ppermute | solution.py:129
  31.8 2.5 %collective-permute-start.26 = (bf16[144,512]{1,0:T(8,128)(2,1)S(1)}, bf16[144,512]{1,0:T(8,128)(2,1)}, u32[]{:S(2)}, u32[]{:S(2)}) collective-permute-start(bf16[144,512]{1,0:T(8,128)(2,1)S(1)} %collective-permute-done.22.refs_8_), channel_id=1, source_target_pairs={{0,2},{1,3},{4,0},{5,1},{8,4},{9,5},{12,8},{13,9},{14,12},{15,13},... | collective-permute-start | bytes 442376 | tf_op jit(solution)/shard_map/ppermute | solution.py:129
  34.8 2.2 %collective-permute-done.26.refs_12_ = bf16[144,512]{1,0:T(8,128)(2,1)} collective-permute-done((bf16[144,512]{1,0:T(8,128)(2,1)S(1)}, bf16[144,512]{1,0:T(8,128)(2,1)}, u32[]{:S(2)}, u32[]{:S(2)}) %collective-permute-start.26) | collective-permute-done | bytes 147488 | tf_op jit(solution)/shard_map/ppermute | solution.py:129
  38.2 2.4 %collective-permute-done.28.refs_14_ = bf16[144,512]{1,0:T(8,128)(2,1)} collective-permute-done((bf16[144,512]{1,0:T(8,128)(2,1)S(1)}, bf16[144,512]{1,0:T(8,128)(2,1)}, u32[]{:S(2)}, u32[]{:S(2)}) %collective-permute-start.28) | collective-permute-done | bytes 147488 | tf_op jit(solution)/shard_map/ppermute | solution.py:129
  59.6 8.4 %project.1 = (bf16[128,512]{1,0:T(8,128)(2,1)S(1)}, bf16[128,128]{1,0:T(8,128)(2,1)S(1)}) custom-call(s32[16]{0:T(128)S(1)} %copy-done.4, bf16[144,512]{1,0:T(8,128)(2,1)S(1)} %pad_maximum_fusion.refs_0_, bf16[144,512]{1,0:T(8,128)(2,1)S(1)} %collective-permute-done.15.refs_1_, bf16[144,512]{1,0:T(8,128)(2,1)S(1)} %collective-permute-done.16.refs_2_, ...), custom_call_target="tpu_custom_call" | custom-call | tf_op jit(solution)/shard_map/project/pallas_call | solution.py:49
  69.2 3.8 %collective-permute-start.13 = (bf16[2,256,128]{2,1,0:T(8,128)(2,1)S(1)}, bf16[2,256,128]{2,1,0:T(8,128)(2,1)S(1)}, u32[]{:S(2)}, u32[]{:S(2)}) collective-permute-start(bf16[2,256,128]{2,1,0:T(8,128)(2,1)S(1)} %get-tuple-element.21), channel_id=1, source_target_pairs={{0,12},{1,13},{2,14},{3,15},{4,8},{5,9},{6,10},{7,11},{8,4},{9,5},... | collective-permute-start | bytes 393224 | tf_op jit(solution)/shard_map/ppermute | solution.py:132
  74.5 3.1 %collective-permute-done.13.refs_14_ = bf16[2,256,128]{2,1,0:T(8,128)(2,1)S(1)} collective-permute-done((bf16[2,256,128]{2,1,0:T(8,128)(2,1)S(1)}, bf16[2,256,128]{2,1,0:T(8,128)(2,1)S(1)}, u32[]{:S(2)}, u32[]{:S(2)}) %collective-permute-start.13) | collective-permute-done | bytes 131104 | tf_op jit(solution)/shard_map/ppermute | solution.py:132
  77.5 5.9 %collective-permute-done.9.refs_10_ = bf16[2,256,128]{2,1,0:T(8,128)(2,1)S(1)} collective-permute-done((bf16[2,256,128]{2,1,0:T(8,128)(2,1)S(1)}, bf16[2,256,128]{2,1,0:T(8,128)(2,1)S(1)}, u32[]{:S(2)}, u32[]{:S(2)}) %collective-permute-start.9) | collective-permute-done | bytes 131104 | tf_op jit(solution)/shard_map/ppermute | solution.py:132
  85.0 4.8 %attend.1 = bf16[128,512]{1,0:T(8,128)(2,1)S(1)} custom-call(bf16[2,256,128]{2,1,0:T(8,128)(2,1)S(1)} %bitcast.89, bf16[2,256,128]{2,1,0:T(8,128)(2,1)S(1)} %collective-permute-done.refs_1_, bf16[2,256,128]{2,1,0:T(8,128)(2,1)S(1)} %get-tuple-element.24.refs_2_, bf16[2,256,128]{2,1,0:T(8,128)(2,1)S(1)} %collective-permute-done.2.refs_3_, ...), custom_call_target="tpu_custom_call" | custom-call | tf_op jit(solution)/shard_map/attend/pallas_call | solution.py:100
  89.9 2.6 %convolution_convert_fusion = bf16[128,8192]{1,0:T(8,128)(2,1)} fusion(bf16[128,512]{1,0:T(8,128)(2,1)S(1)} %attend.1, bf16[512,8192]{1,0:T(8,128)(2,1)S(1)} %copy-done.7), kind=kOutput, calls=%fused_computation | convolution fusion | flops 1074790400 | bytes 10616832 | tf_op jit(solution)/shard_map/dot_general | solution.py:188
  92.5 3.3 %reshape.16 = bf16[128,8,2,512]{3,2,1,0:T(2,128)(2,1)S(1)} reshape(bf16[128,8192]{1,0:T(8,128)(2,1)} %convolution_convert_fusion) | data formatting | bytes 4194304 | tf_op jit(solution)/shard_map/reshape | solution.py:189
  95.8 5.8 %constant_dynamic-slice_fusion.1 = (bf16[128,8,1,512]{3,2,1,0:T(2,128)(2,1)}, bf16[128,8,1,512]{3,2,1,0:T(2,128)(2,1)S(1)}) fusion(bf16[128,8,2,512]{3,2,1,0:T(2,128)(2,1)S(1)} %reshape.16, s32[]{:T(128)S(6)} %select_n.217, s32[]{:T(128)S(6)} %select_n.218), kind=kLoop, calls=%fused_computation.36 | loop fusion | bytes 4194312 | tf_op jit(solution)/shard_map/jit(dynamic_index_in_dim)/dynamic_slice | solution.py:190
  101.6 2.1 %copy.31 = bf16[128,8,1,512]{3,0,1,2:T(8,128)(2,1)} copy(bf16[128,8,1,512]{3,2,1,0:T(2,128)(2,1)S(1)} %get-tuple-element.16) | data formatting | bytes 2097152 | tf_op jit(solution)/shard_map/jit(dynamic_index_in_dim)/dynamic_slice | solution.py:191
  114.4 1.7 %collective-permute-done.32 = bf16[128,512]{1,0:T(8,128)(2,1)S(1)} collective-permute-done((bf16[128,512]{1,0:T(8,128)(2,1)S(1)}, bf16[128,512]{1,0:T(8,128)(2,1)S(1)}, u32[]{:S(2)}, u32[]{:S(2)}) %collective-permute-start.32) | collective-permute-done | bytes 131104 | tf_op jit(solution)/shard_map/ppermute | solution.py:129
  130.2 2.0 %collective-permute-start.35 = (bf16[128,512]{1,0:T(8,128)(2,1)S(1)}, bf16[128,512]{1,0:T(8,128)(2,1)S(1)}, u32[]{:S(2)}, u32[]{:S(2)}) collective-permute-start(bf16[128,512]{1,0:T(8,128)(2,1)S(1)} %get-tuple-element.9), channel_id=1, source_target_pairs={{0,4},{1,5},{4,8},{5,9},{8,12},{9,13},{12,14},{13,15},{14,10},{15,... | collective-permute-start | bytes 393224 | tf_op jit(solution)/shard_map/ppermute | solution.py:129
  135.2 1.9 %collective-permute-done.38 = bf16[128,512]{1,0:T(8,128)(2,1)S(1)} collective-permute-done((bf16[128,512]{1,0:T(8,128)(2,1)S(1)}, bf16[128,512]{1,0:T(8,128)(2,1)S(1)}, u32[]{:S(2)}, u32[]{:S(2)}) %collective-permute-start.38) | collective-permute-done | bytes 131104 | tf_op jit(solution)/shard_map/ppermute | solution.py:129
  137.1 1.6 %fusion.6 = bf16[128,512]{1,0:T(8,128)(2,1)} fusion(bf16[128,512]{1,0:T(8,128)(2,1)S(1)} %collective-permute-done.38, bf16[128,512]{1,0:T(8,128)(2,1)S(1)} %collective-permute-done.35, f32[128,8,512]{2,0,1:T(8,128)} %copy-done.8, s32[]{:T(128)S(6)} %select_n.219), kind=kLoop, calls=%fused_computation.17 | loop fusion | flops 327680 | bytes 655364 | tf_op jit(solution)/shard_map/convert_element_type | solution.py:207
  (106 shorter events, 31.3 us)
Async XLA Ops:
  1.6 11.6 %collective-permute-start.16 = (bf16[144,512]{1,0:T(8,128)(2,1)S(1)}, bf16[144,512]{1,0:T(8,128)(2,1)S(1)}, u32[]{:S(2)}, u32[]{:S(2)}) collective-permute-start(bf16[144,512]{1,0:T(8,128)(2,1)S(1)} %pad_maximum_fusion.refs_0_), channel_id=1, source_target_pairs={{0,4},{1,5},{4,8},{5,9},{8,12},{9,13},{12,14},{13,15},{14,10},{15,... | collective-permute-start | bytes 442376 | tf_op jit(solution)/shard_map/ppermute | solution.py:129
  4.7 13.9 %collective-permute-start.18 = (bf16[144,512]{1,0:T(8,128)(2,1)S(1)}, bf16[144,512]{1,0:T(8,128)(2,1)S(1)}, u32[]{:S(2)}, u32[]{:S(2)}) collective-permute-start(bf16[144,512]{1,0:T(8,128)(2,1)S(1)} %pad_maximum_fusion.refs_0_), channel_id=1, source_target_pairs={{0,2},{1,3},{4,0},{5,1},{8,4},{9,5},{12,8},{13,9},{14,12},{15,13},... | collective-permute-start | bytes 442376 | tf_op jit(solution)/shard_map/ppermute | solution.py:129
  8.4 10.1 %collective-permute-start.3 = (bf16[2,256,128]{2,1,0:T(8,128)(2,1)S(1)}, bf16[2,256,128]{2,1,0:T(8,128)(2,1)}, u32[]{:S(2)}, u32[]{:S(2)}) collective-permute-start(bf16[2,256,128]{2,1,0:T(8,128)(2,1)S(1)} %bitcast.92), channel_id=1, source_target_pairs={{0,4},{1,5},{2,6},{3,7},{4,0},{5,1},{6,2},{7,3},{8,12},{9,13},{10,... | collective-permute-start | bytes 393224 | tf_op jit(solution)/shard_map/ppermute | solution.py:132
  10.5 8.6 %collective-permute-start.7 = (bf16[2,256,128]{2,1,0:T(8,128)(2,1)S(1)}, bf16[2,256,128]{2,1,0:T(8,128)(2,1)}, u32[]{:S(2)}, u32[]{:S(2)}) collective-permute-start(bf16[2,256,128]{2,1,0:T(8,128)(2,1)S(1)} %bitcast.91), channel_id=1, source_target_pairs={{0,8},{1,9},{2,10},{3,11},{4,12},{5,13},{6,14},{7,15},{8,0},{9,1},... | collective-permute-start | bytes 393224 | tf_op jit(solution)/shard_map/ppermute | solution.py:132
  17.0 50.9 %collective-permute-start.1 = (bf16[2,256,4,128]{3,1,0,2:T(8,128)(2,1)}, bf16[2,256,4,128]{3,1,0,2:T(8,128)(2,1)}, u32[]{:S(2)}, u32[]{:S(2)}) collective-permute-start(bf16[2,256,4,128]{3,1,0,2:T(8,128)(2,1)} %bitcast.83), channel_id=1, source_target_pairs={{0,2},{1,3},{2,0},{3,1},{4,6},{5,7},{6,4},{7,5},{8,10},{9,11},{10,... | collective-permute-start | bytes 1572872 | tf_op jit(solution)/shard_map/ppermute | solution.py:132
  18.6 13.2 %collective-permute-start.22 = (bf16[144,512]{1,0:T(8,128)(2,1)S(1)}, bf16[144,512]{1,0:T(8,128)(2,1)S(1)}, u32[]{:S(2)}, u32[]{:S(2)}) collective-permute-start(bf16[144,512]{1,0:T(8,128)(2,1)S(1)} %collective-permute-done.18.refs_4_), channel_id=1, source_target_pairs={{0,2},{1,3},{4,0},{5,1},{8,4},{9,5},{12,8},{13,9},{14,12},{15,13},... | collective-permute-start | bytes 442376 | tf_op jit(solution)/shard_map/ppermute | solution.py:129
  19.1 15.1 %collective-permute-start.19 = (bf16[144,512]{1,0:T(8,128)(2,1)S(1)}, bf16[144,512]{1,0:T(8,128)(2,1)S(1)}, u32[]{:S(2)}, u32[]{:S(2)}) collective-permute-start(bf16[144,512]{1,0:T(8,128)(2,1)S(1)} %collective-permute-done.18.refs_4_), channel_id=1, source_target_pairs={{0,1},{1,0},{2,3},{3,2},{4,5},{5,4},{6,7},{7,6},{8,9},{9,8},{10,11... | collective-permute-start | bytes 442376 | tf_op jit(solution)/shard_map/ppermute | solution.py:132
  19.3 15.0 %collective-permute-start.24 = (bf16[144,512]{1,0:T(8,128)(2,1)S(1)}, bf16[144,512]{1,0:T(8,128)(2,1)S(1)}, u32[]{:S(2)}, u32[]{:S(2)}) collective-permute-start(bf16[144,512]{1,0:T(8,128)(2,1)S(1)} %collective-permute-done.20.refs_6_), channel_id=1, source_target_pairs={{0,4},{1,5},{4,8},{5,9},{8,12},{9,13},{12,14},{13,15},{14,10},{15,... | collective-permute-start | bytes 442376 | tf_op jit(solution)/shard_map/ppermute | solution.py:129
  21.6 13.0 %collective-permute-start.17 = (bf16[144,512]{1,0:T(8,128)(2,1)S(1)}, bf16[144,512]{1,0:T(8,128)(2,1)S(1)}, u32[]{:S(2)}, u32[]{:S(2)}) collective-permute-start(bf16[144,512]{1,0:T(8,128)(2,1)S(1)} %collective-permute-done.16.refs_2_), channel_id=1, source_target_pairs={{0,1},{1,0},{2,3},{3,2},{4,5},{5,4},{6,7},{7,6},{8,9},{9,8},{10,11... | collective-permute-start | bytes 442376 | tf_op jit(solution)/shard_map/ppermute | solution.py:132
  34.5 22.3 %collective-permute-start.21 = (bf16[144,512]{1,0:T(8,128)(2,1)S(1)}, bf16[144,512]{1,0:T(8,128)(2,1)}, u32[]{:S(2)}, u32[]{:S(2)}) collective-permute-start(bf16[144,512]{1,0:T(8,128)(2,1)S(1)} %collective-permute-done.20.refs_6_), channel_id=1, source_target_pairs={{0,1},{1,0},{2,3},{3,2},{4,5},{5,4},{6,7},{7,6},{8,9},{9,8},{10,11... | collective-permute-start | bytes 442376 | tf_op jit(solution)/shard_map/ppermute | solution.py:132
  37.0 20.4 %collective-permute-start.27 = (bf16[144,512]{1,0:T(8,128)(2,1)}, bf16[144,512]{1,0:T(8,128)(2,1)}, u32[]{:S(2)}, u32[]{:S(2)}) collective-permute-start(bf16[144,512]{1,0:T(8,128)(2,1)} %collective-permute-done.26.refs_12_), channel_id=1, source_target_pairs={{0,1},{1,0},{2,3},{3,2},{4,5},{5,4},{6,7},{7,6},{8,9},{9,8},{10,11... | collective-permute-start | bytes 442376 | tf_op jit(solution)/shard_map/ppermute | solution.py:132
  37.7 19.7 %collective-permute-start.25 = (bf16[144,512]{1,0:T(8,128)(2,1)S(1)}, bf16[144,512]{1,0:T(8,128)(2,1)}, u32[]{:S(2)}, u32[]{:S(2)}) collective-permute-start(bf16[144,512]{1,0:T(8,128)(2,1)S(1)} %collective-permute-done.24.refs_10_), channel_id=1, source_target_pairs={{0,1},{1,0},{2,3},{3,2},{4,5},{5,4},{6,7},{7,6},{8,9},{9,8},{10,11... | collective-permute-start | bytes 442376 | tf_op jit(solution)/shard_map/ppermute | solution.py:132
  40.6 16.9 %collective-permute-start.29 = (bf16[144,512]{1,0:T(8,128)(2,1)}, bf16[144,512]{1,0:T(8,128)(2,1)}, u32[]{:S(2)}, u32[]{:S(2)}) collective-permute-start(bf16[144,512]{1,0:T(8,128)(2,1)} %collective-permute-done.28.refs_14_), channel_id=1, source_target_pairs={{0,1},{1,0},{2,3},{3,2},{4,5},{5,4},{6,7},{7,6},{8,9},{9,8},{10,11... | collective-permute-start | bytes 442376 | tf_op jit(solution)/shard_map/ppermute | solution.py:132
  56.9 16.2 %collective-permute-start = (bf16[2,256,128]{2,1,0:T(8,128)(2,1)S(1)}, bf16[2,256,128]{2,1,0:T(8,128)(2,1)S(1)}, u32[]{:S(2)}, u32[]{:S(2)}) collective-permute-start(bf16[2,256,128]{2,1,0:T(8,128)(2,1)S(1)} %bitcast.88), channel_id=1, source_target_pairs={{0,1},{1,0},{2,3},{3,2},{4,5},{5,4},{6,7},{7,6},{8,9},{9,8},{10,11... | collective-permute-start | bytes 393224 | tf_op jit(solution)/shard_map/ppermute | solution.py:132
  57.4 15.7 %collective-permute-start.11 = (bf16[2,256,128]{2,1,0:T(8,128)(2,1)}, bf16[2,256,128]{2,1,0:T(8,128)(2,1)S(1)}, u32[]{:S(2)}, u32[]{:S(2)}) collective-permute-start(bf16[2,256,128]{2,1,0:T(8,128)(2,1)} %bitcast.90), channel_id=1, source_target_pairs={{0,12},{1,13},{2,14},{3,15},{4,8},{5,9},{6,10},{7,11},{8,4},{9,5},... | collective-permute-start | bytes 393224 | tf_op jit(solution)/shard_map/ppermute | solution.py:132
  57.4 16.5 %collective-permute-start.4 = (bf16[2,256,128]{2,1,0:T(8,128)(2,1)}, bf16[2,256,128]{2,1,0:T(8,128)(2,1)S(1)}, u32[]{:S(2)}, u32[]{:S(2)}) collective-permute-start(bf16[2,256,128]{2,1,0:T(8,128)(2,1)} %collective-permute-done.3.refs_4_), channel_id=1, source_target_pairs={{0,1},{1,0},{2,3},{3,2},{4,5},{5,4},{6,7},{7,6},{8,9},{9,8},{10,11... | collective-permute-start | bytes 393224 | tf_op jit(solution)/shard_map/ppermute | solution.py:132
  57.5 16.4 %collective-permute-start.8 = (bf16[2,256,128]{2,1,0:T(8,128)(2,1)}, bf16[2,256,128]{2,1,0:T(8,128)(2,1)S(1)}, u32[]{:S(2)}, u32[]{:S(2)}) collective-permute-start(bf16[2,256,128]{2,1,0:T(8,128)(2,1)} %collective-permute-done.7.refs_8_), channel_id=1, source_target_pairs={{0,1},{1,0},{2,3},{3,2},{4,5},{5,4},{6,7},{7,6},{8,9},{9,8},{10,11... | collective-permute-start | bytes 393224 | tf_op jit(solution)/shard_map/ppermute | solution.py:132
  69.2 8.3 %collective-permute-start.13 = (bf16[2,256,128]{2,1,0:T(8,128)(2,1)S(1)}, bf16[2,256,128]{2,1,0:T(8,128)(2,1)S(1)}, u32[]{:S(2)}, u32[]{:S(2)}) collective-permute-start(bf16[2,256,128]{2,1,0:T(8,128)(2,1)S(1)} %get-tuple-element.21), channel_id=1, source_target_pairs={{0,12},{1,13},{2,14},{3,15},{4,8},{5,9},{6,10},{7,11},{8,4},{9,5},... | collective-permute-start | bytes 393224 | tf_op jit(solution)/shard_map/ppermute | solution.py:132
  73.0 10.4 %collective-permute-start.9 = (bf16[2,256,128]{2,1,0:T(8,128)(2,1)S(1)}, bf16[2,256,128]{2,1,0:T(8,128)(2,1)S(1)}, u32[]{:S(2)}, u32[]{:S(2)}) collective-permute-start(bf16[2,256,128]{2,1,0:T(8,128)(2,1)S(1)} %get-tuple-element.22), channel_id=1, source_target_pairs={{0,8},{1,9},{2,10},{3,11},{4,12},{5,13},{6,14},{7,15},{8,0},{9,1},... | collective-permute-start | bytes 393224 | tf_op jit(solution)/shard_map/ppermute | solution.py:132
  73.1 10.3 %collective-permute-start.5 = (bf16[2,256,128]{2,1,0:T(8,128)(2,1)S(1)}, bf16[2,256,128]{2,1,0:T(8,128)(2,1)S(1)}, u32[]{:S(2)}, u32[]{:S(2)}) collective-permute-start(bf16[2,256,128]{2,1,0:T(8,128)(2,1)S(1)} %get-tuple-element.23), channel_id=1, source_target_pairs={{0,4},{1,5},{2,6},{3,7},{4,0},{5,1},{6,2},{7,3},{8,12},{9,13},{10,... | collective-permute-start | bytes 393224 | tf_op jit(solution)/shard_map/ppermute | solution.py:132
  73.9 10.3 %collective-permute-start.12 = (bf16[2,256,128]{2,1,0:T(8,128)(2,1)S(1)}, bf16[2,256,128]{2,1,0:T(8,128)(2,1)S(1)}, u32[]{:S(2)}, u32[]{:S(2)}) collective-permute-start(bf16[2,256,128]{2,1,0:T(8,128)(2,1)S(1)} %collective-permute-done.11.refs_12_), channel_id=1, source_target_pairs={{0,1},{1,0},{2,3},{3,2},{4,5},{5,4},{6,7},{7,6},{8,9},{9,8},{10,11... | collective-permute-start | bytes 393224 | tf_op jit(solution)/shard_map/ppermute | solution.py:132
  74.0 10.2 %collective-permute-start.2 = (bf16[2,256,128]{2,1,0:T(8,128)(2,1)S(1)}, bf16[2,256,128]{2,1,0:T(8,128)(2,1)S(1)}, u32[]{:S(2)}, u32[]{:S(2)}) collective-permute-start(bf16[2,256,128]{2,1,0:T(8,128)(2,1)S(1)} %get-tuple-element.24.refs_2_), channel_id=1, source_target_pairs={{0,1},{1,0},{2,3},{3,2},{4,5},{5,4},{6,7},{7,6},{8,9},{9,8},{10,11... | collective-permute-start | bytes 393224 | tf_op jit(solution)/shard_map/ppermute | solution.py:132
  77.5 6.6 %collective-permute-start.14 = (bf16[2,256,128]{2,1,0:T(8,128)(2,1)S(1)}, bf16[2,256,128]{2,1,0:T(8,128)(2,1)S(1)}, u32[]{:S(2)}, u32[]{:S(2)}) collective-permute-start(bf16[2,256,128]{2,1,0:T(8,128)(2,1)S(1)} %collective-permute-done.13.refs_14_), channel_id=1, source_target_pairs={{0,1},{1,0},{2,3},{3,2},{4,5},{5,4},{6,7},{7,6},{8,9},{9,8},{10,11... | collective-permute-start | bytes 393224 | tf_op jit(solution)/shard_map/ppermute | solution.py:132
  113.1 8.9 %collective-permute-start.36 = (bf16[128,512]{1,0:T(8,128)(2,1)S(1)}, bf16[128,512]{1,0:T(8,128)(2,1)S(1)}, u32[]{:S(2)}, u32[]{:S(2)}) collective-permute-start(bf16[128,512]{1,0:T(8,128)(2,1)S(1)} %get-tuple-element.14), channel_id=1, source_target_pairs={{0,2},{1,3},{4,0},{5,1},{8,4},{9,5},{12,8},{13,9},{14,12},{15,13},... | collective-permute-start | bytes 393224 | tf_op jit(solution)/shard_map/ppermute | solution.py:129
  (26 other events, 269.0 us)

commit v2 on v1

v2 whole, which is shorter than its diff:
```python
import functools
import math

import jax
import jax.numpy as jnp
from jax import lax
from jax.experimental import pallas as pl
from jax.experimental.pallas import tpu as pltpu
from jax.sharding import PartitionSpec as P

H = 64
KV = 8
DH = 128
EPS = 1e-05
PAD = 16
EARLY = 5
RELEASE = 1
MIB = 1 << 20
TRANS_B = (((1,), (1,)), ((), ()))


def in_vmem(count):
    return [pl.BlockSpec(memory_space=pltpu.VMEM)] * count


def anywhere(count):
    return [pl.BlockSpec(memory_space=pl.ANY)] * count


def cost(flops, moved):
    return pl.CostEstimate(flops=flops, bytes_accessed=moved, transcendentals=0)


def params(mib):
    return pltpu.CompilerParams(vmem_limit_bytes=mib * MIB)


def chip_at(place, chips):
    return jnp.where(place < chips // 2, 2 * place, 2 * (chips - 1 - place) + 1)


def place_of(chip, chips):
    return jnp.where(lax.rem(chip, 2) == 0, lax.div(chip, 2), chips - 1 - lax.div(chip, 2))


def here():
    device = lax.axis_index("seq")
    return lax.div(device, 2), lax.rem(device, 2)


def neighbour_chip(offset, chips):
    chip, _ = here()
    return chip_at(lax.rem(place_of(chip, chips) + offset + chips, chips), chips)


def pack_kernel(tokens, gain, block, sem):
    rows, width = tokens.shape
    copy = pltpu.make_async_copy(tokens, block.at[pl.ds(0, rows), :], sem)
    copy.start()
    wide = gain[...].astype(jnp.float32).reshape(1, width)
    block[rows:, :] = jnp.broadcast_to(wide, (PAD, width)).astype(jnp.bfloat16)
    copy.wait()


def pack(tokens, gain):
    rows, width = tokens.shape
    return pl.pallas_call(
        pack_kernel,
        out_shape=jax.ShapeDtypeStruct((rows + PAD, width), jnp.bfloat16),
        in_specs=anywhere(1) + in_vmem(1),
        out_specs=in_vmem(1)[0],
        scratch_shapes=[pltpu.SemaphoreType.DMA],
        name="pack",
    )(tokens, gain)


def cut_kernel(chips, cache, *pieces):
    chip, _ = here()
    for step, piece in enumerate(pieces):
        head = lax.div(lax.bitwise_xor(chip, step) * KV, chips)
        piece[...] = cache[:, :, pl.ds(pl.multiple_of(head * DH, DH), DH)]


def cut(cache, chips):
    shape = (2, cache.shape[1], DH)
    return pl.pallas_call(
        functools.partial(cut_kernel, chips),
        out_shape=[jax.ShapeDtypeStruct(shape, jnp.bfloat16)] * chips,
        in_specs=in_vmem(1),
        out_specs=in_vmem(chips),
        compiler_params=params(8),
        name="cut",
    )(cache)


def halve_kernel(chips, width, w_out, mine, send, sems):
    _, core = here()
    copies = []
    for side, half in enumerate((send, mine)):
        for offset in range(chips):
            column = 2 * neighbour_chip(offset, chips) + (core if side else 1 - core)
            columns = pl.ds(pl.multiple_of(column * width, width), width)
            copy = pltpu.make_async_copy(w_out.at[:, columns], half.at[offset], sems.at[side, offset])
            copy.start()
            copies.append(copy)
    for copy in copies:
        copy.wait()


def halve(w_out, chips):
    rows, columns = w_out.shape
    width = columns // (2 * chips)
    return pl.pallas_call(
        functools.partial(halve_kernel, chips, width),
        out_shape=[jax.ShapeDtypeStruct((chips, rows, width), jnp.bfloat16)] * 2,
        in_specs=anywhere(1),
        out_specs=in_vmem(2),
        scratch_shapes=[pltpu.SemaphoreType.DMA((2, chips))],
        compiler_params=params(12),
        name="halve",
    )(w_out)


def project_kernel(offsets, chips, rows, *refs):
    count = len(offsets)
    blocks = refs[:count]
    w_query, w_key, w_value, query_ref, own_ref, held, held_own, sems, own_sems = refs[count:]
    width = blocks[0].shape[1]
    _, core = here()
    half = w_key.shape[0]
    own_copies = [
        pltpu.make_async_copy(w_key, held_own.at[pl.ds(0, half), :], own_sems.at[0]),
        pltpu.make_async_copy(w_value, held_own.at[pl.ds(half, half), :], own_sems.at[1]),
    ]
    for copy in own_copies:
        copy.start()
    columns, copies = [], []
    for number, (offset, other) in enumerate(offsets):
        side = 1 - core if other else core
        owner = 2 * neighbour_chip(offset, chips) + side
        columns.append(pl.ds(pl.multiple_of(owner * width, width), width))
        copy = pltpu.make_async_copy(w_query.at[:, columns[number]], held.at[number], sems.at[number])
        copy.start()
        copies.append(copy)
    total = jnp.zeros((rows, 128), jnp.float32)
    for block in blocks:
        wide = block[:rows, :].astype(jnp.float32)
        square = wide * wide
        for lane in range(0, width, 128):
            total += square[:, lane : lane + 128]
    inverse = lax.rsqrt(jnp.sum(total, axis=1, keepdims=True) / (width * count) + EPS)
    query = jnp.zeros(query_ref.shape, jnp.float32)
    own = jnp.zeros(own_ref.shape, jnp.float32)
    for copy in own_copies:
        copy.wait()
    for number, block in enumerate(blocks):
        gain = block[rows : rows + PAD, :].astype(jnp.float32)[0:1, :]
        wide = block[:rows, :].astype(jnp.float32)
        normed = (wide * inverse * gain).astype(jnp.bfloat16)
        own += lax.dot_general(normed, held_own[:, columns[number]], TRANS_B, preferred_element_type=jnp.float32)
        copies[number].wait()
        query += lax.dot_general(normed, held[number], TRANS_B, preferred_element_type=jnp.float32)
    query_ref[...] = query.astype(jnp.bfloat16)
    own_ref[...] = own.astype(jnp.bfloat16)


def project(offsets, chips, blocks, w_query, w_key, w_value, rows):
    count, width = len(blocks), blocks[0].shape[1]
    return pl.pallas_call(
        functools.partial(project_kernel, offsets, chips, rows),
        out_shape=(
            jax.ShapeDtypeStruct((rows, w_query.shape[0]), jnp.bfloat16),
            jax.ShapeDtypeStruct((rows, 2 * w_key.shape[0]), jnp.bfloat16),
        ),
        in_specs=in_vmem(count) + anywhere(3),
        out_specs=tuple(in_vmem(2)),
        scratch_shapes=[
            pltpu.VMEM((count, w_query.shape[0], width), jnp.bfloat16),
            pltpu.VMEM((2 * w_key.shape[0], w_key.shape[1]), jnp.bfloat16),
            pltpu.SemaphoreType.DMA((count,)),
            pltpu.SemaphoreType.DMA((2,)),
        ],
        compiler_params=params(24),
        cost_estimate=cost(8 * rows * w_query.size, 2 * w_query.size),
        name="project",
    )(*blocks, w_query, w_key, w_value)


def attend_kernel(count, parts, heads, *refs):
    caches, owns = refs[:count], refs[count : count + parts]
    query_ref, out_ref, query_all, scores = refs[count + parts :]
    rows = query_ref.shape[0]
    half = owns[0].shape[1] // 2
    scale = 1.0 / math.sqrt(DH)
    _, core = here()
    own_parts = [own[...].astype(jnp.float32) for own in owns]
    if parts == 2:
        own_parts = [jnp.where(core == 0, own_parts[i], own_parts[1 - i]) for i in range(2)]
    own_key = jnp.concatenate([part[:, :half] for part in own_parts], axis=1)
    own_value = jnp.concatenate([part[:, half:] for part in own_parts], axis=1)
    for head in range(heads):
        query_all[head * rows : (head + 1) * rows, :] = query_ref[:, head * DH : (head + 1) * DH]
    query = query_all[...]
    keys_own = jnp.concatenate([own_key] * heads, axis=0)
    values_own = jnp.concatenate([own_value] * heads, axis=0)
    own = jnp.sum(query.astype(jnp.float32) * keys_own, axis=1, keepdims=True) * scale
    step = caches[0].shape[1]
    best = None
    for number, cache in enumerate(caches):
        part = lax.dot_general(query, cache[0], TRANS_B, preferred_element_type=jnp.float32)
        scores[:, number * step : (number + 1) * step] = part
        for lane in range(0, step, 128):
            piece = part[:, lane : lane + 128]
            best = piece if best is None else jnp.maximum(best, piece)
    top = jnp.maximum(jnp.max(best, axis=1, keepdims=True) * scale, own)
    total = jnp.zeros((heads * rows, 128), jnp.float32)
    numerator = jnp.zeros((heads * rows, DH), jnp.float32)
    for number, cache in enumerate(caches):
        weights = jnp.exp(scores[:, number * step : (number + 1) * step] * scale - top)
        for lane in range(0, step, 128):
            total += weights[:, lane : lane + 128]
        numerator += jnp.dot(weights.astype(jnp.bfloat16), cache[1], preferred_element_type=jnp.float32)
    own_weight = jnp.exp(own - top)
    denominator = jnp.sum(total, axis=1, keepdims=True) + own_weight
    rounded = own_weight.astype(jnp.bfloat16).astype(jnp.float32)
    result = ((numerator + rounded * values_own) / denominator).astype(jnp.bfloat16)
    for head in range(heads):
        out_ref[:, head * DH : (head + 1) * DH] = result[head * rows : (head + 1) * rows, :]


def attend(caches, owns, query):
    count, rows = len(caches), query.shape[0]
    heads = query.shape[1] // DH
    positions = count * caches[0].shape[1]
    return pl.pallas_call(
        functools.partial(attend_kernel, count, len(owns), heads),
        out_shape=jax.ShapeDtypeStruct(query.shape, jnp.bfloat16),
        in_specs=in_vmem(count + len(owns) + 1),
        out_specs=in_vmem(1)[0],
        scratch_shapes=[
            pltpu.VMEM((heads * rows, DH), jnp.bfloat16),
            pltpu.VMEM((heads * rows, positions), jnp.float32),
        ],
        compiler_params=params(24),
        name="attend",
    )(*caches, *owns, query)


def near_kernel(attention, weights, out_ref):
    for offset in range(weights.shape[0]):
        out_ref[offset] = jnp.dot(attention[...], weights[offset], preferred_element_type=jnp.float32)


def near(attention, weights):
    chips, _, width = weights.shape
    return pl.pallas_call(
        near_kernel,
        out_shape=jax.ShapeDtypeStruct((chips, attention.shape[0], width), jnp.float32),
        in_specs=in_vmem(2),
        out_specs=in_vmem(1)[0],
        compiler_params=params(12),
        name="near",
    )(attention, weights)


def far_kernel(offsets, attention, weights, base, *outs):
    for out, offset in zip(outs, offsets):
        term = jnp.dot(attention[...], weights[offset], preferred_element_type=jnp.float32)
        out[...] = (base[offset] + term).astype(out.dtype)


def far(attention, weights, base, offsets, dtype):
    return pl.pallas_call(
        functools.partial(far_kernel, offsets),
        out_shape=[jax.ShapeDtypeStruct(base.shape[1:], dtype)] * len(offsets),
        in_specs=in_vmem(3),
        out_specs=in_vmem(len(offsets)),
        compiler_params=params(12),
        name="far",
    )(attention, weights, base)


def body(tokens, gain, w_query, w_key, w_value, w_out, prefix_cache, size):
    chips = size // 2
    outer = chips // 2
    cycle = [2 * a for a in range(outer)] + [2 * a + 1 for a in reversed(range(outer))]

    def around(value, step):
        pairs = [
            (2 * cycle[p] + k, 2 * cycle[(p + step) % chips] + k) for p in range(chips) for k in (0, 1)
        ]
        return lax.ppermute(value, "seq", pairs)

    def swap(value, bits):
        return lax.ppermute(value, "seq", [(i, i ^ bits) for i in range(size)])

    rows = tokens.shape[0]

    block = pack(tokens, gain)
    blocks, offsets = [], []

    def take(value, offset):
        blocks.extend([value, swap(value, 1)])
        offsets.extend([(offset, False), (offset, True)])

    take(block, 0)
    right = left = block
    reach = chips // 2
    for step in range(1, reach + 1):
        right = around(right, 1)
        if step == 1:
            w_out, right = lax.optimization_barrier((w_out, right))
        if step == min(2, reach):
            prefix_cache, right = lax.optimization_barrier((prefix_cache, right))
        if step == max(reach - RELEASE, 1):
            pieces = cut(prefix_cache, chips)
            *pieces, right = lax.optimization_barrier((*pieces, right))
        take(right, -step)
        if step < reach:
            left = around(left, -1)
            take(left, step)
    mine, send = halve(w_out, chips)
    w_other = swap(send, 1)
    query, own = project(tuple(offsets), chips, blocks, w_query, w_key, w_value, rows)

    order = list(range(chips // 2, chips)) + list(range(2, chips // 2)) + [1]
    order = [step for step in order if step < chips]
    parts = {}
    for number, step in enumerate(order):
        if number == EARLY:
            *pieces, query = lax.optimization_barrier((*pieces, query))
        parts[step] = swap(pieces[step], 2 * step)
    held = list(parts.values())
    *held, query = lax.optimization_barrier((*held, query))
    caches = [pieces[0], swap(pieces[0], 1)]
    for part in held:
        caches += [part, swap(part, 1)]

    sharers = size // KV
    if sharers == 1:
        owns = [own]
    elif sharers == 2:
        owns = [own, swap(own, 1)]
    else:
        groups = [list(range(g * sharers, (g + 1) * sharers)) for g in range(KV)]
        gathered = lax.all_gather(own, "seq", axis=0, axis_index_groups=groups)
        owns = [gathered[i] for i in range(sharers)]
    attention = attend(caches, owns, query)

    other = swap(attention, 1)
    base = near(attention, mine)
    first = [reach] + ([chips - reach + 1] if reach > 1 else [])
    rest = [offset for offset in range(chips) if offset not in first]
    terms = dict(zip(first, far(other, w_other, base, tuple(first), jnp.bfloat16)))
    terms.update(zip(rest, far(other, w_other, base, tuple(rest), jnp.float32)))
    right = left = None
    for step in reversed(range(1, reach + 1)):
        term = terms[step]
        right = term if right is None else (right.astype(jnp.float32) + term).astype(jnp.bfloat16)
        right = around(right, 1)
        if step < reach:
            term = terms[chips - step]
            left = term if left is None else (left.astype(jnp.float32) + term).astype(jnp.bfloat16)
            left = around(left, -1)
    total = terms[0] + right.astype(jnp.float32)
    if left is not None:
        total += left.astype(jnp.float32)
    return total.astype(jnp.bfloat16)


def solution(mesh):
    return jax.shard_map(
        functools.partial(body, size=mesh.shape["seq"]),
        mesh=mesh,
        in_specs=(
            P("group", "seq"),
            P("seq"),
            P("seq", None),
            P("seq", None),
            P("seq", None),
            P("seq", None),
            P(None, ("group", "seq"), None),
        ),
        out_specs=P("group", "seq"),
        check_vma=False,
    )
```

time: 140 us -> 96.3 us (0.69)
  between operations: 27 us -> 0.15 us
  local copies, waits for them, and re-layouts: 28.3 us -> 6.78 us
  waiting for transfers between devices: 29.7 us -> 39.7 us
  other arithmetic: 7.14 us -> 0.85 us
  Pallas kernels: 13.2 us -> 16.6 us
  matrix products: 2.62 us -> 0 us
    dynamic_slice x7 -> x0, local copies, waits for them, and re-layouts: 14.4 us -> none  [the longest x1 5.81 us: body(): mine = lax.dynamic_index_in_dim(partial, core, 2, keepdims=False)]
    ppermute x14, waiting for transfers between devices: 19.9 us -> 26.6 us  [around(): return lax.ppermute(value, 'seq', pairs)]
    convert_element_type x4 -> x6, other arithmetic: 4.82 us -> 0.85 us  [the longest x1 0.71 us: body(): return total.astype(jnp.bfloat16)]
    pallas_call x2 -> x8, Pallas kernels: 13.2 us -> 16.6 us  [the longest x1 7.09 us: project(): pl.pallas_call(functools.partial(project_kernel, offsets, chips, rows), o...]
    reshape x1 -> x0, local copies, waits for them, and re-layouts: 3.3 us -> none  [body(): partial = partial.astype(jnp.bfloat16).reshape(rows, chips, 2, features)]
    ppermute x25 -> x26, waiting for transfers between devices: 9.87 us -> 13.1 us  [swap(): return lax.ppermute(value, 'seq', [(i, i ^ bits) for i in range(size)])]
    ppermute x14, starting transfers between devices: 16.4 us -> 19.6 us  [around(): return lax.ppermute(value, 'seq', pairs)]
    dot_general x1 -> x0, matrix products: 2.62 us -> none  [body(): partial = jnp.dot(attention, w_out, preferred_element_type=jnp.float32)]
  transfers between devices with their start and end apart: 39 -> 40, of which waited for: 12 -> 23; matrix products, arithmetic and copies ran while one was open for 10% -> 0% of each run, Pallas kernels for 6% -> 13%
where the time goes in v2:
time: 96.3 us; the launch traced here: 96 us
  waiting for transfers between devices  39.7 us (41%)
  starting transfers between devices  31.9 us (33%)
  Pallas kernels  16.6 us (17%)
  local copies, waits for them, and re-layouts  6.78 us (7%)
    ppermute x14, waiting for transfers between devices, around(): return lax.ppermute(value, 'seq', pairs)  26.6 us
    ppermute x14, starting transfers between devices, around(): return lax.ppermute(value, 'seq', pairs)  19.6 us
    ppermute x26, waiting for transfers between devices, swap(): return lax.ppermute(value, 'seq', [(i, i ^ bits) for i in range(size)])  13.1 us
    ppermute x26, starting transfers between devices, swap(): return lax.ppermute(value, 'seq', [(i, i ^ bits) for i in range(size)])  12.3 us
    pallas_call x1, Pallas kernels, project(): pl.pallas_call(functools.partial(project_kernel, offsets, chips, rows), o...  7.09 us
    unnamed x12, local copies, waits for them, and re-layouts  6.78 us
    pallas_call x1, Pallas kernels, attend(): pl.pallas_call(functools.partial(attend_kernel, count, len(owns), heads),...  3.89 us
    pallas_call x1, Pallas kernels, pack(): pl.pallas_call(pack_kernel, out_shape=jax.ShapeDtypeStruct((rows + PAD, w...  2.25 us
  transfers between devices with their start and end apart: 40, of which 23 were waited for; matrix products, arithmetic and copies ran while one was open for 0% of the time, Pallas kernels for 13%

profile of v2, /device:TPU:0, one launch (start us, length us, event | category | flops | bytes accessed | tf_op | source)
XLA Modules:
  0.0 96.0 jit_solution(6557797852127121734)
XLA Ops:
  0.0 2.3 %pack.1.refs_0_ = bf16[144,512]{1,0:T(8,128)(2,1)} custom-call(bf16[128,512]{1,0:T(8,128)(2,1)} %tokens.1, bf16[512]{0:T(512)(128)(2,1)} %gain.1), custom_call_target="tpu_custom_call" | custom-call | tf_op jit(solution)/shard_map/pack/pallas_call | solution.py:67
  2.3 3.1 %collective-permute-start = (bf16[144,512]{1,0:T(8,128)(2,1)}, bf16[144,512]{1,0:T(8,128)(2,1)S(1)}, u32[]{:S(2)}, u32[]{:S(2)}) collective-permute-start(bf16[144,512]{1,0:T(8,128)(2,1)} %pack.1.refs_0_), channel_id=1, source_target_pairs={{0,4},{1,5},{4,8},{5,9},{8,12},{9,13},{12,14},{13,15},{14,10},{15,... | collective-permute-start | bytes 442376 | tf_op jit(solution)/shard_map/ppermute | solution.py:292
  5.3 4.0 %collective-permute-done.refs_2_ = bf16[144,512]{1,0:T(8,128)(2,1)S(1)} collective-permute-done((bf16[144,512]{1,0:T(8,128)(2,1)}, bf16[144,512]{1,0:T(8,128)(2,1)S(1)}, u32[]{:S(2)}, u32[]{:S(2)}) %collective-permute-start) | collective-permute-done | bytes 147488 | tf_op jit(solution)/shard_map/ppermute | solution.py:292
  9.3 3.4 %copy-done = bf16[512,8192]{1,0:T(8,128)(2,1)S(1)} copy-done((bf16[512,8192]{1,0:T(8,128)(2,1)S(1)}, bf16[512,8192]{1,0:T(8,128)(2,1)}, u32[]{:S(2)}) %copy-start) | copy-done | bytes 8388632
  16.4 4.2 %collective-permute-done.1.refs_6_ = bf16[144,512]{1,0:T(8,128)(2,1)S(1)} collective-permute-done((bf16[144,512]{1,0:T(8,128)(2,1)S(1)}, bf16[144,512]{1,0:T(8,128)(2,1)S(1)}, u32[]{:S(2)}, u32[]{:S(2)}) %collective-permute-start.1) | collective-permute-done | bytes 147488 | tf_op jit(solution)/shard_map/ppermute | solution.py:292
  23.2 2.8 %collective-permute-done.2.refs_10_ = bf16[144,512]{1,0:T(8,128)(2,1)S(1)} collective-permute-done((bf16[144,512]{1,0:T(8,128)(2,1)S(1)}, bf16[144,512]{1,0:T(8,128)(2,1)S(1)}, u32[]{:S(2)}, u32[]{:S(2)}) %collective-permute-start.2) | collective-permute-done | bytes 147488 | tf_op jit(solution)/shard_map/ppermute | solution.py:292
  26.5 2.1 %collective-permute-done.8.refs_8_ = bf16[144,512]{1,0:T(8,128)(2,1)S(1)} collective-permute-done((bf16[144,512]{1,0:T(8,128)(2,1)S(1)}, bf16[144,512]{1,0:T(8,128)(2,1)S(1)}, u32[]{:S(2)}, u32[]{:S(2)}) %collective-permute-start.8) | collective-permute-done | bytes 147488 | tf_op jit(solution)/shard_map/ppermute | solution.py:292
  31.2 2.9 %collective-permute-done.11.refs_12_ = bf16[144,512]{1,0:T(8,128)(2,1)S(1)} collective-permute-done((bf16[144,512]{1,0:T(8,128)(2,1)S(1)}, bf16[144,512]{1,0:T(8,128)(2,1)S(1)}, u32[]{:S(2)}, u32[]{:S(2)}) %collective-permute-start.11) | collective-permute-done | bytes 147488 | tf_op jit(solution)/shard_map/ppermute | solution.py:292
  34.6 2.6 %collective-permute-start.16 = (bf16[2,256,128]{2,1,0:T(8,128)(2,1)S(1)}, bf16[2,256,128]{2,1,0:T(8,128)(2,1)S(1)}, u32[]{:S(2)}, u32[]{:S(2)}) collective-permute-start(bf16[2,256,128]{2,1,0:T(8,128)(2,1)S(1)} %get-tuple-element.65), channel_id=1, source_target_pairs={{0,8},{1,9},{2,10},{3,11},{4,12},{5,13},{6,14},{7,15},{8,0},{9,1},... | collective-permute-start | bytes 393224 | tf_op jit(solution)/shard_map/ppermute | solution.py:295
  38.2 3.6 %collective-permute-start.18 = (bf16[2,256,128]{2,1,0:T(8,128)(2,1)S(1)}, bf16[2,256,128]{2,1,0:T(8,128)(2,1)S(1)}, u32[]{:S(2)}, u32[]{:S(2)}) collective-permute-start(bf16[2,256,128]{2,1,0:T(8,128)(2,1)S(1)} %get-tuple-element.67), channel_id=1, source_target_pairs={{0,12},{1,13},{2,14},{3,15},{4,8},{5,9},{6,10},{7,11},{8,4},{9,5},... | collective-permute-start | bytes 393224 | tf_op jit(solution)/shard_map/ppermute | solution.py:295
  42.3 3.4 %copy-done.3 = bf16[512,8192]{1,0:T(8,128)(2,1)S(1)} copy-done((bf16[512,8192]{1,0:T(8,128)(2,1)S(1)}, bf16[512,8192]{1,0:T(8,128)(2,1)}, u32[]{:S(2)}) %copy-start.3) | copy-done | bytes 8388632
  45.7 7.1 %project.1 = (bf16[128,512]{1,0:T(8,128)(2,1)S(1)}, bf16[128,128]{1,0:T(8,128)(2,1)S(1)}) custom-call(bf16[144,512]{1,0:T(8,128)(2,1)S(1)} %copy-done.2, bf16[144,512]{1,0:T(8,128)(2,1)S(1)} %collective-permute-done.3.refs_1_, bf16[144,512]{1,0:T(8,128)(2,1)S(1)} %collective-permute-done.refs_2_, bf16[144,512]{1,0:T(8,128)(2,1)S(1)} %collective-permute-done.4.refs_3_, ...), custom_call_target="tpu_custom_call" | custom-call | flops 4294967296 | bytes 8388608 | tf_op jit(solution)/shard_map/project/pallas_call | solution.py:169
  53.1 3.4 %collective-permute-done.17.refs_4_ = bf16[2,256,128]{2,1,0:T(8,128)(2,1)S(1)} collective-permute-done((bf16[2,256,128]{2,1,0:T(8,128)(2,1)S(1)}, bf16[2,256,128]{2,1,0:T(8,128)(2,1)S(1)}, u32[]{:S(2)}, u32[]{:S(2)}) %collective-permute-start.17) | collective-permute-done | bytes 131104 | tf_op jit(solution)/shard_map/ppermute | solution.py:295
  58.3 4.1 %collective-permute-done.21.refs_12_ = bf16[2,256,128]{2,1,0:T(8,128)(2,1)S(1)} collective-permute-done((bf16[2,256,128]{2,1,0:T(8,128)(2,1)S(1)}, bf16[2,256,128]{2,1,0:T(8,128)(2,1)S(1)}, u32[]{:S(2)}, u32[]{:S(2)}) %collective-permute-start.21) | collective-permute-done | bytes 131104 | tf_op jit(solution)/shard_map/ppermute | solution.py:295
  62.4 2.4 %collective-permute-done.22.refs_14_ = bf16[2,256,128]{2,1,0:T(8,128)(2,1)S(1)} collective-permute-done((bf16[2,256,128]{2,1,0:T(8,128)(2,1)S(1)}, bf16[2,256,128]{2,1,0:T(8,128)(2,1)S(1)}, u32[]{:S(2)}, u32[]{:S(2)}) %collective-permute-start.22) | collective-permute-done | bytes 131104 | tf_op jit(solution)/shard_map/ppermute | solution.py:295
  68.0 3.9 %attend.1.attention = bf16[128,512]{1,0:T(8,128)(2,1)S(1)} custom-call(bf16[2,256,128]{2,1,0:T(8,128)(2,1)S(1)} %get-tuple-element.71.refs_0_, bf16[2,256,128]{2,1,0:T(8,128)(2,1)S(1)} %collective-permute-done.15.refs_1_, bf16[2,256,128]{2,1,0:T(8,128)(2,1)S(1)} %collective-permute-done.16.refs_2_, bf16[2,256,128]{2,1,0:T(8,128)(2,1)S(1)} %collective-permute-done.23.refs_3_, ...), custom_call_target="tpu_custom_call" | custom-call | tf_op jit(solution)/shard_map/attend/pallas_call | solution.py:235
  73.6 3.0 %collective-permute-start.33 = (bf16[128,512]{1,0:T(8,128)(2,1)S(1)}, bf16[128,512]{1,0:T(8,128)(2,1)S(1)}, u32[]{:S(2)}, u32[]{:S(2)}) collective-permute-start(bf16[128,512]{1,0:T(8,128)(2,1)S(1)} %get-tuple-element.88), channel_id=1, source_target_pairs={{0,4},{1,5},{4,8},{5,9},{8,12},{9,13},{12,14},{13,15},{14,10},{15,... | collective-permute-start | bytes 393224 | tf_op jit(solution)/shard_map/ppermute | solution.py:292
  77.2 2.5 %collective-permute-done.33 = bf16[128,512]{1,0:T(8,128)(2,1)S(1)} collective-permute-done((bf16[128,512]{1,0:T(8,128)(2,1)S(1)}, bf16[128,512]{1,0:T(8,128)(2,1)S(1)}, u32[]{:S(2)}, u32[]{:S(2)}) %collective-permute-start.33) | collective-permute-done | bytes 131104 | tf_op jit(solution)/shard_map/ppermute | solution.py:292
  79.7 2.5 %collective-permute-start.34 = (bf16[128,512]{1,0:T(8,128)(2,1)S(1)}, bf16[128,512]{1,0:T(8,128)(2,1)S(1)}, u32[]{:S(2)}, u32[]{:S(2)}) collective-permute-start(bf16[128,512]{1,0:T(8,128)(2,1)S(1)} %add_convert_fusion.5), channel_id=1, source_target_pairs={{0,4},{1,5},{4,8},{5,9},{8,12},{9,13},{12,14},{13,15},{14,10},{15,... | collective-permute-start | bytes 393224 | tf_op jit(solution)/shard_map/ppermute | solution.py:292
  82.6 2.1 %collective-permute-done.34 = bf16[128,512]{1,0:T(8,128)(2,1)S(1)} collective-permute-done((bf16[128,512]{1,0:T(8,128)(2,1)S(1)}, bf16[128,512]{1,0:T(8,128)(2,1)S(1)}, u32[]{:S(2)}, u32[]{:S(2)}) %collective-permute-start.34) | collective-permute-done | bytes 131104 | tf_op jit(solution)/shard_map/ppermute | solution.py:292
  84.8 2.5 %collective-permute-start.35 = (bf16[128,512]{1,0:T(8,128)(2,1)S(1)}, bf16[128,512]{1,0:T(8,128)(2,1)S(1)}, u32[]{:S(2)}, u32[]{:S(2)}) collective-permute-start(bf16[128,512]{1,0:T(8,128)(2,1)S(1)} %add_convert_fusion.4), channel_id=1, source_target_pairs={{0,4},{1,5},{4,8},{5,9},{8,12},{9,13},{12,14},{13,15},{14,10},{15,... | collective-permute-start | bytes 393224 | tf_op jit(solution)/shard_map/ppermute | solution.py:292
  87.8 2.4 %collective-permute-done.35 = bf16[128,512]{1,0:T(8,128)(2,1)S(1)} collective-permute-done((bf16[128,512]{1,0:T(8,128)(2,1)S(1)}, bf16[128,512]{1,0:T(8,128)(2,1)S(1)}, u32[]{:S(2)}, u32[]{:S(2)}) %collective-permute-start.35) | collective-permute-done | bytes 131104 | tf_op jit(solution)/shard_map/ppermute | solution.py:292
  90.2 2.3 %collective-permute-start.36 = (bf16[128,512]{1,0:T(8,128)(2,1)S(1)}, bf16[128,512]{1,0:T(8,128)(2,1)S(1)}, u32[]{:S(2)}, u32[]{:S(2)}) collective-permute-start(bf16[128,512]{1,0:T(8,128)(2,1)S(1)} %add_convert_fusion.3), channel_id=1, source_target_pairs={{0,4},{1,5},{4,8},{5,9},{8,12},{9,13},{12,14},{13,15},{14,10},{15,... | collective-permute-start | bytes 393224 | tf_op jit(solution)/shard_map/ppermute | solution.py:292
  92.7 2.5 %collective-permute-done.36 = bf16[128,512]{1,0:T(8,128)(2,1)S(1)} collective-permute-done((bf16[128,512]{1,0:T(8,128)(2,1)S(1)}, bf16[128,512]{1,0:T(8,128)(2,1)S(1)}, u32[]{:S(2)}, u32[]{:S(2)}) %collective-permute-start.36) | collective-permute-done | bytes 131104 | tf_op jit(solution)/shard_map/ppermute | solution.py:292
  (82 shorter events, 20.8 us)
Async XLA Ops:
  2.3 7.1 %collective-permute-start = (bf16[144,512]{1,0:T(8,128)(2,1)}, bf16[144,512]{1,0:T(8,128)(2,1)S(1)}, u32[]{:S(2)}, u32[]{:S(2)}) collective-permute-start(bf16[144,512]{1,0:T(8,128)(2,1)} %pack.1.refs_0_), channel_id=1, source_target_pairs={{0,4},{1,5},{4,8},{5,9},{8,12},{9,13},{12,14},{13,15},{14,10},{15,... | collective-permute-start | bytes 442376 | tf_op jit(solution)/shard_map/ppermute | solution.py:292
  14.2 59.1 %collective-permute-start.32 = (bf16[8,512,512]{2,1,0:T(8,128)(2,1)S(1)}, bf16[8,512,512]{2,1,0:T(8,128)(2,1)S(1)}, u32[]{:S(2)}, u32[]{:S(2)}) collective-permute-start(bf16[8,512,512]{2,1,0:T(8,128)(2,1)S(1)} %get-tuple-element.85), channel_id=1, source_target_pairs={{0,1},{1,0},{2,3},{3,2},{4,5},{5,4},{6,7},{7,6},{8,9},{9,8},{10,11... | collective-permute-start | bytes 12582920 | tf_op jit(solution)/shard_map/ppermute | solution.py:295
  14.3 6.2 %collective-permute-start.1 = (bf16[144,512]{1,0:T(8,128)(2,1)S(1)}, bf16[144,512]{1,0:T(8,128)(2,1)S(1)}, u32[]{:S(2)}, u32[]{:S(2)}) collective-permute-start(bf16[144,512]{1,0:T(8,128)(2,1)S(1)} %collective-permute-done.refs_2_), channel_id=1, source_target_pairs={{0,4},{1,5},{4,8},{5,9},{8,12},{9,13},{12,14},{13,15},{14,10},{15,... | collective-permute-start | bytes 442376 | tf_op jit(solution)/shard_map/ppermute | solution.py:292
  16.2 6.2 %collective-permute-start.5 = (bf16[144,512]{1,0:T(8,128)(2,1)S(1)}, bf16[144,512]{1,0:T(8,128)(2,1)S(1)}, u32[]{:S(2)}, u32[]{:S(2)}) collective-permute-start(bf16[144,512]{1,0:T(8,128)(2,1)S(1)} %copy-done.2), channel_id=1, source_target_pairs={{0,2},{1,3},{4,0},{5,1},{8,4},{9,5},{12,8},{13,9},{14,12},{15,13},... | collective-permute-start | bytes 442376 | tf_op jit(solution)/shard_map/ppermute | solution.py:292
  20.6 5.4 %collective-permute-start.2 = (bf16[144,512]{1,0:T(8,128)(2,1)S(1)}, bf16[144,512]{1,0:T(8,128)(2,1)S(1)}, u32[]{:S(2)}, u32[]{:S(2)}) collective-permute-start(bf16[144,512]{1,0:T(8,128)(2,1)S(1)} %collective-permute-done.1.refs_6_), channel_id=1, source_target_pairs={{0,4},{1,5},{4,8},{5,9},{8,12},{9,13},{12,14},{13,15},{14,10},{15,... | collective-permute-start | bytes 442376 | tf_op jit(solution)/shard_map/ppermute | solution.py:292
  22.4 6.3 %collective-permute-start.8 = (bf16[144,512]{1,0:T(8,128)(2,1)S(1)}, bf16[144,512]{1,0:T(8,128)(2,1)S(1)}, u32[]{:S(2)}, u32[]{:S(2)}) collective-permute-start(bf16[144,512]{1,0:T(8,128)(2,1)S(1)} %collective-permute-done.5.refs_4_), channel_id=1, source_target_pairs={{0,2},{1,3},{4,0},{5,1},{8,4},{9,5},{12,8},{13,9},{14,12},{15,13},... | collective-permute-start | bytes 442376 | tf_op jit(solution)/shard_map/ppermute | solution.py:292
  22.6 6.3 %collective-permute-start.4 = (bf16[144,512]{1,0:T(8,128)(2,1)S(1)}, bf16[144,512]{1,0:T(8,128)(2,1)S(1)}, u32[]{:S(2)}, u32[]{:S(2)}) collective-permute-start(bf16[144,512]{1,0:T(8,128)(2,1)S(1)} %collective-permute-done.refs_2_), channel_id=1, source_target_pairs={{0,1},{1,0},{2,3},{3,2},{4,5},{5,4},{6,7},{7,6},{8,9},{9,8},{10,11... | collective-permute-start | bytes 442376 | tf_op jit(solution)/shard_map/ppermute | solution.py:295
  28.6 5.5 %collective-permute-start.11 = (bf16[144,512]{1,0:T(8,128)(2,1)S(1)}, bf16[144,512]{1,0:T(8,128)(2,1)S(1)}, u32[]{:S(2)}, u32[]{:S(2)}) collective-permute-start(bf16[144,512]{1,0:T(8,128)(2,1)S(1)} %collective-permute-done.8.refs_8_), channel_id=1, source_target_pairs={{0,2},{1,3},{4,0},{5,1},{8,4},{9,5},{12,8},{13,9},{14,12},{15,13},... | collective-permute-start | bytes 442376 | tf_op jit(solution)/shard_map/ppermute | solution.py:292
  28.9 5.3 %collective-permute-start.13 = (bf16[144,512]{1,0:T(8,128)(2,1)S(1)}, bf16[144,512]{1,0:T(8,128)(2,1)S(1)}, u32[]{:S(2)}, u32[]{:S(2)}) collective-permute-start(bf16[144,512]{1,0:T(8,128)(2,1)S(1)} %collective-permute-done.2.refs_10_), channel_id=1, source_target_pairs={{0,4},{1,5},{4,8},{5,9},{8,12},{9,13},{12,14},{13,15},{14,10},{15,... | collective-permute-start | bytes 442376 | tf_op jit(solution)/shard_map/ppermute | solution.py:292
  30.7 6.5 %collective-permute-start.10 = (bf16[144,512]{1,0:T(8,128)(2,1)S(1)}, bf16[144,512]{1,0:T(8,128)(2,1)S(1)}, u32[]{:S(2)}, u32[]{:S(2)}) collective-permute-start(bf16[144,512]{1,0:T(8,128)(2,1)S(1)} %collective-permute-done.2.refs_10_), channel_id=1, source_target_pairs={{0,1},{1,0},{2,3},{3,2},{4,5},{5,4},{6,7},{7,6},{8,9},{9,8},{10,11... | collective-permute-start | bytes 442376 | tf_op jit(solution)/shard_map/ppermute | solution.py:295
  34.2 7.6 %collective-permute-start.14 = (bf16[144,512]{1,0:T(8,128)(2,1)S(1)}, bf16[144,512]{1,0:T(8,128)(2,1)S(1)}, u32[]{:S(2)}, u32[]{:S(2)}) collective-permute-start(bf16[144,512]{1,0:T(8,128)(2,1)S(1)} %collective-permute-done.13.refs_14_), channel_id=1, source_target_pairs={{0,1},{1,0},{2,3},{3,2},{4,5},{5,4},{6,7},{7,6},{8,9},{9,8},{10,11... | collective-permute-start | bytes 442376 | tf_op jit(solution)/shard_map/ppermute | solution.py:295
  34.6 18.5 %collective-permute-start.16 = (bf16[2,256,128]{2,1,0:T(8,128)(2,1)S(1)}, bf16[2,256,128]{2,1,0:T(8,128)(2,1)S(1)}, u32[]{:S(2)}, u32[]{:S(2)}) collective-permute-start(bf16[2,256,128]{2,1,0:T(8,128)(2,1)S(1)} %get-tuple-element.65), channel_id=1, source_target_pairs={{0,8},{1,9},{2,10},{3,11},{4,12},{5,13},{6,14},{7,15},{8,0},{9,1},... | collective-permute-start | bytes 393224 | tf_op jit(solution)/shard_map/ppermute | solution.py:295
  37.2 19.3 %collective-permute-start.17 = (bf16[2,256,128]{2,1,0:T(8,128)(2,1)S(1)}, bf16[2,256,128]{2,1,0:T(8,128)(2,1)S(1)}, u32[]{:S(2)}, u32[]{:S(2)}) collective-permute-start(bf16[2,256,128]{2,1,0:T(8,128)(2,1)S(1)} %get-tuple-element.66), channel_id=1, source_target_pairs={{0,10},{1,11},{2,8},{3,9},{4,14},{5,15},{6,12},{7,13},{8,2},{9,3},... | collective-permute-start | bytes 393224 | tf_op jit(solution)/shard_map/ppermute | solution.py:295
  38.2 18.6 %collective-permute-start.18 = (bf16[2,256,128]{2,1,0:T(8,128)(2,1)S(1)}, bf16[2,256,128]{2,1,0:T(8,128)(2,1)S(1)}, u32[]{:S(2)}, u32[]{:S(2)}) collective-permute-start(bf16[2,256,128]{2,1,0:T(8,128)(2,1)S(1)} %get-tuple-element.67), channel_id=1, source_target_pairs={{0,12},{1,13},{2,14},{3,15},{4,8},{5,9},{6,10},{7,11},{8,4},{9,5},... | collective-permute-start | bytes 393224 | tf_op jit(solution)/shard_map/ppermute | solution.py:295
  41.8 15.6 %collective-permute-start.19 = (bf16[2,256,128]{2,1,0:T(8,128)(2,1)S(1)}, bf16[2,256,128]{2,1,0:T(8,128)(2,1)S(1)}, u32[]{:S(2)}, u32[]{:S(2)}) collective-permute-start(bf16[2,256,128]{2,1,0:T(8,128)(2,1)S(1)} %get-tuple-element.68), channel_id=1, source_target_pairs={{0,14},{1,15},{2,12},{3,13},{4,10},{5,11},{6,8},{7,9},{8,6},{9,7},... | collective-permute-start | bytes 393224 | tf_op jit(solution)/shard_map/ppermute | solution.py:295
  53.1 5.2 %collective-permute-start.20 = (bf16[2,256,128]{2,1,0:T(8,128)(2,1)S(1)}, bf16[2,256,128]{2,1,0:T(8,128)(2,1)S(1)}, u32[]{:S(2)}, u32[]{:S(2)}) collective-permute-start(bf16[2,256,128]{2,1,0:T(8,128)(2,1)S(1)} %get-tuple-element.63), channel_id=1, source_target_pairs={{0,4},{1,5},{2,6},{3,7},{4,0},{5,1},{6,2},{7,3},{8,12},{9,13},{10,... | collective-permute-start | bytes 393224 | tf_op jit(solution)/shard_map/ppermute | solution.py:295
  56.5 5.9 %collective-permute-start.21 = (bf16[2,256,128]{2,1,0:T(8,128)(2,1)S(1)}, bf16[2,256,128]{2,1,0:T(8,128)(2,1)S(1)}, u32[]{:S(2)}, u32[]{:S(2)}) collective-permute-start(bf16[2,256,128]{2,1,0:T(8,128)(2,1)S(1)} %get-tuple-element.72), channel_id=1, source_target_pairs={{0,6},{1,7},{2,4},{3,5},{4,2},{5,3},{6,0},{7,1},{8,14},{9,15},{10,... | collective-permute-start | bytes 393224 | tf_op jit(solution)/shard_map/ppermute | solution.py:295
  56.8 8.0 %collective-permute-start.22 = (bf16[2,256,128]{2,1,0:T(8,128)(2,1)S(1)}, bf16[2,256,128]{2,1,0:T(8,128)(2,1)S(1)}, u32[]{:S(2)}, u32[]{:S(2)}) collective-permute-start(bf16[2,256,128]{2,1,0:T(8,128)(2,1)S(1)} %get-tuple-element.73), channel_id=1, source_target_pairs={{0,2},{1,3},{2,0},{3,1},{4,6},{5,7},{6,4},{7,5},{8,10},{9,11},{10,... | collective-permute-start | bytes 393224 | tf_op jit(solution)/shard_map/ppermute | solution.py:295
  57.4 7.9 %collective-permute-start.30 = (bf16[128,128]{1,0:T(8,128)(2,1)S(1)}, bf16[128,128]{1,0:T(8,128)(2,1)S(1)}, u32[]{:S(2)}, u32[]{:S(2)}) collective-permute-start(bf16[128,128]{1,0:T(8,128)(2,1)S(1)} %get-tuple-element.82.refs_16_), channel_id=1, source_target_pairs={{0,1},{1,0},{2,3},{3,2},{4,5},{5,4},{6,7},{7,6},{8,9},{9,8},{10,11... | collective-permute-start | bytes 98312 | tf_op jit(solution)/shard_map/ppermute | solution.py:295
  58.3 7.0 %collective-permute-start.15 = (bf16[2,256,128]{2,1,0:T(8,128)(2,1)S(1)}, bf16[2,256,128]{2,1,0:T(8,128)(2,1)S(1)}, u32[]{:S(2)}, u32[]{:S(2)}) collective-permute-start(bf16[2,256,128]{2,1,0:T(8,128)(2,1)S(1)} %get-tuple-element.71.refs_0_), channel_id=1, source_target_pairs={{0,1},{1,0},{2,3},{3,2},{4,5},{5,4},{6,7},{7,6},{8,9},{9,8},{10,11... | collective-permute-start | bytes 393224 | tf_op jit(solution)/shard_map/ppermute | solution.py:295
  73.6 6.1 %collective-permute-start.33 = (bf16[128,512]{1,0:T(8,128)(2,1)S(1)}, bf16[128,512]{1,0:T(8,128)(2,1)S(1)}, u32[]{:S(2)}, u32[]{:S(2)}) collective-permute-start(bf16[128,512]{1,0:T(8,128)(2,1)S(1)} %get-tuple-element.88), channel_id=1, source_target_pairs={{0,4},{1,5},{4,8},{5,9},{8,12},{9,13},{12,14},{13,15},{14,10},{15,... | collective-permute-start | bytes 393224 | tf_op jit(solution)/shard_map/ppermute | solution.py:292
  76.6 5.9 %collective-permute-start.37 = (bf16[128,512]{1,0:T(8,128)(2,1)S(1)}, bf16[128,512]{1,0:T(8,128)(2,1)S(1)}, u32[]{:S(2)}, u32[]{:S(2)}) collective-permute-start(bf16[128,512]{1,0:T(8,128)(2,1)S(1)} %get-tuple-element.92), channel_id=1, source_target_pairs={{0,2},{1,3},{4,0},{5,1},{8,4},{9,5},{12,8},{13,9},{14,12},{15,13},... | collective-permute-start | bytes 393224 | tf_op jit(solution)/shard_map/ppermute | solution.py:292
  82.6 5.1 %collective-permute-start.38 = (bf16[128,512]{1,0:T(8,128)(2,1)S(1)}, bf16[128,512]{1,0:T(8,128)(2,1)S(1)}, u32[]{:S(2)}, u32[]{:S(2)}) collective-permute-start(bf16[128,512]{1,0:T(8,128)(2,1)S(1)} %add_convert_fusion.2), channel_id=1, source_target_pairs={{0,2},{1,3},{4,0},{5,1},{8,4},{9,5},{12,8},{13,9},{14,12},{15,13},... | collective-permute-start | bytes 393224 | tf_op jit(solution)/shard_map/ppermute | solution.py:292
  84.8 5.4 %collective-permute-start.35 = (bf16[128,512]{1,0:T(8,128)(2,1)S(1)}, bf16[128,512]{1,0:T(8,128)(2,1)S(1)}, u32[]{:S(2)}, u32[]{:S(2)}) collective-permute-start(bf16[128,512]{1,0:T(8,128)(2,1)S(1)} %add_convert_fusion.4), channel_id=1, source_target_pairs={{0,4},{1,5},{4,8},{5,9},{8,12},{9,13},{12,14},{13,15},{14,10},{15,... | collective-permute-start | bytes 393224 | tf_op jit(solution)/shard_map/ppermute | solution.py:292
  (22 other events, 126.9 us)

commit v3 on v2

v3 whole, which is shorter than its diff:
```python
import functools
import math

import jax
import jax.numpy as jnp
from jax import lax
from jax.experimental import pallas as pl
from jax.experimental.pallas import tpu as pltpu
from jax.sharding import PartitionSpec as P

H = 64
KV = 8
DH = 128
EPS = 1e-05
PAD = 16
MIB = 1 << 20
TRANS_B = (((1,), (1,)), ((), ()))


def in_vmem(count):
    return [pl.BlockSpec(memory_space=pltpu.VMEM)] * count


def anywhere(count):
    return [pl.BlockSpec(memory_space=pl.ANY)] * count


def cost(flops, moved):
    return pl.CostEstimate(flops=flops, bytes_accessed=moved, transcendentals=0)


def params(mib):
    return pltpu.CompilerParams(vmem_limit_bytes=mib * MIB)


def chip_at(place, chips):
    return jnp.where(place < chips // 2, 2 * place, 2 * (chips - 1 - place) + 1)


def place_of(chip, chips):
    return jnp.where(lax.rem(chip, 2) == 0, lax.div(chip, 2), chips - 1 - lax.div(chip, 2))


def here():
    device = lax.axis_index("seq")
    return lax.div(device, 2), lax.rem(device, 2)


def neighbour_chip(offset, chips):
    chip, _ = here()
    return chip_at(lax.rem(place_of(chip, chips) + offset + chips, chips), chips)


def pack_kernel(tokens, gain, block, sem):
    rows, width = tokens.shape
    copy = pltpu.make_async_copy(tokens, block.at[pl.ds(0, rows), :], sem)
    copy.start()
    wide = gain[...].astype(jnp.float32).reshape(1, width)
    block[rows:, :] = jnp.broadcast_to(wide, (PAD, width)).astype(jnp.bfloat16)
    copy.wait()


def pack(tokens, gain):
    rows, width = tokens.shape
    return pl.pallas_call(
        pack_kernel,
        out_shape=pltpu.VMEM((rows + PAD, width), jnp.bfloat16),
        in_specs=anywhere(1) + in_vmem(1),
        out_specs=in_vmem(1)[0],
        scratch_shapes=[pltpu.SemaphoreType.DMA],
        name="pack",
    )(tokens, gain)


def cut_kernel(chips, cache, *pieces):
    chip, _ = here()
    for step, piece in enumerate(pieces):
        head = lax.div(lax.bitwise_xor(chip, step) * KV, chips)
        piece[...] = cache[:, :, pl.ds(pl.multiple_of(head * DH, DH), DH)]


def cut(cache, chips):
    shape = (2, cache.shape[1], DH)
    return pl.pallas_call(
        functools.partial(cut_kernel, chips),
        out_shape=[jax.ShapeDtypeStruct(shape, jnp.bfloat16)] * chips,
        in_specs=in_vmem(1),
        out_specs=in_vmem(chips),
        compiler_params=params(8),
        name="cut",
    )(cache)


def half_kernel(groups, chips, width, w_out, *refs):
    outs, sems = refs[:-1], refs[-1]
    _, core = here()
    copies = []
    for out, (mine, offsets) in zip(outs, groups):
        for number, offset in enumerate(offsets):
            column = 2 * neighbour_chip(offset, chips) + (core if mine else 1 - core)
            columns = pl.ds(pl.multiple_of(column * width, width), width)
            copy = pltpu.make_async_copy(w_out.at[:, columns], out.at[number], sems.at[len(copies)])
            copy.start()
            copies.append(copy)
    for copy in copies:
        copy.wait()


def in_hbm(value):
    return pltpu.with_memory_space_constraint(value, pltpu.HBM)


def half(w_out, chips, *groups):
    rows, columns = w_out.shape
    width = columns // (2 * chips)
    return pl.pallas_call(
        functools.partial(half_kernel, groups, chips, width),
        out_shape=[jax.ShapeDtypeStruct((len(offsets), rows, width), jnp.bfloat16) for _, offsets in groups],
        in_specs=anywhere(1),
        out_specs=in_vmem(len(groups)),
        scratch_shapes=[pltpu.SemaphoreType.DMA((sum(len(offsets) for _, offsets in groups),))],
        compiler_params=params(12),
        name="half",
    )(in_hbm(w_out))


def project_kernel(offsets, chips, rows, *refs):
    count = len(offsets)
    blocks = refs[:count]
    w_query, w_key, w_value, query_ref, own_ref, held, held_own, sems, own_sems = refs[count:]
    width = blocks[0].shape[1]
    side = w_key.shape[0]
    _, core = here()
    own_copies = [
        pltpu.make_async_copy(w_key, held_own.at[pl.ds(0, side), :], own_sems.at[0]),
        pltpu.make_async_copy(w_value, held_own.at[pl.ds(side, side), :], own_sems.at[1]),
    ]
    for copy in own_copies:
        copy.start()
    columns, copies = [], []
    for number, (offset, other) in enumerate(offsets):
        owner = 2 * neighbour_chip(offset, chips) + (1 - core if other else core)
        columns.append(pl.ds(pl.multiple_of(owner * width, width), width))
        copy = pltpu.make_async_copy(w_query.at[:, columns[number]], held.at[number], sems.at[number])
        copy.start()
        copies.append(copy)
    total = jnp.zeros((rows, 128), jnp.float32)
    for block in blocks:
        wide = block[:rows, :].astype(jnp.float32)
        square = wide * wide
        for lane in range(0, width, 128):
            total += square[:, lane : lane + 128]
    inverse = lax.rsqrt(jnp.sum(total, axis=1, keepdims=True) / (width * count) + EPS)
    query = jnp.zeros(query_ref.shape, jnp.float32)
    own = jnp.zeros(own_ref.shape, jnp.float32)
    for copy in own_copies:
        copy.wait()
    for number, block in enumerate(blocks):
        gain = block[rows : rows + PAD, :].astype(jnp.float32)[0:1, :]
        wide = block[:rows, :].astype(jnp.float32)
        normed = (wide * inverse * gain).astype(jnp.bfloat16)
        own += lax.dot_general(normed, held_own[:, columns[number]], TRANS_B, preferred_element_type=jnp.float32)
        copies[number].wait()
        query += lax.dot_general(normed, held[number], TRANS_B, preferred_element_type=jnp.float32)
    query_ref[...] = query.astype(jnp.bfloat16)
    own_ref[...] = own.astype(jnp.bfloat16)


def project(offsets, chips, blocks, w_query, w_key, w_value, rows):
    count, width = len(blocks), blocks[0].shape[1]
    return pl.pallas_call(
        functools.partial(project_kernel, offsets, chips, rows),
        out_shape=(
            jax.ShapeDtypeStruct((rows, w_query.shape[0]), jnp.bfloat16),
            jax.ShapeDtypeStruct((rows, 2 * w_key.shape[0]), jnp.bfloat16),
        ),
        in_specs=in_vmem(count) + anywhere(3),
        out_specs=tuple(in_vmem(2)),
        scratch_shapes=[
            pltpu.VMEM((count, w_query.shape[0], width), jnp.bfloat16),
            pltpu.VMEM((2 * w_key.shape[0], w_key.shape[1]), jnp.bfloat16),
            pltpu.SemaphoreType.DMA((count,)),
            pltpu.SemaphoreType.DMA((2,)),
        ],
        compiler_params=params(24),
        name="project",
    )(*blocks, in_hbm(w_query), in_hbm(w_key), in_hbm(w_value))


def weigh(query, caches, scores, top, total, numerator):
    scale = 1.0 / math.sqrt(DH)
    step = caches[0].shape[1]
    best = None
    for number, cache in enumerate(caches):
        part = lax.dot_general(query, cache[0], TRANS_B, preferred_element_type=jnp.float32)
        scores[:, number * step : (number + 1) * step] = part
        for lane in range(0, step, 128):
            piece = part[:, lane : lane + 128]
            best = piece if best is None else jnp.maximum(best, piece)
    before = top
    top = jnp.maximum(jnp.max(best, axis=1, keepdims=True) * scale, top)
    shrink = jnp.exp(before - top)
    total, numerator = total * shrink, numerator * shrink
    for number, cache in enumerate(caches):
        weights = jnp.exp(scores[:, number * step : (number + 1) * step] * scale - top)
        for lane in range(0, step, 128):
            total += weights[:, lane : lane + 128]
        numerator += jnp.dot(weights.astype(jnp.bfloat16), cache[1], preferred_element_type=jnp.float32)
    return top, total, numerator


def begin_kernel(count, parts, heads, *refs):
    caches, owns = refs[:count], refs[count : count + parts]
    mine, other, query_all, top_ref, total_ref, numerator_ref, scores = refs[count + parts :]
    rows = mine.shape[0]
    lines = heads * rows
    side = owns[0].shape[1] // 2
    _, core = here()
    own_parts = [own[...].astype(jnp.float32) for own in owns]
    if parts == 2:
        own_parts = [jnp.where(core == 0, own_parts[i], own_parts[1 - i]) for i in range(2)]
    own_key = jnp.concatenate([part[:, :side] for part in own_parts], axis=1)
    own_value = jnp.concatenate([part[:, side:] for part in own_parts], axis=1)
    for number, query_ref in enumerate((mine, other)):
        for head in range(heads):
            start = number * lines + head * rows
            query_all[start : start + rows, :] = query_ref[:, head * DH : (head + 1) * DH]
    query = query_all[...]
    keys_own = jnp.concatenate([own_key] * (2 * heads), axis=0)
    own = jnp.sum(query.astype(jnp.float32) * keys_own, axis=1, keepdims=True) / math.sqrt(DH)
    lane = lax.broadcasted_iota(jnp.int32, (2 * lines, 128), 1)
    line = lax.broadcasted_iota(jnp.int32, (2 * lines, 128), 0)
    total = jnp.where((lane == 0) & (line < lines), 1.0, 0.0)
    numerator = jnp.concatenate([own_value] * heads + [jnp.zeros((lines, DH), jnp.float32)], axis=0)
    top, total, numerator = weigh(query, caches, scores, own, total, numerator)
    top_ref[...] = jnp.broadcast_to(top, top_ref.shape)
    total_ref[...] = total
    numerator_ref[...] = numerator


def begin(caches, owns, mine, other):
    count, rows = len(caches), mine.shape[0]
    heads = mine.shape[1] // DH
    lines = 2 * heads * rows
    positions = count * caches[0].shape[1]
    return pl.pallas_call(
        functools.partial(begin_kernel, count, len(owns), heads),
        out_shape=[jax.ShapeDtypeStruct((lines, DH), jnp.bfloat16)]
        + [jax.ShapeDtypeStruct((lines, 128), jnp.float32)] * 3,
        in_specs=in_vmem(count + len(owns) + 2),
        out_specs=in_vmem(4),
        scratch_shapes=[pltpu.VMEM((lines, positions), jnp.float32)],
        compiler_params=params(24),
        cost_estimate=cost(1, 1),
        name="begin",
    )(*caches, *owns, mine, other)


def finish_kernel(count, *refs):
    caches = refs[:count]
    query_all, top_ref, total_ref, numerator_ref, state_ref, sum_ref, scores = refs[count:]
    top, total, numerator = weigh(
        query_all[...], caches, scores, top_ref[:, 0:1], total_ref[...], numerator_ref[...]
    )
    lane = lax.broadcasted_iota(jnp.int32, total.shape, 1)
    state_ref[...] = jnp.where(lane < 64, top, jnp.sum(total, axis=1, keepdims=True))
    sum_ref[...] = numerator


def finish(caches, state):
    count = len(caches)
    lines = state[0].shape[0]
    positions = count * caches[0].shape[1]
    return pl.pallas_call(
        functools.partial(finish_kernel, count),
        out_shape=[jax.ShapeDtypeStruct((lines, 128), jnp.float32)] * 2,
        in_specs=in_vmem(count + 4),
        out_specs=in_vmem(2),
        scratch_shapes=[pltpu.VMEM((lines, positions), jnp.float32)],
        compiler_params=params(24),
        name="finish",
    )(*caches, *state)


def output_term(attention, weights):
    return sum(
        jnp.dot(part, weight, preferred_element_type=jnp.float32) for part, weight in zip(attention, weights)
    )


def merge_kernel(rows, *refs):
    state, sums, far_state, far_sums, mine, other = refs[:6]
    attention_ref, outs = refs[6], refs[7:]
    lines = state.shape[0] // 2
    heads = lines // rows
    parts = []
    for number in range(2):
        near_lines = slice(number * lines, (number + 1) * lines)
        far_lines = slice((1 - number) * lines, (2 - number) * lines)
        top, far_top = state[near_lines, 0:1], far_state[far_lines, 0:1]
        peak = jnp.maximum(top, far_top)
        scale, far_scale = jnp.exp(top - peak), jnp.exp(far_top - peak)
        denominator = state[near_lines, 64:65] * scale + far_state[far_lines, 64:65] * far_scale
        numerator = sums[near_lines, :] * scale + far_sums[far_lines, :] * far_scale
        result = (numerator / denominator).astype(jnp.bfloat16)
        for head in range(heads):
            attention_ref[number, :, head * DH : (head + 1) * DH] = result[head * rows : (head + 1) * rows, :]
        parts.append(attention_ref[number])
    for number, out in enumerate(outs):
        out[...] = output_term(parts, (mine[number], other[number])).astype(out.dtype)


def merge(state, sums, far_state, far_sums, mine, other, rows):
    count, depth, width = mine.shape
    return pl.pallas_call(
        functools.partial(merge_kernel, rows),
        out_shape=[jax.ShapeDtypeStruct((2, rows, depth), jnp.bfloat16)]
        + [jax.ShapeDtypeStruct((rows, width), jnp.bfloat16)] * count,
        in_specs=in_vmem(6),
        out_specs=in_vmem(1 + count),
        compiler_params=params(16),
        name="merge",
    )(state, sums, far_state, far_sums, mine, other)


def rest_kernel(attention, mine, other, *outs):
    for number, out in enumerate(outs):
        out[...] = output_term((attention[0], attention[1]), (mine[number], other[number]))


def rest(attention, mine, other):
    count, _, width = mine.shape
    return pl.pallas_call(
        rest_kernel,
        out_shape=[jax.ShapeDtypeStruct((attention.shape[1], width), jnp.float32)] * count,
        in_specs=in_vmem(3),
        out_specs=in_vmem(count),
        compiler_params=params(12),
        name="rest",
    )(attention, mine, other)


def body(tokens, gain, w_query, w_key, w_value, w_out, prefix_cache, size):
    chips = size // 2
    outer = chips // 2
    cycle = [2 * a for a in range(outer)] + [2 * a + 1 for a in reversed(range(outer))]

    def around(value, step):
        pairs = [
            (2 * cycle[p] + k, 2 * cycle[(p + step) % chips] + k) for p in range(chips) for k in (0, 1)
        ]
        return lax.ppermute(value, "seq", pairs)

    def swap(value, bits):
        return lax.ppermute(value, "seq", [(i, i ^ bits) for i in range(size)])

    rows = tokens.shape[0]

    block = pack(tokens, gain)
    blocks, offsets = [], []

    def take(value, offset):
        blocks.extend([value, swap(value, 1)])
        offsets.extend([(offset, False), (offset, True)])

    right = left = block
    reach = chips // 2
    take(block, 0)
    for step in range(1, reach + 1):
        right = around(right, 1)
        if step == min(2, reach):
            prefix_cache, right = lax.optimization_barrier((prefix_cache, right))
        if step == max(reach - 1, 1):
            pieces = cut(prefix_cache, chips)
            pieces, right = lax.optimization_barrier((pieces, right))
        take(right, -step)
        if step < reach:
            left = around(left, -1)
            take(left, step)

    parts = {step: swap(pieces[step], 2 * step) for step in [*range(reach, chips), *range(1, reach)]}
    query, own = project(tuple(offsets), chips, blocks, w_query, w_key, w_value, rows)

    sharers = size // KV
    other_query = swap(query, 1)
    if sharers == 2:
        owns = [own, swap(own, 1)]
    else:
        groups = [list(range(g * sharers, (g + 1) * sharers)) for g in range(KV)]
        gathered = lax.all_gather(own, "seq", axis=0, axis_index_groups=groups)
        owns = [gathered[i] for i in range(sharers)]

    first = tuple([reach] + ([chips - reach + 1] if reach > 1 else []))
    others = tuple(offset for offset in range(chips) if offset not in first)
    w_out, query = lax.optimization_barrier((w_out, query))
    send_first, send_others, mine_first, mine_others = half(
        w_out, chips, (False, first), (False, others), (True, first), (True, others)
    )
    other_first = swap(send_first, 1)
    far_parts = [parts[step] for step in range(reach, chips)]
    send_others, far_parts, owns, other_query = lax.optimization_barrier(
        (send_others, far_parts, owns, other_query)
    )
    other_others = swap(send_others, 1)

    query, mine_first = lax.optimization_barrier((query, mine_first))
    state = begin(far_parts, owns, query, other_query)
    state, sums = finish([pieces[0]] + [parts[step] for step in range(1, reach)], state)

    attention, *terms = merge(state, sums, swap(state, 1), swap(sums, 1), mine_first, other_first, rows)
    terms = dict(zip(first, terms))
    terms.update(zip(others, rest(attention, mine_others, other_others)))
    right = left = None
    for step in reversed(range(1, reach + 1)):
        term = terms[step]
        right = term if right is None else (right.astype(jnp.float32) + term).astype(jnp.bfloat16)
        right = around(right, 1)
        if step < reach:
            term = terms[chips - step]
            left = term if left is None else (left.astype(jnp.float32) + term).astype(jnp.bfloat16)
            left = around(left, -1)
    total = terms[0] + right.astype(jnp.float32)
    if left is not None:
        total += left.astype(jnp.float32)
    return total.astype(jnp.bfloat16)


def solution(mesh):
    return jax.shard_map(
        functools.partial(body, size=mesh.shape["seq"]),
        mesh=mesh,
        in_specs=(
            P("group", "seq"),
            P("seq"),
            P("seq", None),
            P("seq", None),
            P("seq", None),
            P("seq", None),
            P(None, ("group", "seq"), None),
        ),
        out_specs=P("group", "seq"),
        check_vma=False,
    )
```

time: 96.3 us -> 89.3 us (0.927)
  waiting for transfers between devices: 39.7 us -> 29.3 us
  Pallas kernels: 16.6 us -> 22.6 us
  local copies, waits for them, and re-layouts: 6.78 us -> 1.22 us
  starting transfers between devices: 31.9 us -> 34.8 us
    ppermute x26 -> x21, waiting for transfers between devices: 13.1 us -> 7.38 us  [swap(): return lax.ppermute(value, 'seq', [(i, i ^ bits) for i in range(size)])]
    unnamed x12 -> x2, local copies, waits for them, and re-layouts: 6.78 us -> 1.22 us
    ppermute x26 -> x21, starting transfers between devices: 12.3 us -> 17.6 us  [swap(): return lax.ppermute(value, 'seq', [(i, i ^ bits) for i in range(size)])]
    ppermute x14, waiting for transfers between devices: 26.6 us -> 21.9 us  [around(): return lax.ppermute(value, 'seq', pairs)]
    pallas_call x6, Pallas kernels: 9.24 us -> 13.1 us  [the longest x1 3.57 us: half(): pl.pallas_call(functools.partial(half_kernel, groups, chips, width), out_...]
    ppermute x14, starting transfers between devices: 19.6 us -> 17.2 us  [around(): return lax.ppermute(value, 'seq', pairs)]
    pallas_call x1, Pallas kernels: 7.09 us -> 9.28 us  [project(): pl.pallas_call(functools.partial(project_kernel, offsets, chips, rows), o...]
  transfers between devices with their start and end apart: 40 -> 35, of which waited for: 23 -> 16; matrix products, arithmetic and copies ran while one was open for 0% -> 0% of each run, Pallas kernels for 13% -> 24%
where the time goes in v3:
time: 89.3 us; the launch traced here: 89.1 us
  starting transfers between devices  34.8 us (39%)
  waiting for transfers between devices  29.3 us (33%)
  Pallas kernels  22.6 us (25%)
  local copies, waits for them, and re-layouts  1.22 us (1%)
    ppermute x14, waiting for transfers between devices, around(): return lax.ppermute(value, 'seq', pairs)  21.9 us
    ppermute x21, starting transfers between devices, swap(): return lax.ppermute(value, 'seq', [(i, i ^ bits) for i in range(size)])  17.6 us
    ppermute x14, starting transfers between devices, around(): return lax.ppermute(value, 'seq', pairs)  17.2 us
    pallas_call x1, Pallas kernels, project(): pl.pallas_call(functools.partial(project_kernel, offsets, chips, rows), o...  9.28 us
    ppermute x21, waiting for transfers between devices, swap(): return lax.ppermute(value, 'seq', [(i, i ^ bits) for i in range(size)])  7.38 us
    pallas_call x1, Pallas kernels, half(): pl.pallas_call(functools.partial(half_kernel, groups, chips, width), out_...  3.57 us
    pallas_call x1, Pallas kernels, finish(): pl.pallas_call(functools.partial(finish_kernel, count), out_shape=[jax.Sh...  3.1 us
    pallas_call x1, Pallas kernels, begin(): pl.pallas_call(functools.partial(begin_kernel, count, len(owns), heads),...  2.46 us
  transfers between devices with their start and end apart: 35, of which 16 were waited for; matrix products, arithmetic and copies ran while one was open for 0% of the time, Pallas kernels for 24%

profile of v3, /device:TPU:0, one launch (start us, length us, event | category | flops | bytes accessed | tf_op | source)
XLA Modules:
  0.0 89.1 jit_solution(4838565484100010466)
XLA Ops:
  0.0 1.6 %pack.1.refs_0_ = bf16[144,512]{1,0:T(8,128)(2,1)S(1)} custom-call(bf16[128,512]{1,0:T(8,128)(2,1)} %tokens.1, bf16[512]{0:T(512)(128)(2,1)} %gain.1), custom_call_target="tpu_custom_call" | custom-call | tf_op jit(solution)/shard_map/pack/pallas_call | solution.py:65
  1.6 3.1 %collective-permute-start = (bf16[144,512]{1,0:T(8,128)(2,1)S(1)}, bf16[144,512]{1,0:T(8,128)(2,1)S(1)}, u32[]{:S(2)}, u32[]{:S(2)}) collective-permute-start(bf16[144,512]{1,0:T(8,128)(2,1)S(1)} %pack.1.refs_0_), channel_id=1, source_target_pairs={{0,4},{1,5},{4,8},{5,9},{8,12},{9,13},{12,14},{13,15},{14,10},{15,... | collective-permute-start | bytes 442376 | tf_op jit(solution)/shard_map/ppermute | solution.py:352
  4.7 3.8 %collective-permute-done.refs_2_ = bf16[144,512]{1,0:T(8,128)(2,1)S(1)} collective-permute-done((bf16[144,512]{1,0:T(8,128)(2,1)S(1)}, bf16[144,512]{1,0:T(8,128)(2,1)S(1)}, u32[]{:S(2)}, u32[]{:S(2)}) %collective-permute-start) | collective-permute-done | bytes 147488 | tf_op jit(solution)/shard_map/ppermute | solution.py:352
  8.5 1.8 %collective-permute-start.1 = (bf16[144,512]{1,0:T(8,128)(2,1)S(1)}, bf16[144,512]{1,0:T(8,128)(2,1)S(1)}, u32[]{:S(2)}, u32[]{:S(2)}) collective-permute-start(bf16[144,512]{1,0:T(8,128)(2,1)S(1)} %collective-permute-done.refs_2_), channel_id=1, source_target_pairs={{0,4},{1,5},{4,8},{5,9},{8,12},{9,13},{12,14},{13,15},{14,10},{15,... | collective-permute-start | bytes 442376 | tf_op jit(solution)/shard_map/ppermute | solution.py:352
  10.5 3.1 %collective-permute-done.1.refs_6_ = bf16[144,512]{1,0:T(8,128)(2,1)S(1)} collective-permute-done((bf16[144,512]{1,0:T(8,128)(2,1)S(1)}, bf16[144,512]{1,0:T(8,128)(2,1)S(1)}, u32[]{:S(2)}, u32[]{:S(2)}) %collective-permute-start.1) | collective-permute-done | bytes 147488 | tf_op jit(solution)/shard_map/ppermute | solution.py:352
  13.6 1.8 %collective-permute-start.2 = (bf16[144,512]{1,0:T(8,128)(2,1)S(1)}, bf16[144,512]{1,0:T(8,128)(2,1)S(1)}, u32[]{:S(2)}, u32[]{:S(2)}) collective-permute-start(bf16[144,512]{1,0:T(8,128)(2,1)S(1)} %collective-permute-done.1.refs_6_), channel_id=1, source_target_pairs={{0,4},{1,5},{4,8},{5,9},{8,12},{9,13},{12,14},{13,15},{14,10},{15,... | collective-permute-start | bytes 442376 | tf_op jit(solution)/shard_map/ppermute | solution.py:352
  18.8 1.8 %collective-permute-start.16 = (bf16[144,512]{1,0:T(8,128)(2,1)S(1)}, bf16[144,512]{1,0:T(8,128)(2,1)S(1)}, u32[]{:S(2)}, u32[]{:S(2)}) collective-permute-start(bf16[144,512]{1,0:T(8,128)(2,1)S(1)} %collective-permute-done.2.refs_10_), channel_id=1, source_target_pairs={{0,4},{1,5},{4,8},{5,9},{8,12},{9,13},{12,14},{13,15},{14,10},{15,... | collective-permute-start | bytes 442376 | tf_op jit(solution)/shard_map/ppermute | solution.py:352
  21.1 2.7 %collective-permute-done.14.refs_12_ = bf16[144,512]{1,0:T(8,128)(2,1)S(1)} collective-permute-done((bf16[144,512]{1,0:T(8,128)(2,1)S(1)}, bf16[144,512]{1,0:T(8,128)(2,1)S(1)}, u32[]{:S(2)}, u32[]{:S(2)}) %collective-permute-start.14) | collective-permute-done | bytes 147488 | tf_op jit(solution)/shard_map/ppermute | solution.py:352
  24.3 2.6 %collective-permute-start.18 = (bf16[2,256,128]{2,1,0:T(8,128)(2,1)S(1)}, bf16[2,256,128]{2,1,0:T(8,128)(2,1)S(1)}, u32[]{:S(2)}, u32[]{:S(2)}) collective-permute-start(bf16[2,256,128]{2,1,0:T(8,128)(2,1)S(1)} %get-tuple-element.75), channel_id=1, source_target_pairs={{0,8},{1,9},{2,10},{3,11},{4,12},{5,13},{6,14},{7,15},{8,0},{9,1},... | collective-permute-start | bytes 393224 | tf_op jit(solution)/shard_map/ppermute | solution.py:355
  28.0 3.6 %collective-permute-start.20 = (bf16[2,256,128]{2,1,0:T(8,128)(2,1)S(1)}, bf16[2,256,128]{2,1,0:T(8,128)(2,1)S(1)}, u32[]{:S(2)}, u32[]{:S(2)}) collective-permute-start(bf16[2,256,128]{2,1,0:T(8,128)(2,1)S(1)} %get-tuple-element.77), channel_id=1, source_target_pairs={{0,12},{1,13},{2,14},{3,15},{4,8},{5,9},{6,10},{7,11},{8,4},{9,5},... | collective-permute-start | bytes 393224 | tf_op jit(solution)/shard_map/ppermute | solution.py:355
  32.0 9.3 %project.1 = (bf16[128,512]{1,0:T(8,128)(2,1)S(1)}, bf16[128,128]{1,0:T(8,128)(2,1)S(1)}) custom-call(bf16[144,512]{1,0:T(8,128)(2,1)S(1)} %pack.1.refs_0_, bf16[144,512]{1,0:T(8,128)(2,1)S(1)} %collective-permute-done.6.refs_1_, bf16[144,512]{1,0:T(8,128)(2,1)S(1)} %collective-permute-done.refs_2_, bf16[144,512]{1,0:T(8,128)(2,1)S(1)} %collective-permute-done.7.refs_3_, ...), custom_call_target="tpu_custom_call" | custom-call | tf_op jit(solution)/shard_map/project/pallas_call | solution.py:171
  42.8 3.6 %half.1 = (bf16[2,512,512]{2,1,0:T(8,128)(2,1)S(1)}, bf16[6,512,512]{2,1,0:T(8,128)(2,1)S(1)}, bf16[2,512,512]{2,1,0:T(8,128)(2,1)S(1)}, bf16[6,512,512]{2,1,0:T(8,128)(2,1)S(1)}) custom-call(bf16[512,8192]{1,0:T(8,128)(2,1)} %w_out), custom_call_target="tpu_custom_call" | custom-call | tf_op jit(solution)/shard_map/half/pallas_call | solution.py:116
  48.4 5.0 %collective-permute-start.4 = (bf16[2,256,128]{2,1,0:T(8,128)(2,1)S(1)}, bf16[2,256,128]{2,1,0:T(8,128)(2,1)S(1)}, u32[]{:S(2)}, u32[]{:S(2)}) collective-permute-start(bf16[2,256,128]{2,1,0:T(8,128)(2,1)S(1)} %get-tuple-element.69), channel_id=1, source_target_pairs={{0,4},{1,5},{2,6},{3,7},{4,0},{5,1},{6,2},{7,3},{8,12},{9,13},{10,... | collective-permute-start | bytes 393224 | tf_op jit(solution)/shard_map/ppermute | solution.py:355
  54.1 2.5 %begin.1 = (bf16[1024,128]{1,0:T(8,128)(2,1)S(1)}, f32[1024,128]{1,0:T(8,128)S(1)}, f32[1024,128]{1,0:T(8,128)S(1)}, f32[1024,128]{1,0:T(8,128)S(1)}) custom-call(bf16[2,256,128]{2,1,0:T(8,128)(2,1)S(1)} %collective-permute-done.18.refs_0_, bf16[2,256,128]{2,1,0:T(8,128)(2,1)S(1)} %collective-permute-done.19.refs_1_, ...), custom_call_target="tpu_custom_call" | custom-call | flops 1 | bytes 1 | tf_op jit(solution)/shard_map/begin/pallas_call | solution.py:246
  57.3 3.0 %collective-permute-done.5.refs_3_ = bf16[2,256,128]{2,1,0:T(8,128)(2,1)S(1)} collective-permute-done((bf16[2,256,128]{2,1,0:T(8,128)(2,1)S(1)}, bf16[2,256,128]{2,1,0:T(8,128)(2,1)S(1)}, u32[]{:S(2)}, u32[]{:S(2)}) %collective-permute-start.5) | collective-permute-done | bytes 131104 | tf_op jit(solution)/shard_map/ppermute | solution.py:355
  60.4 3.1 %finish.1 = (f32[1024,128]{1,0:T(8,128)S(1)}, f32[1024,128]{1,0:T(8,128)S(1)}) custom-call(bf16[2,256,128]{2,1,0:T(8,128)(2,1)S(1)} %get-tuple-element.67.refs_0_, bf16[2,256,128]{2,1,0:T(8,128)(2,1)S(1)} %collective-permute-done.3.refs_1_, bf16[2,256,128]{2,1,0:T(8,128)(2,1)S(1)} %collective-permute-done.4.refs_2_, ...), custom_call_target="tpu_custom_call" | custom-call | tf_op jit(solution)/shard_map/finish/pallas_call | solution.py:274
  67.6 1.8 %collective-permute-start.28 = (bf16[128,512]{1,0:T(8,128)(2,1)S(1)}, bf16[128,512]{1,0:T(8,128)(2,1)S(1)}, u32[]{:S(2)}, u32[]{:S(2)}) collective-permute-start(bf16[128,512]{1,0:T(8,128)(2,1)S(1)} %get-tuple-element.102), channel_id=1, source_target_pairs={{0,4},{1,5},{4,8},{5,9},{8,12},{9,13},{12,14},{13,15},{14,10},{15,... | collective-permute-start | bytes 393224 | tf_op jit(solution)/shard_map/ppermute | solution.py:352
  70.7 2.5 %collective-permute-done.28 = bf16[128,512]{1,0:T(8,128)(2,1)S(1)} collective-permute-done((bf16[128,512]{1,0:T(8,128)(2,1)S(1)}, bf16[128,512]{1,0:T(8,128)(2,1)S(1)}, u32[]{:S(2)}, u32[]{:S(2)}) %collective-permute-start.28) | collective-permute-done | bytes 131104 | tf_op jit(solution)/shard_map/ppermute | solution.py:352
  73.2 1.9 %collective-permute-start.29 = (bf16[128,512]{1,0:T(8,128)(2,1)S(1)}, bf16[128,512]{1,0:T(8,128)(2,1)S(1)}, u32[]{:S(2)}, u32[]{:S(2)}) collective-permute-start(bf16[128,512]{1,0:T(8,128)(2,1)S(1)} %add_convert_fusion.5), channel_id=1, source_target_pairs={{0,4},{1,5},{4,8},{5,9},{8,12},{9,13},{12,14},{13,15},{14,10},{15,... | collective-permute-start | bytes 393224 | tf_op jit(solution)/shard_map/ppermute | solution.py:352
  75.6 2.6 %collective-permute-done.29 = bf16[128,512]{1,0:T(8,128)(2,1)S(1)} collective-permute-done((bf16[128,512]{1,0:T(8,128)(2,1)S(1)}, bf16[128,512]{1,0:T(8,128)(2,1)S(1)}, u32[]{:S(2)}, u32[]{:S(2)}) %collective-permute-start.29) | collective-permute-done | bytes 131104 | tf_op jit(solution)/shard_map/ppermute | solution.py:352
  78.3 1.9 %collective-permute-start.30 = (bf16[128,512]{1,0:T(8,128)(2,1)S(1)}, bf16[128,512]{1,0:T(8,128)(2,1)S(1)}, u32[]{:S(2)}, u32[]{:S(2)}) collective-permute-start(bf16[128,512]{1,0:T(8,128)(2,1)S(1)} %add_convert_fusion.4), channel_id=1, source_target_pairs={{0,4},{1,5},{4,8},{5,9},{8,12},{9,13},{12,14},{13,15},{14,10},{15,... | collective-permute-start | bytes 393224 | tf_op jit(solution)/shard_map/ppermute | solution.py:352
  80.7 2.6 %collective-permute-done.30 = bf16[128,512]{1,0:T(8,128)(2,1)S(1)} collective-permute-done((bf16[128,512]{1,0:T(8,128)(2,1)S(1)}, bf16[128,512]{1,0:T(8,128)(2,1)S(1)}, u32[]{:S(2)}, u32[]{:S(2)}) %collective-permute-start.30) | collective-permute-done | bytes 131104 | tf_op jit(solution)/shard_map/ppermute | solution.py:352
  83.3 2.2 %collective-permute-start.31 = (bf16[128,512]{1,0:T(8,128)(2,1)S(1)}, bf16[128,512]{1,0:T(8,128)(2,1)S(1)}, u32[]{:S(2)}, u32[]{:S(2)}) collective-permute-start(bf16[128,512]{1,0:T(8,128)(2,1)S(1)} %add_convert_fusion.3), channel_id=1, source_target_pairs={{0,4},{1,5},{4,8},{5,9},{8,12},{9,13},{12,14},{13,15},{14,10},{15,... | collective-permute-start | bytes 393224 | tf_op jit(solution)/shard_map/ppermute | solution.py:352
  85.7 2.6 %collective-permute-done.31 = bf16[128,512]{1,0:T(8,128)(2,1)S(1)} collective-permute-done((bf16[128,512]{1,0:T(8,128)(2,1)S(1)}, bf16[128,512]{1,0:T(8,128)(2,1)S(1)}, u32[]{:S(2)}, u32[]{:S(2)}) %collective-permute-start.31) | collective-permute-done | bytes 131104 | tf_op jit(solution)/shard_map/ppermute | solution.py:352
  (62 shorter events, 18.4 us)
Async XLA Ops:
  1.6 6.9 %collective-permute-start = (bf16[144,512]{1,0:T(8,128)(2,1)S(1)}, bf16[144,512]{1,0:T(8,128)(2,1)S(1)}, u32[]{:S(2)}, u32[]{:S(2)}) collective-permute-start(bf16[144,512]{1,0:T(8,128)(2,1)S(1)} %pack.1.refs_0_), channel_id=1, source_target_pairs={{0,4},{1,5},{4,8},{5,9},{8,12},{9,13},{12,14},{13,15},{14,10},{15,... | collective-permute-start | bytes 442376 | tf_op jit(solution)/shard_map/ppermute | solution.py:352
  4.7 5.6 %collective-permute-start.8 = (bf16[144,512]{1,0:T(8,128)(2,1)S(1)}, bf16[144,512]{1,0:T(8,128)(2,1)S(1)}, u32[]{:S(2)}, u32[]{:S(2)}) collective-permute-start(bf16[144,512]{1,0:T(8,128)(2,1)S(1)} %pack.1.refs_0_), channel_id=1, source_target_pairs={{0,2},{1,3},{4,0},{5,1},{8,4},{9,5},{12,8},{13,9},{14,12},{15,13},... | collective-permute-start | bytes 442376 | tf_op jit(solution)/shard_map/ppermute | solution.py:352
  8.5 5.1 %collective-permute-start.1 = (bf16[144,512]{1,0:T(8,128)(2,1)S(1)}, bf16[144,512]{1,0:T(8,128)(2,1)S(1)}, u32[]{:S(2)}, u32[]{:S(2)}) collective-permute-start(bf16[144,512]{1,0:T(8,128)(2,1)S(1)} %collective-permute-done.refs_2_), channel_id=1, source_target_pairs={{0,4},{1,5},{4,8},{5,9},{8,12},{9,13},{12,14},{13,15},{14,10},{15,... | collective-permute-start | bytes 442376 | tf_op jit(solution)/shard_map/ppermute | solution.py:352
  10.3 7.2 %collective-permute-start.11 = (bf16[144,512]{1,0:T(8,128)(2,1)S(1)}, bf16[144,512]{1,0:T(8,128)(2,1)S(1)}, u32[]{:S(2)}, u32[]{:S(2)}) collective-permute-start(bf16[144,512]{1,0:T(8,128)(2,1)S(1)} %collective-permute-done.8.refs_4_), channel_id=1, source_target_pairs={{0,2},{1,3},{4,0},{5,1},{8,4},{9,5},{12,8},{13,9},{14,12},{15,13},... | collective-permute-start | bytes 442376 | tf_op jit(solution)/shard_map/ppermute | solution.py:352
  13.6 5.1 %collective-permute-start.2 = (bf16[144,512]{1,0:T(8,128)(2,1)S(1)}, bf16[144,512]{1,0:T(8,128)(2,1)S(1)}, u32[]{:S(2)}, u32[]{:S(2)}) collective-permute-start(bf16[144,512]{1,0:T(8,128)(2,1)S(1)} %collective-permute-done.1.refs_6_), channel_id=1, source_target_pairs={{0,4},{1,5},{4,8},{5,9},{8,12},{9,13},{12,14},{13,15},{14,10},{15,... | collective-permute-start | bytes 442376 | tf_op jit(solution)/shard_map/ppermute | solution.py:352
  15.4 5.1 %collective-permute-start.6 = (bf16[144,512]{1,0:T(8,128)(2,1)S(1)}, bf16[144,512]{1,0:T(8,128)(2,1)S(1)}, u32[]{:S(2)}, u32[]{:S(2)}) collective-permute-start(bf16[144,512]{1,0:T(8,128)(2,1)S(1)} %pack.1.refs_0_), channel_id=1, source_target_pairs={{0,1},{1,0},{2,3},{3,2},{4,5},{5,4},{6,7},{7,6},{8,9},{9,8},{10,11... | collective-permute-start | bytes 442376 | tf_op jit(solution)/shard_map/ppermute | solution.py:355
  15.4 5.1 %collective-permute-start.9 = (bf16[144,512]{1,0:T(8,128)(2,1)S(1)}, bf16[144,512]{1,0:T(8,128)(2,1)S(1)}, u32[]{:S(2)}, u32[]{:S(2)}) collective-permute-start(bf16[144,512]{1,0:T(8,128)(2,1)S(1)} %collective-permute-done.8.refs_4_), channel_id=1, source_target_pairs={{0,1},{1,0},{2,3},{3,2},{4,5},{5,4},{6,7},{7,6},{8,9},{9,8},{10,11... | collective-permute-start | bytes 442376 | tf_op jit(solution)/shard_map/ppermute | solution.py:355
  15.9 7.8 %collective-permute-start.7 = (bf16[144,512]{1,0:T(8,128)(2,1)S(1)}, bf16[144,512]{1,0:T(8,128)(2,1)S(1)}, u32[]{:S(2)}, u32[]{:S(2)}) collective-permute-start(bf16[144,512]{1,0:T(8,128)(2,1)S(1)} %collective-permute-done.refs_2_), channel_id=1, source_target_pairs={{0,1},{1,0},{2,3},{3,2},{4,5},{5,4},{6,7},{7,6},{8,9},{9,8},{10,11... | collective-permute-start | bytes 442376 | tf_op jit(solution)/shard_map/ppermute | solution.py:355
  17.4 6.3 %collective-permute-start.14 = (bf16[144,512]{1,0:T(8,128)(2,1)S(1)}, bf16[144,512]{1,0:T(8,128)(2,1)S(1)}, u32[]{:S(2)}, u32[]{:S(2)}) collective-permute-start(bf16[144,512]{1,0:T(8,128)(2,1)S(1)} %collective-permute-done.11.refs_8_), channel_id=1, source_target_pairs={{0,2},{1,3},{4,0},{5,1},{8,4},{9,5},{12,8},{13,9},{14,12},{15,13},... | collective-permute-start | bytes 442376 | tf_op jit(solution)/shard_map/ppermute | solution.py:352
  18.8 5.5 %collective-permute-start.16 = (bf16[144,512]{1,0:T(8,128)(2,1)S(1)}, bf16[144,512]{1,0:T(8,128)(2,1)S(1)}, u32[]{:S(2)}, u32[]{:S(2)}) collective-permute-start(bf16[144,512]{1,0:T(8,128)(2,1)S(1)} %collective-permute-done.2.refs_10_), channel_id=1, source_target_pairs={{0,4},{1,5},{4,8},{5,9},{8,12},{9,13},{12,14},{13,15},{14,10},{15,... | collective-permute-start | bytes 442376 | tf_op jit(solution)/shard_map/ppermute | solution.py:352
  20.6 6.4 %collective-permute-start.10 = (bf16[144,512]{1,0:T(8,128)(2,1)S(1)}, bf16[144,512]{1,0:T(8,128)(2,1)S(1)}, u32[]{:S(2)}, u32[]{:S(2)}) collective-permute-start(bf16[144,512]{1,0:T(8,128)(2,1)S(1)} %collective-permute-done.1.refs_6_), channel_id=1, source_target_pairs={{0,1},{1,0},{2,3},{3,2},{4,5},{5,4},{6,7},{7,6},{8,9},{9,8},{10,11... | collective-permute-start | bytes 442376 | tf_op jit(solution)/shard_map/ppermute | solution.py:355
  23.8 7.9 %collective-permute-start.13 = (bf16[144,512]{1,0:T(8,128)(2,1)S(1)}, bf16[144,512]{1,0:T(8,128)(2,1)S(1)}, u32[]{:S(2)}, u32[]{:S(2)}) collective-permute-start(bf16[144,512]{1,0:T(8,128)(2,1)S(1)} %collective-permute-done.2.refs_10_), channel_id=1, source_target_pairs={{0,1},{1,0},{2,3},{3,2},{4,5},{5,4},{6,7},{7,6},{8,9},{9,8},{10,11... | collective-permute-start | bytes 442376 | tf_op jit(solution)/shard_map/ppermute | solution.py:355
  24.3 7.7 %collective-permute-start.17 = (bf16[144,512]{1,0:T(8,128)(2,1)S(1)}, bf16[144,512]{1,0:T(8,128)(2,1)S(1)}, u32[]{:S(2)}, u32[]{:S(2)}) collective-permute-start(bf16[144,512]{1,0:T(8,128)(2,1)S(1)} %collective-permute-done.16.refs_14_), channel_id=1, source_target_pairs={{0,1},{1,0},{2,3},{3,2},{4,5},{5,4},{6,7},{7,6},{8,9},{9,8},{10,11... | collective-permute-start | bytes 442376 | tf_op jit(solution)/shard_map/ppermute | solution.py:355
  24.3 18.4 %collective-permute-start.18 = (bf16[2,256,128]{2,1,0:T(8,128)(2,1)S(1)}, bf16[2,256,128]{2,1,0:T(8,128)(2,1)S(1)}, u32[]{:S(2)}, u32[]{:S(2)}) collective-permute-start(bf16[2,256,128]{2,1,0:T(8,128)(2,1)S(1)} %get-tuple-element.75), channel_id=1, source_target_pairs={{0,8},{1,9},{2,10},{3,11},{4,12},{5,13},{6,14},{7,15},{8,0},{9,1},... | collective-permute-start | bytes 393224 | tf_op jit(solution)/shard_map/ppermute | solution.py:355
  26.9 19.4 %collective-permute-start.19 = (bf16[2,256,128]{2,1,0:T(8,128)(2,1)S(1)}, bf16[2,256,128]{2,1,0:T(8,128)(2,1)S(1)}, u32[]{:S(2)}, u32[]{:S(2)}) collective-permute-start(bf16[2,256,128]{2,1,0:T(8,128)(2,1)S(1)} %get-tuple-element.76), channel_id=1, source_target_pairs={{0,10},{1,11},{2,8},{3,9},{4,14},{5,15},{6,12},{7,13},{8,2},{9,3},... | collective-permute-start | bytes 393224 | tf_op jit(solution)/shard_map/ppermute | solution.py:355
  28.0 18.4 %collective-permute-start.20 = (bf16[2,256,128]{2,1,0:T(8,128)(2,1)S(1)}, bf16[2,256,128]{2,1,0:T(8,128)(2,1)S(1)}, u32[]{:S(2)}, u32[]{:S(2)}) collective-permute-start(bf16[2,256,128]{2,1,0:T(8,128)(2,1)S(1)} %get-tuple-element.77), channel_id=1, source_target_pairs={{0,12},{1,13},{2,14},{3,15},{4,8},{5,9},{6,10},{7,11},{8,4},{9,5},... | collective-permute-start | bytes 393224 | tf_op jit(solution)/shard_map/ppermute | solution.py:355
  31.6 14.8 %collective-permute-start.21 = (bf16[2,256,128]{2,1,0:T(8,128)(2,1)S(1)}, bf16[2,256,128]{2,1,0:T(8,128)(2,1)S(1)}, u32[]{:S(2)}, u32[]{:S(2)}) collective-permute-start(bf16[2,256,128]{2,1,0:T(8,128)(2,1)S(1)} %get-tuple-element.78), channel_id=1, source_target_pairs={{0,14},{1,15},{2,12},{3,13},{4,10},{5,11},{6,8},{7,9},{8,6},{9,7},... | collective-permute-start | bytes 393224 | tf_op jit(solution)/shard_map/ppermute | solution.py:355
  46.4 23.3 %collective-permute-start.27 = (bf16[6,512,512]{2,1,0:T(8,128)(2,1)S(1)}, bf16[6,512,512]{2,1,0:T(8,128)(2,1)S(1)}, u32[]{:S(2)}, u32[]{:S(2)}) collective-permute-start(bf16[6,512,512]{2,1,0:T(8,128)(2,1)S(1)} %get-tuple-element.100), channel_id=1, source_target_pairs={{0,1},{1,0},{2,3},{3,2},{4,5},{5,4},{6,7},{7,6},{8,9},{9,8},{10,11... | collective-permute-start | bytes 9437192 | tf_op jit(solution)/shard_map/ppermute | solution.py:355
  47.0 19.2 %collective-permute-start.26 = (bf16[2,512,512]{2,1,0:T(8,128)(2,1)S(1)}, bf16[2,512,512]{2,1,0:T(8,128)(2,1)S(1)}, u32[]{:S(2)}, u32[]{:S(2)}) collective-permute-start(bf16[2,512,512]{2,1,0:T(8,128)(2,1)S(1)} %get-tuple-element.97), channel_id=1, source_target_pairs={{0,1},{1,0},{2,3},{3,2},{4,5},{5,4},{6,7},{7,6},{8,9},{9,8},{10,11... | collective-permute-start | bytes 3145736 | tf_op jit(solution)/shard_map/ppermute | solution.py:355
  47.1 9.5 %collective-permute-start.3 = (bf16[2,256,128]{2,1,0:T(8,128)(2,1)S(1)}, bf16[2,256,128]{2,1,0:T(8,128)(2,1)S(1)}, u32[]{:S(2)}, u32[]{:S(2)}) collective-permute-start(bf16[2,256,128]{2,1,0:T(8,128)(2,1)S(1)} %get-tuple-element.68), channel_id=1, source_target_pairs={{0,2},{1,3},{2,0},{3,1},{4,6},{5,7},{6,4},{7,5},{8,10},{9,11},{10,... | collective-permute-start | bytes 393224 | tf_op jit(solution)/shard_map/ppermute | solution.py:355
  48.4 9.0 %collective-permute-start.4 = (bf16[2,256,128]{2,1,0:T(8,128)(2,1)S(1)}, bf16[2,256,128]{2,1,0:T(8,128)(2,1)S(1)}, u32[]{:S(2)}, u32[]{:S(2)}) collective-permute-start(bf16[2,256,128]{2,1,0:T(8,128)(2,1)S(1)} %get-tuple-element.69), channel_id=1, source_target_pairs={{0,4},{1,5},{2,6},{3,7},{4,0},{5,1},{6,2},{7,3},{8,12},{9,13},{10,... | collective-permute-start | bytes 393224 | tf_op jit(solution)/shard_map/ppermute | solution.py:355
  53.3 7.0 %collective-permute-start.5 = (bf16[2,256,128]{2,1,0:T(8,128)(2,1)S(1)}, bf16[2,256,128]{2,1,0:T(8,128)(2,1)S(1)}, u32[]{:S(2)}, u32[]{:S(2)}) collective-permute-start(bf16[2,256,128]{2,1,0:T(8,128)(2,1)S(1)} %get-tuple-element.70), channel_id=1, source_target_pairs={{0,6},{1,7},{2,4},{3,5},{4,2},{5,3},{6,0},{7,1},{8,14},{9,15},{10,... | collective-permute-start | bytes 393224 | tf_op jit(solution)/shard_map/ppermute | solution.py:355
  67.6 5.6 %collective-permute-start.28 = (bf16[128,512]{1,0:T(8,128)(2,1)S(1)}, bf16[128,512]{1,0:T(8,128)(2,1)S(1)}, u32[]{:S(2)}, u32[]{:S(2)}) collective-permute-start(bf16[128,512]{1,0:T(8,128)(2,1)S(1)} %get-tuple-element.102), channel_id=1, source_target_pairs={{0,4},{1,5},{4,8},{5,9},{8,12},{9,13},{12,14},{13,15},{14,10},{15,... | collective-permute-start | bytes 393224 | tf_op jit(solution)/shard_map/ppermute | solution.py:352
  69.4 6.1 %collective-permute-start.32 = (bf16[128,512]{1,0:T(8,128)(2,1)S(1)}, bf16[128,512]{1,0:T(8,128)(2,1)S(1)}, u32[]{:S(2)}, u32[]{:S(2)}) collective-permute-start(bf16[128,512]{1,0:T(8,128)(2,1)S(1)} %get-tuple-element.106), channel_id=1, source_target_pairs={{0,2},{1,3},{4,0},{5,1},{8,4},{9,5},{12,8},{13,9},{14,12},{15,13},... | collective-permute-start | bytes 393224 | tf_op jit(solution)/shard_map/ppermute | solution.py:352
  (12 other events, 47.8 us)

commit v4 on v3

--- a/solution.py
+++ b/solution.py
@@ -124,12 +124,31 @@
     )(in_hbm(w_out))
 
 
+def fetch_kernel(start, size, source, target, sem):
+    copy = pltpu.make_async_copy(source.at[pl.ds(start, size), :], target, sem)
+    copy.start()
+    copy.wait()
+
+
+def fetch(value, start, size):
+    return pl.pallas_call(
+        functools.partial(fetch_kernel, start, size),
+        out_shape=pltpu.VMEM((size, value.shape[1]), jnp.bfloat16),
+        in_specs=anywhere(1),
+        out_specs=in_vmem(1)[0],
+        scratch_shapes=[pltpu.SemaphoreType.DMA],
+        compiler_params=params(8),
+        cost_estimate=cost(0, 4 * size * value.shape[1]),
+        name="fetch",
+    )(in_hbm(value))
+
+
 def project_kernel(offsets, chips, rows, *refs):
     count = len(offsets)
     blocks = refs[:count]
-    w_query, w_key, w_value, query_ref, own_ref, held, held_own, sems, own_sems = refs[count:]
+    w_first, w_second, w_key, w_value, query_ref, own_ref, held_own, own_sems = refs[count:]
     width = blocks[0].shape[1]
-    side = w_key.shape[0]
+    side, middle = w_key.shape[0], w_first.shape[0]
     _, core = here()
     own_copies = [
         pltpu.make_async_copy(w_key, held_own.at[pl.ds(0, side), :], own_sems.at[0]),
@@ -137,13 +156,6 @@
     ]
     for copy in own_copies:
         copy.start()
-    columns, copies = [], []
-    for number, (offset, other) in enumerate(offsets):
-        owner = 2 * neighbour_chip(offset, chips) + (1 - core if other else core)
-        columns.append(pl.ds(pl.multiple_of(owner * width, width), width))
-        copy = pltpu.make_async_copy(w_query.at[:, columns[number]], held.at[number], sems.at[number])
-        copy.start()
-        copies.append(copy)
     total = jnp.zeros((rows, 128), jnp.float32)
     for block in blocks:
         wide = block[:rows, :].astype(jnp.float32)
@@ -151,40 +163,42 @@
         for lane in range(0, width, 128):
             total += square[:, lane : lane + 128]
     inverse = lax.rsqrt(jnp.sum(total, axis=1, keepdims=True) / (width * count) + EPS)
-    query = jnp.zeros(query_ref.shape, jnp.float32)
+    first = jnp.zeros((rows, middle), jnp.float32)
+    second = jnp.zeros((rows, middle), jnp.float32)
     own = jnp.zeros(own_ref.shape, jnp.float32)
     for copy in own_copies:
         copy.wait()
-    for number, block in enumerate(blocks):
+    for block, (offset, other) in zip(blocks, offsets):
+        owner = 2 * neighbour_chip(offset, chips) + (1 - core if other else core)
+        columns = pl.ds(pl.multiple_of(owner * width, width), width)
         gain = block[rows : rows + PAD, :].astype(jnp.float32)[0:1, :]
         wide = block[:rows, :].astype(jnp.float32)
         normed = (wide * inverse * gain).astype(jnp.bfloat16)
-        own += lax.dot_general(normed, held_own[:, columns[number]], TRANS_B, preferred_element_type=jnp.float32)
-        copies[number].wait()
-        query += lax.dot_general(normed, held[number], TRANS_B, preferred_element_type=jnp.float32)
-    query_ref[...] = query.astype(jnp.bfloat16)
+        own += lax.dot_general(normed, held_own[:, columns], TRANS_B, preferred_element_type=jnp.float32)
+        first += lax.dot_general(normed, w_first[:, columns], TRANS_B, preferred_element_type=jnp.float32)
+        second += lax.dot_general(normed, w_second[:, columns], TRANS_B, preferred_element_type=jnp.float32)
+    query_ref[:, :middle] = first.astype(jnp.bfloat16)
+    query_ref[:, middle:] = second.astype(jnp.bfloat16)
     own_ref[...] = own.astype(jnp.bfloat16)
 
 
-def project(offsets, chips, blocks, w_query, w_key, w_value, rows):
-    count, width = len(blocks), blocks[0].shape[1]
+def project(offsets, chips, blocks, w_first, w_second, w_key, w_value, rows):
+    count = len(blocks)
     return pl.pallas_call(
         functools.partial(project_kernel, offsets, chips, rows),
         out_shape=(
-            jax.ShapeDtypeStruct((rows, w_query.shape[0]), jnp.bfloat16),
+            jax.ShapeDtypeStruct((rows, 2 * w_first.shape[0]), jnp.bfloat16),
             jax.ShapeDtypeStruct((rows, 2 * w_key.shape[0]), jnp.bfloat16),
         ),
-        in_specs=in_vmem(count) + anywhere(3),
+        in_specs=in_vmem(count + 2) + anywhere(2),
         out_specs=tuple(in_vmem(2)),
         scratch_shapes=[
-            pltpu.VMEM((count, w_query.shape[0], width), jnp.bfloat16),
             pltpu.VMEM((2 * w_key.shape[0], w_key.shape[1]), jnp.bfloat16),
-            pltpu.SemaphoreType.DMA((count,)),
             pltpu.SemaphoreType.DMA((2,)),
         ],
-        compiler_params=params(24),
+        compiler_params=params(12),
         name="project",
-    )(*blocks, in_hbm(w_query), in_hbm(w_key), in_hbm(w_value))
+    )(*blocks, w_first, w_second, in_hbm(w_key), in_hbm(w_value))
 
 
 def weigh(query, caches, scores, top, total, numerator):
@@ -366,20 +380,40 @@
     right = left = block
     reach = chips // 2
     take(block, 0)
+    middle = w_query.shape[0] // 2
+    weights = []
+    first = tuple([reach] + ([chips - reach + 1] if reach > 1 else []))
+    others = tuple(offset for offset in range(chips) if offset not in first)
     for step in range(1, reach + 1):
+        if step > 1:
+            right, weights = lax.optimization_barrier((right, weights))
+        if step <= 2:
+            w_query, right = lax.optimization_barrier((w_query, right))
+            weights = [*weights, fetch(w_query, (step - 1) * middle, middle)]
+        if step == min(3, reach):
+            w_out, right = lax.optimization_barrier((w_out, right))
+            sends = half(w_out, chips, (False, first), (False, others))
+        if step == reach and reach > 3:
+            sends, right = lax.optimization_barrier((sends, right))
         right = around(right, 1)
+        if step == 1:
+            prefix_cache, right = lax.optimization_barrier((prefix_cache, right))
+            pieces = cut(prefix_cache, chips)
         if step == min(2, reach):
-            prefix_cache, right = lax.optimization_barrier((prefix_cache, right))
+            pieces, right = lax.optimization_barrier((pieces, right))
         if step == max(reach - 1, 1):
-            pieces = cut(prefix_cache, chips)
             pieces, right = lax.optimization_barrier((pieces, right))
         take(right, -step)
         if step < reach:
             left = around(left, -1)
             take(left, step)
 
-    parts = {step: swap(pieces[step], 2 * step) for step in [*range(reach, chips), *range(1, reach)]}
-    query, own = project(tuple(offsets), chips, blocks, w_query, w_key, w_value, rows)
+    close = [swap(pieces[step], 2 * step) for step in range(1, reach)]
+    soon = (chips - reach) // 2
+    far_parts = [swap(pieces[step], 2 * step) for step in range(reach, reach + soon)]
+    pieces, close, far_parts = lax.optimization_barrier((pieces, close, far_parts))
+    far_parts += [swap(pieces[step], 2 * step) for step in range(reach + soon, chips)]
+    query, own = project(tuple(offsets), chips, blocks, *weights, w_key, w_value, rows)
 
     sharers = size // KV
     other_query = swap(query, 1)
@@ -390,22 +424,17 @@
         gathered = lax.all_gather(own, "seq", axis=0, axis_index_groups=groups)
         owns = [gathered[i] for i in range(sharers)]
 
-    first = tuple([reach] + ([chips - reach + 1] if reach > 1 else []))
-    others = tuple(offset for offset in range(chips) if offset not in first)
-    w_out, query = lax.optimization_barrier((w_out, query))
-    send_first, send_others, mine_first, mine_others = half(
-        w_out, chips, (False, first), (False, others), (True, first), (True, others)
-    )
+    send_first, send_others = sends
     other_first = swap(send_first, 1)
-    far_parts = [parts[step] for step in range(reach, chips)]
-    send_others, far_parts, owns, other_query = lax.optimization_barrier(
-        (send_others, far_parts, owns, other_query)
+    send_others, owns, other_query, far_parts[:soon] = lax.optimization_barrier(
+        (send_others, owns, other_query, far_parts[:soon])
     )
     other_others = swap(send_others, 1)
-
-    query, mine_first = lax.optimization_barrier((query, mine_first))
-    state = begin(far_parts, owns, query, other_query)
-    state, sums = finish([pieces[0]] + [parts[step] for step in range(1, reach)], state)
+    state = begin([pieces[0], *close, *far_parts[:soon]], owns, query, other_query)
+    w_out, state = lax.optimization_barrier((w_out, state))
+    mine_first, mine_others = half(w_out, chips, (True, first), (True, others))
+    state, mine_first, mine_others = lax.optimization_barrier((state, mine_first, mine_others))
+    state, sums = finish(far_parts[soon:], state)
 
     attention, *terms = merge(state, sums, swap(state, 1), swap(sums, 1), mine_first, other_first, rows)
     terms = dict(zip(first, terms))

time: 89.3 us -> 84.9 us (0.951)
  waiting for transfers between devices: 29.3 us -> 25.3 us
  Pallas kernels: 22.6 us -> 24.1 us
  local copies, waits for them, and re-layouts: 1.22 us -> 0.01 us
    ppermute x14, waiting for transfers between devices: 21.9 us -> 15.5 us  [around(): return lax.ppermute(value, 'seq', pairs)]
    pallas_call x0 -> x2, Pallas kernels: none -> 4.39 us  [fetch(): pl.pallas_call(functools.partial(fetch_kernel, start, size), out_shape=pl...]
    pallas_call x1, Pallas kernels: 9.28 us -> 4.93 us  [project(): pl.pallas_call(functools.partial(project_kernel, offsets, chips, rows), o...]
    ppermute x21, starting transfers between devices: 17.6 us -> 14.2 us  [swap(): return lax.ppermute(value, 'seq', [(i, i ^ bits) for i in range(size)])]
    ppermute x14, starting transfers between devices: 17.2 us -> 19.9 us  [around(): return lax.ppermute(value, 'seq', pairs)]
    ppermute x21, waiting for transfers between devices: 7.38 us -> 9.78 us  [swap(): return lax.ppermute(value, 'seq', [(i, i ^ bits) for i in range(size)])]
    unnamed x2, local copies, waits for them, and re-layouts: 1.22 us -> 0.01 us
    pallas_call x1, Pallas kernels: 2.46 us -> 3.65 us  [begin(): pl.pallas_call(functools.partial(begin_kernel, count, len(owns), heads),...]
  transfers between devices with their start and end apart: 35 -> 35, of which waited for: 16 -> 14; matrix products, arithmetic and copies ran while one was open for 0% -> 0% of each run, Pallas kernels for 24% -> 27%
where the time goes in v4:
time: 84.9 us; the launch traced here: 84.6 us
  starting transfers between devices  34.1 us (40%)
  waiting for transfers between devices  25.3 us (30%)
  Pallas kernels  24.1 us (28%)
  other arithmetic  0.86 us (1%)
    ppermute x14, starting transfers between devices, around(): return lax.ppermute(value, 'seq', pairs)  19.9 us
    ppermute x14, waiting for transfers between devices, around(): return lax.ppermute(value, 'seq', pairs)  15.5 us
    ppermute x21, starting transfers between devices, swap(): return lax.ppermute(value, 'seq', [(i, i ^ bits) for i in range(size)])  14.2 us
    ppermute x21, waiting for transfers between devices, swap(): return lax.ppermute(value, 'seq', [(i, i ^ bits) for i in range(size)])  9.78 us
    pallas_call x1, Pallas kernels, project(): pl.pallas_call(functools.partial(project_kernel, offsets, chips, rows), o...  4.93 us
    pallas_call x2, Pallas kernels, half(): pl.pallas_call(functools.partial(half_kernel, groups, chips, width), out_...  4.52 us
    pallas_call x2, Pallas kernels, fetch(): pl.pallas_call(functools.partial(fetch_kernel, start, size), out_shape=pl...  4.39 us
    pallas_call x1, Pallas kernels, begin(): pl.pallas_call(functools.partial(begin_kernel, count, len(owns), heads),...  3.65 us
  transfers between devices with their start and end apart: 35, of which 14 were waited for; matrix products, arithmetic and copies ran while one was open for 0% of the time, Pallas kernels for 27%

profile of v4, /device:TPU:0, one launch (start us, length us, event | category | flops | bytes accessed | tf_op | source)
XLA Modules:
  0.0 84.6 jit_solution(9340039853312376596)
XLA Ops:
  1.6 3.1 %collective-permute-start = (bf16[144,512]{1,0:T(8,128)(2,1)S(1)}, bf16[144,512]{1,0:T(8,128)(2,1)S(1)}, u32[]{:S(2)}, u32[]{:S(2)}) collective-permute-start(bf16[144,512]{1,0:T(8,128)(2,1)S(1)} %pack.1.refs_0_), channel_id=1, source_target_pairs={{0,4},{1,5},{4,8},{5,9},{8,12},{9,13},{12,14},{13,15},{14,10},{15,... | collective-permute-start | bytes 442376 | tf_op jit(solution)/shard_map/ppermute | solution.py:366
  4.7 2.2 %fetch.2.refs_16_ = bf16[256,8192]{1,0:T(8,128)(2,1)S(1)} custom-call(bf16[512,8192]{1,0:T(8,128)(2,1)} %source.1), custom_call_target="tpu_custom_call" | custom-call | bytes 8388608 | tf_op jit(solution)/shard_map/fetch/pallas_call | solution.py:134
  8.5 1.8 %collective-permute-start.1 = (bf16[144,512]{1,0:T(8,128)(2,1)S(1)}, bf16[144,512]{1,0:T(8,128)(2,1)S(1)}, u32[]{:S(2)}, u32[]{:S(2)}) collective-permute-start(bf16[144,512]{1,0:T(8,128)(2,1)S(1)} %collective-permute-done.refs_2_), channel_id=1, source_target_pairs={{0,4},{1,5},{4,8},{5,9},{8,12},{9,13},{12,14},{13,15},{14,10},{15,... | collective-permute-start | bytes 442376 | tf_op jit(solution)/shard_map/ppermute | solution.py:366
  10.6 2.2 %fetch.3.refs_17_ = bf16[256,8192]{1,0:T(8,128)(2,1)S(1)} custom-call(bf16[512,8192]{1,0:T(8,128)(2,1)} %source.1), custom_call_target="tpu_custom_call" | custom-call | bytes 8388608 | tf_op jit(solution)/shard_map/fetch/pallas_call | solution.py:134
  13.6 1.8 %collective-permute-start.2 = (bf16[144,512]{1,0:T(8,128)(2,1)S(1)}, bf16[144,512]{1,0:T(8,128)(2,1)S(1)}, u32[]{:S(2)}, u32[]{:S(2)}) collective-permute-start(bf16[144,512]{1,0:T(8,128)(2,1)S(1)} %collective-permute-done.1.refs_6_), channel_id=1, source_target_pairs={{0,4},{1,5},{4,8},{5,9},{8,12},{9,13},{12,14},{13,15},{14,10},{15,... | collective-permute-start | bytes 442376 | tf_op jit(solution)/shard_map/ppermute | solution.py:366
  15.9 2.2 %half.2 = (bf16[2,512,512]{2,1,0:T(8,128)(2,1)S(1)}, bf16[6,512,512]{2,1,0:T(8,128)(2,1)S(1)}) custom-call(bf16[512,8192]{1,0:T(8,128)(2,1)} %w_out.1), custom_call_target="tpu_custom_call" | custom-call | tf_op jit(solution)/shard_map/half/pallas_call | solution.py:116
  18.8 1.8 %collective-permute-start.20 = (bf16[144,512]{1,0:T(8,128)(2,1)S(1)}, bf16[144,512]{1,0:T(8,128)(2,1)S(1)}, u32[]{:S(2)}, u32[]{:S(2)}) collective-permute-start(bf16[144,512]{1,0:T(8,128)(2,1)S(1)} %collective-permute-done.2.refs_10_), channel_id=1, source_target_pairs={{0,4},{1,5},{4,8},{5,9},{8,12},{9,13},{12,14},{13,15},{14,10},{15,... | collective-permute-start | bytes 442376 | tf_op jit(solution)/shard_map/ppermute | solution.py:366
  21.1 3.4 %collective-permute-done.18.refs_12_ = bf16[144,512]{1,0:T(8,128)(2,1)S(1)} collective-permute-done((bf16[144,512]{1,0:T(8,128)(2,1)S(1)}, bf16[144,512]{1,0:T(8,128)(2,1)S(1)}, u32[]{:S(2)}, u32[]{:S(2)}) %collective-permute-start.18) | collective-permute-done | bytes 147488 | tf_op jit(solution)/shard_map/ppermute | solution.py:366
  28.6 2.6 %collective-permute-start.6 = (bf16[2,256,128]{2,1,0:T(8,128)(2,1)S(1)}, bf16[2,256,128]{2,1,0:T(8,128)(2,1)S(1)}, u32[]{:S(2)}, u32[]{:S(2)}) collective-permute-start(bf16[2,256,128]{2,1,0:T(8,128)(2,1)S(1)} %get-tuple-element.127), channel_id=1, source_target_pairs={{0,8},{1,9},{2,10},{3,11},{4,12},{5,13},{6,14},{7,15},{8,0},{9,1},... | collective-permute-start | bytes 393224 | tf_op jit(solution)/shard_map/ppermute | solution.py:369
  32.1 4.9 %project.1 = (bf16[128,512]{1,0:T(8,128)(2,1)S(1)}, bf16[128,128]{1,0:T(8,128)(2,1)S(1)}) custom-call(bf16[144,512]{1,0:T(8,128)(2,1)S(1)} %pack.1.refs_0_, bf16[144,512]{1,0:T(8,128)(2,1)S(1)} %collective-permute-done.10.refs_1_, bf16[144,512]{1,0:T(8,128)(2,1)S(1)} %collective-permute-done.refs_2_, bf16[144,512]{1,0:T(8,128)(2,1)S(1)} %collective-permute-done.11.refs_3_, ...), custom_call_target="tpu_custom_call" | custom-call | tf_op jit(solution)/shard_map/project/pallas_call | solution.py:187
  37.6 2.0 %collective-permute-done.5.refs_3_ = bf16[2,256,128]{2,1,0:T(8,128)(2,1)S(1)} collective-permute-done((bf16[2,256,128]{2,1,0:T(8,128)(2,1)S(1)}, bf16[2,256,128]{2,1,0:T(8,128)(2,1)S(1)}, u32[]{:S(2)}, u32[]{:S(2)}) %collective-permute-start.5) | collective-permute-done | bytes 131104 | tf_op jit(solution)/shard_map/ppermute | solution.py:369
  39.7 3.9 %collective-permute-done.7.refs_5_ = bf16[2,256,128]{2,1,0:T(8,128)(2,1)S(1)} collective-permute-done((bf16[2,256,128]{2,1,0:T(8,128)(2,1)S(1)}, bf16[2,256,128]{2,1,0:T(8,128)(2,1)S(1)}, u32[]{:S(2)}, u32[]{:S(2)}) %collective-permute-start.7) | collective-permute-done | bytes 131104 | tf_op jit(solution)/shard_map/ppermute | solution.py:369
  44.1 3.6 %collective-permute-start.8 = (bf16[2,256,128]{2,1,0:T(8,128)(2,1)S(1)}, bf16[2,256,128]{2,1,0:T(8,128)(2,1)S(1)}, u32[]{:S(2)}, u32[]{:S(2)}) collective-permute-start(bf16[2,256,128]{2,1,0:T(8,128)(2,1)S(1)} %get-tuple-element.131), channel_id=1, source_target_pairs={{0,12},{1,13},{2,14},{3,15},{4,8},{5,9},{6,10},{7,11},{8,4},{9,5},... | collective-permute-start | bytes 393224 | tf_op jit(solution)/shard_map/ppermute | solution.py:369
  48.4 3.6 %begin.1 = (bf16[1024,128]{1,0:T(8,128)(2,1)S(1)}, f32[1024,128]{1,0:T(8,128)S(1)}, f32[1024,128]{1,0:T(8,128)S(1)}, f32[1024,128]{1,0:T(8,128)S(1)}) custom-call(bf16[2,256,128]{2,1,0:T(8,128)(2,1)S(1)} %get-tuple-element.134.refs_0_, bf16[2,256,128]{2,1,0:T(8,128)(2,1)S(1)} %collective-permute-done.3.refs_1_, ...), custom_call_target="tpu_custom_call" | custom-call | flops 1 | bytes 1 | tf_op jit(solution)/shard_map/begin/pallas_call | solution.py:260
  52.0 2.3 %half.3 = (bf16[2,512,512]{2,1,0:T(8,128)(2,1)S(1)}, bf16[6,512,512]{2,1,0:T(8,128)(2,1)S(1)}) custom-call(bf16[512,8192]{1,0:T(8,128)(2,1)} %w_out.1), custom_call_target="tpu_custom_call" | custom-call | tf_op jit(solution)/shard_map/half/pallas_call | solution.py:116
  55.7 2.4 %finish.1 = (f32[1024,128]{1,0:T(8,128)S(1)}, f32[1024,128]{1,0:T(8,128)S(1)}) custom-call(bf16[2,256,128]{2,1,0:T(8,128)(2,1)S(1)} %collective-permute-done.8.refs_0_, bf16[2,256,128]{2,1,0:T(8,128)(2,1)S(1)} %collective-permute-done.9.refs_1_, bf16[1024,128]{1,0:T(8,128)(2,1)S(1)} %get-tuple-element.168.refs_2_, ...), custom_call_target="tpu_custom_call" | custom-call | tf_op jit(solution)/shard_map/finish/pallas_call | solution.py:288
  62.2 3.1 %collective-permute-start.28 = (bf16[128,512]{1,0:T(8,128)(2,1)S(1)}, bf16[128,512]{1,0:T(8,128)(2,1)S(1)}, u32[]{:S(2)}, u32[]{:S(2)}) collective-permute-start(bf16[128,512]{1,0:T(8,128)(2,1)S(1)} %get-tuple-element.180), channel_id=1, source_target_pairs={{0,4},{1,5},{4,8},{5,9},{8,12},{9,13},{12,14},{13,15},{14,10},{15,... | collective-permute-start | bytes 393224 | tf_op jit(solution)/shard_map/ppermute | solution.py:366
  66.3 2.1 %collective-permute-done.28 = bf16[128,512]{1,0:T(8,128)(2,1)S(1)} collective-permute-done((bf16[128,512]{1,0:T(8,128)(2,1)S(1)}, bf16[128,512]{1,0:T(8,128)(2,1)S(1)}, u32[]{:S(2)}, u32[]{:S(2)}) %collective-permute-start.28) | collective-permute-done | bytes 131104 | tf_op jit(solution)/shard_map/ppermute | solution.py:366
  68.4 2.5 %collective-permute-start.29 = (bf16[128,512]{1,0:T(8,128)(2,1)S(1)}, bf16[128,512]{1,0:T(8,128)(2,1)S(1)}, u32[]{:S(2)}, u32[]{:S(2)}) collective-permute-start(bf16[128,512]{1,0:T(8,128)(2,1)S(1)} %add_convert_fusion.5), channel_id=1, source_target_pairs={{0,4},{1,5},{4,8},{5,9},{8,12},{9,13},{12,14},{13,15},{14,10},{15,... | collective-permute-start | bytes 393224 | tf_op jit(solution)/shard_map/ppermute | solution.py:366
  71.0 2.4 %collective-permute-done.29 = bf16[128,512]{1,0:T(8,128)(2,1)S(1)} collective-permute-done((bf16[128,512]{1,0:T(8,128)(2,1)S(1)}, bf16[128,512]{1,0:T(8,128)(2,1)S(1)}, u32[]{:S(2)}, u32[]{:S(2)}) %collective-permute-start.29) | collective-permute-done | bytes 131104 | tf_op jit(solution)/shard_map/ppermute | solution.py:366
  73.5 2.5 %collective-permute-start.30 = (bf16[128,512]{1,0:T(8,128)(2,1)S(1)}, bf16[128,512]{1,0:T(8,128)(2,1)S(1)}, u32[]{:S(2)}, u32[]{:S(2)}) collective-permute-start(bf16[128,512]{1,0:T(8,128)(2,1)S(1)} %add_convert_fusion.4), channel_id=1, source_target_pairs={{0,4},{1,5},{4,8},{5,9},{8,12},{9,13},{12,14},{13,15},{14,10},{15,... | collective-permute-start | bytes 393224 | tf_op jit(solution)/shard_map/ppermute | solution.py:366
  76.1 2.7 %collective-permute-done.30 = bf16[128,512]{1,0:T(8,128)(2,1)S(1)} collective-permute-done((bf16[128,512]{1,0:T(8,128)(2,1)S(1)}, bf16[128,512]{1,0:T(8,128)(2,1)S(1)}, u32[]{:S(2)}, u32[]{:S(2)}) %collective-permute-start.30) | collective-permute-done | bytes 131104 | tf_op jit(solution)/shard_map/ppermute | solution.py:366
  78.8 2.5 %collective-permute-start.31 = (bf16[128,512]{1,0:T(8,128)(2,1)S(1)}, bf16[128,512]{1,0:T(8,128)(2,1)S(1)}, u32[]{:S(2)}, u32[]{:S(2)}) collective-permute-start(bf16[128,512]{1,0:T(8,128)(2,1)S(1)} %add_convert_fusion.3), channel_id=1, source_target_pairs={{0,4},{1,5},{4,8},{5,9},{8,12},{9,13},{12,14},{13,15},{14,10},{15,... | collective-permute-start | bytes 393224 | tf_op jit(solution)/shard_map/ppermute | solution.py:366
  81.4 2.5 %collective-permute-done.31 = bf16[128,512]{1,0:T(8,128)(2,1)S(1)} collective-permute-done((bf16[128,512]{1,0:T(8,128)(2,1)S(1)}, bf16[128,512]{1,0:T(8,128)(2,1)S(1)}, u32[]{:S(2)}, u32[]{:S(2)}) %collective-permute-start.31) | collective-permute-done | bytes 131104 | tf_op jit(solution)/shard_map/ppermute | solution.py:366
  (65 shorter events, 20.1 us)
Async XLA Ops:
  1.6 6.9 %collective-permute-start = (bf16[144,512]{1,0:T(8,128)(2,1)S(1)}, bf16[144,512]{1,0:T(8,128)(2,1)S(1)}, u32[]{:S(2)}, u32[]{:S(2)}) collective-permute-start(bf16[144,512]{1,0:T(8,128)(2,1)S(1)} %pack.1.refs_0_), channel_id=1, source_target_pairs={{0,4},{1,5},{4,8},{5,9},{8,12},{9,13},{12,14},{13,15},{14,10},{15,... | collective-permute-start | bytes 442376 | tf_op jit(solution)/shard_map/ppermute | solution.py:366
  4.7 8.1 %collective-permute-start.12 = (bf16[144,512]{1,0:T(8,128)(2,1)S(1)}, bf16[144,512]{1,0:T(8,128)(2,1)S(1)}, u32[]{:S(2)}, u32[]{:S(2)}) collective-permute-start(bf16[144,512]{1,0:T(8,128)(2,1)S(1)} %pack.1.refs_0_), channel_id=1, source_target_pairs={{0,2},{1,3},{4,0},{5,1},{8,4},{9,5},{12,8},{13,9},{14,12},{15,13},... | collective-permute-start | bytes 442376 | tf_op jit(solution)/shard_map/ppermute | solution.py:366
  12.8 5.4 %collective-permute-start.15 = (bf16[144,512]{1,0:T(8,128)(2,1)S(1)}, bf16[144,512]{1,0:T(8,128)(2,1)S(1)}, u32[]{:S(2)}, u32[]{:S(2)}) collective-permute-start(bf16[144,512]{1,0:T(8,128)(2,1)S(1)} %collective-permute-done.12.refs_4_), channel_id=1, source_target_pairs={{0,2},{1,3},{4,0},{5,1},{8,4},{9,5},{12,8},{13,9},{14,12},{15,13},... | collective-permute-start | bytes 442376 | tf_op jit(solution)/shard_map/ppermute | solution.py:366
  15.4 5.1 %collective-permute-start.11 = (bf16[144,512]{1,0:T(8,128)(2,1)S(1)}, bf16[144,512]{1,0:T(8,128)(2,1)S(1)}, u32[]{:S(2)}, u32[]{:S(2)}) collective-permute-start(bf16[144,512]{1,0:T(8,128)(2,1)S(1)} %collective-permute-done.refs_2_), channel_id=1, source_target_pairs={{0,1},{1,0},{2,3},{3,2},{4,5},{5,4},{6,7},{7,6},{8,9},{9,8},{10,11... | collective-permute-start | bytes 442376 | tf_op jit(solution)/shard_map/ppermute | solution.py:369
  15.9 8.6 %collective-permute-start.13 = (bf16[144,512]{1,0:T(8,128)(2,1)S(1)}, bf16[144,512]{1,0:T(8,128)(2,1)S(1)}, u32[]{:S(2)}, u32[]{:S(2)}) collective-permute-start(bf16[144,512]{1,0:T(8,128)(2,1)S(1)} %collective-permute-done.12.refs_4_), channel_id=1, source_target_pairs={{0,1},{1,0},{2,3},{3,2},{4,5},{5,4},{6,7},{7,6},{8,9},{9,8},{10,11... | collective-permute-start | bytes 442376 | tf_op jit(solution)/shard_map/ppermute | solution.py:369
  18.2 6.3 %collective-permute-start.18 = (bf16[144,512]{1,0:T(8,128)(2,1)S(1)}, bf16[144,512]{1,0:T(8,128)(2,1)S(1)}, u32[]{:S(2)}, u32[]{:S(2)}) collective-permute-start(bf16[144,512]{1,0:T(8,128)(2,1)S(1)} %collective-permute-done.15.refs_8_), channel_id=1, source_target_pairs={{0,2},{1,3},{4,0},{5,1},{8,4},{9,5},{12,8},{13,9},{14,12},{15,13},... | collective-permute-start | bytes 442376 | tf_op jit(solution)/shard_map/ppermute | solution.py:366
  18.8 6.3 %collective-permute-start.20 = (bf16[144,512]{1,0:T(8,128)(2,1)S(1)}, bf16[144,512]{1,0:T(8,128)(2,1)S(1)}, u32[]{:S(2)}, u32[]{:S(2)}) collective-permute-start(bf16[144,512]{1,0:T(8,128)(2,1)S(1)} %collective-permute-done.2.refs_10_), channel_id=1, source_target_pairs={{0,4},{1,5},{4,8},{5,9},{8,12},{9,13},{12,14},{13,15},{14,10},{15,... | collective-permute-start | bytes 442376 | tf_op jit(solution)/shard_map/ppermute | solution.py:366
  20.6 5.6 %collective-permute-start.14 = (bf16[144,512]{1,0:T(8,128)(2,1)S(1)}, bf16[144,512]{1,0:T(8,128)(2,1)S(1)}, u32[]{:S(2)}, u32[]{:S(2)}) collective-permute-start(bf16[144,512]{1,0:T(8,128)(2,1)S(1)} %collective-permute-done.1.refs_6_), channel_id=1, source_target_pairs={{0,1},{1,0},{2,3},{3,2},{4,5},{5,4},{6,7},{7,6},{8,9},{9,8},{10,11... | collective-permute-start | bytes 442376 | tf_op jit(solution)/shard_map/ppermute | solution.py:369
  25.0 6.2 %collective-permute-start.21 = (bf16[144,512]{1,0:T(8,128)(2,1)S(1)}, bf16[144,512]{1,0:T(8,128)(2,1)S(1)}, u32[]{:S(2)}, u32[]{:S(2)}) collective-permute-start(bf16[144,512]{1,0:T(8,128)(2,1)S(1)} %collective-permute-done.20.refs_14_), channel_id=1, source_target_pairs={{0,1},{1,0},{2,3},{3,2},{4,5},{5,4},{6,7},{7,6},{8,9},{9,8},{10,11... | collective-permute-start | bytes 442376 | tf_op jit(solution)/shard_map/ppermute | solution.py:369
  25.1 11.9 %collective-permute-start.3 = (bf16[2,256,128]{2,1,0:T(8,128)(2,1)S(1)}, bf16[2,256,128]{2,1,0:T(8,128)(2,1)S(1)}, u32[]{:S(2)}, u32[]{:S(2)}) collective-permute-start(bf16[2,256,128]{2,1,0:T(8,128)(2,1)S(1)} %get-tuple-element.124), channel_id=1, source_target_pairs={{0,2},{1,3},{2,0},{3,1},{4,6},{5,7},{6,4},{7,5},{8,10},{9,11},{10,... | collective-permute-start | bytes 393224 | tf_op jit(solution)/shard_map/ppermute | solution.py:369
  26.2 11.1 %collective-permute-start.4 = (bf16[2,256,128]{2,1,0:T(8,128)(2,1)S(1)}, bf16[2,256,128]{2,1,0:T(8,128)(2,1)S(1)}, u32[]{:S(2)}, u32[]{:S(2)}) collective-permute-start(bf16[2,256,128]{2,1,0:T(8,128)(2,1)S(1)} %get-tuple-element.125), channel_id=1, source_target_pairs={{0,4},{1,5},{2,6},{3,7},{4,0},{5,1},{6,2},{7,3},{8,12},{9,13},{10,... | collective-permute-start | bytes 393224 | tf_op jit(solution)/shard_map/ppermute | solution.py:369
  27.8 11.9 %collective-permute-start.5 = (bf16[2,256,128]{2,1,0:T(8,128)(2,1)S(1)}, bf16[2,256,128]{2,1,0:T(8,128)(2,1)S(1)}, u32[]{:S(2)}, u32[]{:S(2)}) collective-permute-start(bf16[2,256,128]{2,1,0:T(8,128)(2,1)S(1)} %get-tuple-element.126), channel_id=1, source_target_pairs={{0,6},{1,7},{2,4},{3,5},{4,2},{5,3},{6,0},{7,1},{8,14},{9,15},{10,... | collective-permute-start | bytes 393224 | tf_op jit(solution)/shard_map/ppermute | solution.py:369
  28.6 11.1 %collective-permute-start.6 = (bf16[2,256,128]{2,1,0:T(8,128)(2,1)S(1)}, bf16[2,256,128]{2,1,0:T(8,128)(2,1)S(1)}, u32[]{:S(2)}, u32[]{:S(2)}) collective-permute-start(bf16[2,256,128]{2,1,0:T(8,128)(2,1)S(1)} %get-tuple-element.127), channel_id=1, source_target_pairs={{0,8},{1,9},{2,10},{3,11},{4,12},{5,13},{6,14},{7,15},{8,0},{9,1},... | collective-permute-start | bytes 393224 | tf_op jit(solution)/shard_map/ppermute | solution.py:369
  31.2 12.4 %collective-permute-start.7 = (bf16[2,256,128]{2,1,0:T(8,128)(2,1)S(1)}, bf16[2,256,128]{2,1,0:T(8,128)(2,1)S(1)}, u32[]{:S(2)}, u32[]{:S(2)}) collective-permute-start(bf16[2,256,128]{2,1,0:T(8,128)(2,1)S(1)} %get-tuple-element.128), channel_id=1, source_target_pairs={{0,10},{1,11},{2,8},{3,9},{4,14},{5,15},{6,12},{7,13},{8,2},{9,3},... | collective-permute-start | bytes 393224 | tf_op jit(solution)/shard_map/ppermute | solution.py:369
  37.0 6.6 %collective-permute-start.23 = (bf16[128,512]{1,0:T(8,128)(2,1)S(1)}, bf16[128,512]{1,0:T(8,128)(2,1)S(1)}, u32[]{:S(2)}, u32[]{:S(2)}) collective-permute-start(bf16[128,512]{1,0:T(8,128)(2,1)S(1)} %get-tuple-element.149.refs_8_), channel_id=1, source_target_pairs={{0,1},{1,0},{2,3},{3,2},{4,5},{5,4},{6,7},{7,6},{8,9},{9,8},{10,11... | collective-permute-start | bytes 393224 | tf_op jit(solution)/shard_map/ppermute | solution.py:369
  37.3 6.3 %collective-permute-start.22 = (bf16[128,128]{1,0:T(8,128)(2,1)S(1)}, bf16[128,128]{1,0:T(8,128)(2,1)S(1)}, u32[]{:S(2)}, u32[]{:S(2)}) collective-permute-start(bf16[128,128]{1,0:T(8,128)(2,1)S(1)} %get-tuple-element.154.refs_6_), channel_id=1, source_target_pairs={{0,1},{1,0},{2,3},{3,2},{4,5},{5,4},{6,7},{7,6},{8,9},{9,8},{10,11... | collective-permute-start | bytes 98312 | tf_op jit(solution)/shard_map/ppermute | solution.py:369
  43.6 21.7 %collective-permute-start.27 = (bf16[6,512,512]{2,1,0:T(8,128)(2,1)S(1)}, bf16[6,512,512]{2,1,0:T(8,128)(2,1)S(1)}, u32[]{:S(2)}, u32[]{:S(2)}) collective-permute-start(bf16[6,512,512]{2,1,0:T(8,128)(2,1)S(1)} %get-tuple-element.178), channel_id=1, source_target_pairs={{0,1},{1,0},{2,3},{3,2},{4,5},{5,4},{6,7},{7,6},{8,9},{9,8},{10,11... | collective-permute-start | bytes 9437192 | tf_op jit(solution)/shard_map/ppermute | solution.py:369
  43.6 17.2 %collective-permute-start.26 = (bf16[2,512,512]{2,1,0:T(8,128)(2,1)S(1)}, bf16[2,512,512]{2,1,0:T(8,128)(2,1)S(1)}, u32[]{:S(2)}, u32[]{:S(2)}) collective-permute-start(bf16[2,512,512]{2,1,0:T(8,128)(2,1)S(1)} %get-tuple-element.175), channel_id=1, source_target_pairs={{0,1},{1,0},{2,3},{3,2},{4,5},{5,4},{6,7},{7,6},{8,9},{9,8},{10,11... | collective-permute-start | bytes 3145736 | tf_op jit(solution)/shard_map/ppermute | solution.py:369
  44.1 10.2 %collective-permute-start.8 = (bf16[2,256,128]{2,1,0:T(8,128)(2,1)S(1)}, bf16[2,256,128]{2,1,0:T(8,128)(2,1)S(1)}, u32[]{:S(2)}, u32[]{:S(2)}) collective-permute-start(bf16[2,256,128]{2,1,0:T(8,128)(2,1)S(1)} %get-tuple-element.131), channel_id=1, source_target_pairs={{0,12},{1,13},{2,14},{3,15},{4,8},{5,9},{6,10},{7,11},{8,4},{9,5},... | collective-permute-start | bytes 393224 | tf_op jit(solution)/shard_map/ppermute | solution.py:369
  47.7 8.0 %collective-permute-start.9 = (bf16[2,256,128]{2,1,0:T(8,128)(2,1)S(1)}, bf16[2,256,128]{2,1,0:T(8,128)(2,1)S(1)}, u32[]{:S(2)}, u32[]{:S(2)}) collective-permute-start(bf16[2,256,128]{2,1,0:T(8,128)(2,1)S(1)} %get-tuple-element.132), channel_id=1, source_target_pairs={{0,14},{1,15},{2,12},{3,13},{4,10},{5,11},{6,8},{7,9},{8,6},{9,7},... | collective-permute-start | bytes 393224 | tf_op jit(solution)/shard_map/ppermute | solution.py:369
  62.2 6.2 %collective-permute-start.28 = (bf16[128,512]{1,0:T(8,128)(2,1)S(1)}, bf16[128,512]{1,0:T(8,128)(2,1)S(1)}, u32[]{:S(2)}, u32[]{:S(2)}) collective-permute-start(bf16[128,512]{1,0:T(8,128)(2,1)S(1)} %get-tuple-element.180), channel_id=1, source_target_pairs={{0,4},{1,5},{4,8},{5,9},{8,12},{9,13},{12,14},{13,15},{14,10},{15,... | collective-permute-start | bytes 393224 | tf_op jit(solution)/shard_map/ppermute | solution.py:366
  65.3 5.6 %collective-permute-start.32 = (bf16[128,512]{1,0:T(8,128)(2,1)S(1)}, bf16[128,512]{1,0:T(8,128)(2,1)S(1)}, u32[]{:S(2)}, u32[]{:S(2)}) collective-permute-start(bf16[128,512]{1,0:T(8,128)(2,1)S(1)} %get-tuple-element.184), channel_id=1, source_target_pairs={{0,2},{1,3},{4,0},{5,1},{8,4},{9,5},{12,8},{13,9},{14,12},{15,13},... | collective-permute-start | bytes 393224 | tf_op jit(solution)/shard_map/ppermute | solution.py:366
  73.5 5.3 %collective-permute-start.30 = (bf16[128,512]{1,0:T(8,128)(2,1)S(1)}, bf16[128,512]{1,0:T(8,128)(2,1)S(1)}, u32[]{:S(2)}, u32[]{:S(2)}) collective-permute-start(bf16[128,512]{1,0:T(8,128)(2,1)S(1)} %add_convert_fusion.4), channel_id=1, source_target_pairs={{0,4},{1,5},{4,8},{5,9},{8,12},{9,13},{12,14},{13,15},{14,10},{15,... | collective-permute-start | bytes 393224 | tf_op jit(solution)/shard_map/ppermute | solution.py:366
  76.0 5.3 %collective-permute-start.34 = (bf16[128,512]{1,0:T(8,128)(2,1)S(1)}, bf16[128,512]{1,0:T(8,128)(2,1)S(1)}, u32[]{:S(2)}, u32[]{:S(2)}) collective-permute-start(bf16[128,512]{1,0:T(8,128)(2,1)S(1)} %add_convert_fusion.1), channel_id=1, source_target_pairs={{0,2},{1,3},{4,0},{5,1},{8,4},{9,5},{12,8},{13,9},{14,12},{15,13},... | collective-permute-start | bytes 393224 | tf_op jit(solution)/shard_map/ppermute | solution.py:366
  (12 other events, 55.8 us)

commit v5 on v4

--- a/solution.py
+++ b/solution.py
@@ -390,11 +390,6 @@
         if step <= 2:
             w_query, right = lax.optimization_barrier((w_query, right))
             weights = [*weights, fetch(w_query, (step - 1) * middle, middle)]
-        if step == min(3, reach):
-            w_out, right = lax.optimization_barrier((w_out, right))
-            sends = half(w_out, chips, (False, first), (False, others))
-        if step == reach and reach > 3:
-            sends, right = lax.optimization_barrier((sends, right))
         right = around(right, 1)
         if step == 1:
             prefix_cache, right = lax.optimization_barrier((prefix_cache, right))
@@ -408,12 +403,17 @@
             left = around(left, -1)
             take(left, step)
 
-    close = [swap(pieces[step], 2 * step) for step in range(1, reach)]
     soon = (chips - reach) // 2
-    far_parts = [swap(pieces[step], 2 * step) for step in range(reach, reach + soon)]
-    pieces, close, far_parts = lax.optimization_barrier((pieces, close, far_parts))
-    far_parts += [swap(pieces[step], 2 * step) for step in range(reach + soon, chips)]
+    sooner = [*range(reach, reach + soon), *range(1, reach)]
+    later = [step for step in range(1, chips) if step not in sooner]
+    close = [swap(pieces[step], 2 * step) for step in sooner]
+    pieces, close = lax.optimization_barrier((pieces, close))
+    far_parts = [swap(pieces[step], 2 * step) for step in later]
     query, own = project(tuple(offsets), chips, blocks, *weights, w_key, w_value, rows)
+
+    w_out, query = lax.optimization_barrier((w_out, query))
+    sends = half(w_out, chips, (False, first), (False, others))
+    query, own, sends = lax.optimization_barrier((query, own, sends))
 
     sharers = size // KV
     other_query = swap(query, 1)
@@ -426,15 +426,13 @@
 
     send_first, send_others = sends
     other_first = swap(send_first, 1)
-    send_others, owns, other_query, far_parts[:soon] = lax.optimization_barrier(
-        (send_others, owns, other_query, far_parts[:soon])
-    )
+    send_others, owns, other_query, close = lax.optimization_barrier((send_others, owns, other_query, close))
     other_others = swap(send_others, 1)
-    state = begin([pieces[0], *close, *far_parts[:soon]], owns, query, other_query)
+    state = begin([pieces[0], *close], owns, query, other_query)
     w_out, state = lax.optimization_barrier((w_out, state))
     mine_first, mine_others = half(w_out, chips, (True, first), (True, others))
     state, mine_first, mine_others = lax.optimization_barrier((state, mine_first, mine_others))
-    state, sums = finish(far_parts[soon:], state)
+    state, sums = finish(far_parts, state)
 
     attention, *terms = merge(state, sums, swap(state, 1), swap(sums, 1), mine_first, other_first, rows)
     terms = dict(zip(first, terms))

time: 84.9 us -> 83.9 us (0.988)
    ppermute x21, waiting for transfers between devices: 9.78 us -> 7.28 us  [swap(): return lax.ppermute(value, 'seq', [(i, i ^ bits) for i in range(size)])]
    ppermute x14, waiting for transfers between devices: 15.5 us -> 17.2 us  [around(): return lax.ppermute(value, 'seq', pairs)]
  transfers between devices with their start and end apart: 35 -> 35, of which waited for: 14 -> 15; matrix products, arithmetic and copies ran while one was open for 0% -> 0% of each run, Pallas kernels for 27% -> 27%
where the time goes in v5:
time: 83.9 us; the launch traced here: 83.6 us
  starting transfers between devices  34 us (41%)
  waiting for transfers between devices  24.5 us (29%)
  Pallas kernels  24.1 us (29%)
  other arithmetic  0.86 us (1%)
    ppermute x14, starting transfers between devices, around(): return lax.ppermute(value, 'seq', pairs)  19.5 us
    ppermute x14, waiting for transfers between devices, around(): return lax.ppermute(value, 'seq', pairs)  17.2 us
    ppermute x21, starting transfers between devices, swap(): return lax.ppermute(value, 'seq', [(i, i ^ bits) for i in range(size)])  14.4 us
    ppermute x21, waiting for transfers between devices, swap(): return lax.ppermute(value, 'seq', [(i, i ^ bits) for i in range(size)])  7.28 us
    pallas_call x1, Pallas kernels, project(): pl.pallas_call(functools.partial(project_kernel, offsets, chips, rows), o...  4.93 us
    pallas_call x2, Pallas kernels, half(): pl.pallas_call(functools.partial(half_kernel, groups, chips, width), out_...  4.55 us
    pallas_call x2, Pallas kernels, fetch(): pl.pallas_call(functools.partial(fetch_kernel, start, size), out_shape=pl...  4.39 us
    pallas_call x1, Pallas kernels, begin(): pl.pallas_call(functools.partial(begin_kernel, count, len(owns), heads),...  3.65 us
  transfers between devices with their start and end apart: 35, of which 15 were waited for; matrix products, arithmetic and copies ran while one was open for 0% of the time, Pallas kernels for 27%

profile of v5, /device:TPU:0, one launch (start us, length us, event | category | flops | bytes accessed | tf_op | source)
XLA Modules:
  0.0 83.6 jit_solution(17404516219728397187)
XLA Ops:
  1.6 3.1 %collective-permute-start = (bf16[144,512]{1,0:T(8,128)(2,1)S(1)}, bf16[144,512]{1,0:T(8,128)(2,1)S(1)}, u32[]{:S(2)}, u32[]{:S(2)}) collective-permute-start(bf16[144,512]{1,0:T(8,128)(2,1)S(1)} %pack.1.refs_0_), channel_id=1, source_target_pairs={{0,4},{1,5},{4,8},{5,9},{8,12},{9,13},{12,14},{13,15},{14,10},{15,... | collective-permute-start | bytes 442376 | tf_op jit(solution)/shard_map/ppermute | solution.py:366
  4.7 2.2 %fetch.2.refs_16_ = bf16[256,8192]{1,0:T(8,128)(2,1)S(1)} custom-call(bf16[512,8192]{1,0:T(8,128)(2,1)} %source.1), custom_call_target="tpu_custom_call" | custom-call | bytes 8388608 | tf_op jit(solution)/shard_map/fetch/pallas_call | solution.py:134
  8.5 1.8 %collective-permute-start.1 = (bf16[144,512]{1,0:T(8,128)(2,1)S(1)}, bf16[144,512]{1,0:T(8,128)(2,1)S(1)}, u32[]{:S(2)}, u32[]{:S(2)}) collective-permute-start(bf16[144,512]{1,0:T(8,128)(2,1)S(1)} %collective-permute-done.refs_2_), channel_id=1, source_target_pairs={{0,4},{1,5},{4,8},{5,9},{8,12},{9,13},{12,14},{13,15},{14,10},{15,... | collective-permute-start | bytes 442376 | tf_op jit(solution)/shard_map/ppermute | solution.py:366
  10.6 2.2 %fetch.3.refs_17_ = bf16[256,8192]{1,0:T(8,128)(2,1)S(1)} custom-call(bf16[512,8192]{1,0:T(8,128)(2,1)} %source.1), custom_call_target="tpu_custom_call" | custom-call | bytes 8388608 | tf_op jit(solution)/shard_map/fetch/pallas_call | solution.py:134
  13.6 1.8 %collective-permute-start.2 = (bf16[144,512]{1,0:T(8,128)(2,1)S(1)}, bf16[144,512]{1,0:T(8,128)(2,1)S(1)}, u32[]{:S(2)}, u32[]{:S(2)}) collective-permute-start(bf16[144,512]{1,0:T(8,128)(2,1)S(1)} %collective-permute-done.1.refs_6_), channel_id=1, source_target_pairs={{0,4},{1,5},{4,8},{5,9},{8,12},{9,13},{12,14},{13,15},{14,10},{15,... | collective-permute-start | bytes 442376 | tf_op jit(solution)/shard_map/ppermute | solution.py:366
  15.9 2.0 %collective-permute-done.15.refs_8_ = bf16[144,512]{1,0:T(8,128)(2,1)S(1)} collective-permute-done((bf16[144,512]{1,0:T(8,128)(2,1)S(1)}, bf16[144,512]{1,0:T(8,128)(2,1)S(1)}, u32[]{:S(2)}, u32[]{:S(2)}) %collective-permute-start.15) | collective-permute-done | bytes 147488 | tf_op jit(solution)/shard_map/ppermute | solution.py:366
  18.8 1.8 %collective-permute-start.20 = (bf16[144,512]{1,0:T(8,128)(2,1)S(1)}, bf16[144,512]{1,0:T(8,128)(2,1)S(1)}, u32[]{:S(2)}, u32[]{:S(2)}) collective-permute-start(bf16[144,512]{1,0:T(8,128)(2,1)S(1)} %collective-permute-done.2.refs_10_), channel_id=1, source_target_pairs={{0,4},{1,5},{4,8},{5,9},{8,12},{9,13},{12,14},{13,15},{14,10},{15,... | collective-permute-start | bytes 442376 | tf_op jit(solution)/shard_map/ppermute | solution.py:366
  21.2 2.0 %collective-permute-done.18.refs_12_ = bf16[144,512]{1,0:T(8,128)(2,1)S(1)} collective-permute-done((bf16[144,512]{1,0:T(8,128)(2,1)S(1)}, bf16[144,512]{1,0:T(8,128)(2,1)S(1)}, u32[]{:S(2)}, u32[]{:S(2)}) %collective-permute-start.18) | collective-permute-done | bytes 147488 | tf_op jit(solution)/shard_map/ppermute | solution.py:366
  23.9 2.8 %collective-permute-start.3 = (bf16[2,256,128]{2,1,0:T(8,128)(2,1)S(1)}, bf16[2,256,128]{2,1,0:T(8,128)(2,1)S(1)}, u32[]{:S(2)}, u32[]{:S(2)}) collective-permute-start(bf16[2,256,128]{2,1,0:T(8,128)(2,1)S(1)} %get-tuple-element.130), channel_id=1, source_target_pairs={{0,8},{1,9},{2,10},{3,11},{4,12},{5,13},{6,14},{7,15},{8,0},{9,1},... | collective-permute-start | bytes 393224 | tf_op jit(solution)/shard_map/ppermute | solution.py:369
  31.5 4.9 %project.1 = (bf16[128,512]{1,0:T(8,128)(2,1)S(1)}, bf16[128,128]{1,0:T(8,128)(2,1)S(1)}) custom-call(bf16[144,512]{1,0:T(8,128)(2,1)S(1)} %pack.1.refs_0_, bf16[144,512]{1,0:T(8,128)(2,1)S(1)} %collective-permute-done.10.refs_1_, bf16[144,512]{1,0:T(8,128)(2,1)S(1)} %collective-permute-done.refs_2_, bf16[144,512]{1,0:T(8,128)(2,1)S(1)} %collective-permute-done.11.refs_3_, ...), custom_call_target="tpu_custom_call" | custom-call | tf_op jit(solution)/shard_map/project/pallas_call | solution.py:187
  36.5 2.3 %half.2 = (bf16[2,512,512]{2,1,0:T(8,128)(2,1)S(1)}, bf16[6,512,512]{2,1,0:T(8,128)(2,1)S(1)}) custom-call(bf16[512,8192]{1,0:T(8,128)(2,1)} %w_out.1), custom_call_target="tpu_custom_call" | custom-call | tf_op jit(solution)/shard_map/half/pallas_call | solution.py:116
  42.4 4.6 %collective-permute-start.8 = (bf16[2,256,128]{2,1,0:T(8,128)(2,1)S(1)}, bf16[2,256,128]{2,1,0:T(8,128)(2,1)S(1)}, u32[]{:S(2)}, u32[]{:S(2)}) collective-permute-start(bf16[2,256,128]{2,1,0:T(8,128)(2,1)S(1)} %get-tuple-element.134), channel_id=1, source_target_pairs={{0,12},{1,13},{2,14},{3,15},{4,8},{5,9},{6,10},{7,11},{8,4},{9,5},... | collective-permute-start | bytes 393224 | tf_op jit(solution)/shard_map/ppermute | solution.py:369
  47.0 3.6 %begin.1 = (bf16[1024,128]{1,0:T(8,128)(2,1)S(1)}, f32[1024,128]{1,0:T(8,128)S(1)}, f32[1024,128]{1,0:T(8,128)S(1)}, f32[1024,128]{1,0:T(8,128)S(1)}) custom-call(bf16[2,256,128]{2,1,0:T(8,128)(2,1)S(1)} %get-tuple-element.144.refs_0_, bf16[2,256,128]{2,1,0:T(8,128)(2,1)S(1)} %collective-permute-done.3.refs_1_, ...), custom_call_target="tpu_custom_call" | custom-call | flops 1 | bytes 1 | tf_op jit(solution)/shard_map/begin/pallas_call | solution.py:260
  50.7 2.3 %half.3 = (bf16[2,512,512]{2,1,0:T(8,128)(2,1)S(1)}, bf16[6,512,512]{2,1,0:T(8,128)(2,1)S(1)}) custom-call(bf16[512,8192]{1,0:T(8,128)(2,1)} %w_out.1), custom_call_target="tpu_custom_call" | custom-call | tf_op jit(solution)/shard_map/half/pallas_call | solution.py:116
  53.0 2.0 %collective-permute-done.9.refs_1_ = bf16[2,256,128]{2,1,0:T(8,128)(2,1)S(1)} collective-permute-done((bf16[2,256,128]{2,1,0:T(8,128)(2,1)S(1)}, bf16[2,256,128]{2,1,0:T(8,128)(2,1)S(1)}, u32[]{:S(2)}, u32[]{:S(2)}) %collective-permute-start.9) | collective-permute-done | bytes 131104 | tf_op jit(solution)/shard_map/ppermute | solution.py:369
  55.0 2.4 %finish.1 = (f32[1024,128]{1,0:T(8,128)S(1)}, f32[1024,128]{1,0:T(8,128)S(1)}) custom-call(bf16[2,256,128]{2,1,0:T(8,128)(2,1)S(1)} %collective-permute-done.8.refs_0_, bf16[2,256,128]{2,1,0:T(8,128)(2,1)S(1)} %collective-permute-done.9.refs_1_, bf16[1024,128]{1,0:T(8,128)(2,1)S(1)} %get-tuple-element.176.refs_2_, ...), custom_call_target="tpu_custom_call" | custom-call | tf_op jit(solution)/shard_map/finish/pallas_call | solution.py:288
  61.5 2.9 %collective-permute-start.28 = (bf16[128,512]{1,0:T(8,128)(2,1)S(1)}, bf16[128,512]{1,0:T(8,128)(2,1)S(1)}, u32[]{:S(2)}, u32[]{:S(2)}) collective-permute-start(bf16[128,512]{1,0:T(8,128)(2,1)S(1)} %get-tuple-element.188), channel_id=1, source_target_pairs={{0,4},{1,5},{4,8},{5,9},{8,12},{9,13},{12,14},{13,15},{14,10},{15,... | collective-permute-start | bytes 393224 | tf_op jit(solution)/shard_map/ppermute | solution.py:366
  65.3 2.1 %collective-permute-done.28 = bf16[128,512]{1,0:T(8,128)(2,1)S(1)} collective-permute-done((bf16[128,512]{1,0:T(8,128)(2,1)S(1)}, bf16[128,512]{1,0:T(8,128)(2,1)S(1)}, u32[]{:S(2)}, u32[]{:S(2)}) %collective-permute-start.28) | collective-permute-done | bytes 131104 | tf_op jit(solution)/shard_map/ppermute | solution.py:366
  67.4 2.5 %collective-permute-start.29 = (bf16[128,512]{1,0:T(8,128)(2,1)S(1)}, bf16[128,512]{1,0:T(8,128)(2,1)S(1)}, u32[]{:S(2)}, u32[]{:S(2)}) collective-permute-start(bf16[128,512]{1,0:T(8,128)(2,1)S(1)} %add_convert_fusion.5), channel_id=1, source_target_pairs={{0,4},{1,5},{4,8},{5,9},{8,12},{9,13},{12,14},{13,15},{14,10},{15,... | collective-permute-start | bytes 393224 | tf_op jit(solution)/shard_map/ppermute | solution.py:366
  70.1 2.4 %collective-permute-done.29 = bf16[128,512]{1,0:T(8,128)(2,1)S(1)} collective-permute-done((bf16[128,512]{1,0:T(8,128)(2,1)S(1)}, bf16[128,512]{1,0:T(8,128)(2,1)S(1)}, u32[]{:S(2)}, u32[]{:S(2)}) %collective-permute-start.29) | collective-permute-done | bytes 131104 | tf_op jit(solution)/shard_map/ppermute | solution.py:366
  72.5 2.5 %collective-permute-start.30 = (bf16[128,512]{1,0:T(8,128)(2,1)S(1)}, bf16[128,512]{1,0:T(8,128)(2,1)S(1)}, u32[]{:S(2)}, u32[]{:S(2)}) collective-permute-start(bf16[128,512]{1,0:T(8,128)(2,1)S(1)} %add_convert_fusion.4), channel_id=1, source_target_pairs={{0,4},{1,5},{4,8},{5,9},{8,12},{9,13},{12,14},{13,15},{14,10},{15,... | collective-permute-start | bytes 393224 | tf_op jit(solution)/shard_map/ppermute | solution.py:366
  75.1 2.7 %collective-permute-done.30 = bf16[128,512]{1,0:T(8,128)(2,1)S(1)} collective-permute-done((bf16[128,512]{1,0:T(8,128)(2,1)S(1)}, bf16[128,512]{1,0:T(8,128)(2,1)S(1)}, u32[]{:S(2)}, u32[]{:S(2)}) %collective-permute-start.30) | collective-permute-done | bytes 131104 | tf_op jit(solution)/shard_map/ppermute | solution.py:366
  77.9 2.5 %collective-permute-start.31 = (bf16[128,512]{1,0:T(8,128)(2,1)S(1)}, bf16[128,512]{1,0:T(8,128)(2,1)S(1)}, u32[]{:S(2)}, u32[]{:S(2)}) collective-permute-start(bf16[128,512]{1,0:T(8,128)(2,1)S(1)} %add_convert_fusion.3), channel_id=1, source_target_pairs={{0,4},{1,5},{4,8},{5,9},{8,12},{9,13},{12,14},{13,15},{14,10},{15,... | collective-permute-start | bytes 393224 | tf_op jit(solution)/shard_map/ppermute | solution.py:366
  80.4 2.5 %collective-permute-done.31 = bf16[128,512]{1,0:T(8,128)(2,1)S(1)} collective-permute-done((bf16[128,512]{1,0:T(8,128)(2,1)S(1)}, bf16[128,512]{1,0:T(8,128)(2,1)S(1)}, u32[]{:S(2)}, u32[]{:S(2)}) %collective-permute-start.31) | collective-permute-done | bytes 131104 | tf_op jit(solution)/shard_map/ppermute | solution.py:366
  (65 shorter events, 21.5 us)
Async XLA Ops:
  1.6 6.9 %collective-permute-start = (bf16[144,512]{1,0:T(8,128)(2,1)S(1)}, bf16[144,512]{1,0:T(8,128)(2,1)S(1)}, u32[]{:S(2)}, u32[]{:S(2)}) collective-permute-start(bf16[144,512]{1,0:T(8,128)(2,1)S(1)} %pack.1.refs_0_), channel_id=1, source_target_pairs={{0,4},{1,5},{4,8},{5,9},{8,12},{9,13},{12,14},{13,15},{14,10},{15,... | collective-permute-start | bytes 442376 | tf_op jit(solution)/shard_map/ppermute | solution.py:366
  4.7 8.1 %collective-permute-start.12 = (bf16[144,512]{1,0:T(8,128)(2,1)S(1)}, bf16[144,512]{1,0:T(8,128)(2,1)S(1)}, u32[]{:S(2)}, u32[]{:S(2)}) collective-permute-start(bf16[144,512]{1,0:T(8,128)(2,1)S(1)} %pack.1.refs_0_), channel_id=1, source_target_pairs={{0,2},{1,3},{4,0},{5,1},{8,4},{9,5},{12,8},{13,9},{14,12},{15,13},... | collective-permute-start | bytes 442376 | tf_op jit(solution)/shard_map/ppermute | solution.py:366
  8.5 5.1 %collective-permute-start.1 = (bf16[144,512]{1,0:T(8,128)(2,1)S(1)}, bf16[144,512]{1,0:T(8,128)(2,1)S(1)}, u32[]{:S(2)}, u32[]{:S(2)}) collective-permute-start(bf16[144,512]{1,0:T(8,128)(2,1)S(1)} %collective-permute-done.refs_2_), channel_id=1, source_target_pairs={{0,4},{1,5},{4,8},{5,9},{8,12},{9,13},{12,14},{13,15},{14,10},{15,... | collective-permute-start | bytes 442376 | tf_op jit(solution)/shard_map/ppermute | solution.py:366
  12.8 5.2 %collective-permute-start.15 = (bf16[144,512]{1,0:T(8,128)(2,1)S(1)}, bf16[144,512]{1,0:T(8,128)(2,1)S(1)}, u32[]{:S(2)}, u32[]{:S(2)}) collective-permute-start(bf16[144,512]{1,0:T(8,128)(2,1)S(1)} %collective-permute-done.12.refs_4_), channel_id=1, source_target_pairs={{0,2},{1,3},{4,0},{5,1},{8,4},{9,5},{12,8},{13,9},{14,12},{15,13},... | collective-permute-start | bytes 442376 | tf_op jit(solution)/shard_map/ppermute | solution.py:366
  15.4 5.1 %collective-permute-start.10 = (bf16[144,512]{1,0:T(8,128)(2,1)S(1)}, bf16[144,512]{1,0:T(8,128)(2,1)S(1)}, u32[]{:S(2)}, u32[]{:S(2)}) collective-permute-start(bf16[144,512]{1,0:T(8,128)(2,1)S(1)} %pack.1.refs_0_), channel_id=1, source_target_pairs={{0,1},{1,0},{2,3},{3,2},{4,5},{5,4},{6,7},{7,6},{8,9},{9,8},{10,11... | collective-permute-start | bytes 442376 | tf_op jit(solution)/shard_map/ppermute | solution.py:369
  15.4 5.1 %collective-permute-start.11 = (bf16[144,512]{1,0:T(8,128)(2,1)S(1)}, bf16[144,512]{1,0:T(8,128)(2,1)S(1)}, u32[]{:S(2)}, u32[]{:S(2)}) collective-permute-start(bf16[144,512]{1,0:T(8,128)(2,1)S(1)} %collective-permute-done.refs_2_), channel_id=1, source_target_pairs={{0,1},{1,0},{2,3},{3,2},{4,5},{5,4},{6,7},{7,6},{8,9},{9,8},{10,11... | collective-permute-start | bytes 442376 | tf_op jit(solution)/shard_map/ppermute | solution.py:369
  15.9 5.2 %collective-permute-start.13 = (bf16[144,512]{1,0:T(8,128)(2,1)S(1)}, bf16[144,512]{1,0:T(8,128)(2,1)S(1)}, u32[]{:S(2)}, u32[]{:S(2)}) collective-permute-start(bf16[144,512]{1,0:T(8,128)(2,1)S(1)} %collective-permute-done.12.refs_4_), channel_id=1, source_target_pairs={{0,1},{1,0},{2,3},{3,2},{4,5},{5,4},{6,7},{7,6},{8,9},{9,8},{10,11... | collective-permute-start | bytes 442376 | tf_op jit(solution)/shard_map/ppermute | solution.py:369
  20.6 6.2 %collective-permute-start.16 = (bf16[144,512]{1,0:T(8,128)(2,1)S(1)}, bf16[144,512]{1,0:T(8,128)(2,1)S(1)}, u32[]{:S(2)}, u32[]{:S(2)}) collective-permute-start(bf16[144,512]{1,0:T(8,128)(2,1)S(1)} %collective-permute-done.15.refs_8_), channel_id=1, source_target_pairs={{0,1},{1,0},{2,3},{3,2},{4,5},{5,4},{6,7},{7,6},{8,9},{9,8},{10,11... | collective-permute-start | bytes 442376 | tf_op jit(solution)/shard_map/ppermute | solution.py:369
  21.1 6.9 %collective-permute-start.17 = (bf16[144,512]{1,0:T(8,128)(2,1)S(1)}, bf16[144,512]{1,0:T(8,128)(2,1)S(1)}, u32[]{:S(2)}, u32[]{:S(2)}) collective-permute-start(bf16[144,512]{1,0:T(8,128)(2,1)S(1)} %collective-permute-done.2.refs_10_), channel_id=1, source_target_pairs={{0,1},{1,0},{2,3},{3,2},{4,5},{5,4},{6,7},{7,6},{8,9},{9,8},{10,11... | collective-permute-start | bytes 442376 | tf_op jit(solution)/shard_map/ppermute | solution.py:369
  23.1 5.2 %collective-permute-start.19 = (bf16[144,512]{1,0:T(8,128)(2,1)S(1)}, bf16[144,512]{1,0:T(8,128)(2,1)S(1)}, u32[]{:S(2)}, u32[]{:S(2)}) collective-permute-start(bf16[144,512]{1,0:T(8,128)(2,1)S(1)} %collective-permute-done.18.refs_12_), channel_id=1, source_target_pairs={{0,1},{1,0},{2,3},{3,2},{4,5},{5,4},{6,7},{7,6},{8,9},{9,8},{10,11... | collective-permute-start | bytes 442376 | tf_op jit(solution)/shard_map/ppermute | solution.py:369
  23.9 6.2 %collective-permute-start.21 = (bf16[144,512]{1,0:T(8,128)(2,1)S(1)}, bf16[144,512]{1,0:T(8,128)(2,1)S(1)}, u32[]{:S(2)}, u32[]{:S(2)}) collective-permute-start(bf16[144,512]{1,0:T(8,128)(2,1)S(1)} %collective-permute-done.20.refs_14_), channel_id=1, source_target_pairs={{0,1},{1,0},{2,3},{3,2},{4,5},{5,4},{6,7},{7,6},{8,9},{9,8},{10,11... | collective-permute-start | bytes 442376 | tf_op jit(solution)/shard_map/ppermute | solution.py:369
  23.9 14.8 %collective-permute-start.3 = (bf16[2,256,128]{2,1,0:T(8,128)(2,1)S(1)}, bf16[2,256,128]{2,1,0:T(8,128)(2,1)S(1)}, u32[]{:S(2)}, u32[]{:S(2)}) collective-permute-start(bf16[2,256,128]{2,1,0:T(8,128)(2,1)S(1)} %get-tuple-element.130), channel_id=1, source_target_pairs={{0,8},{1,9},{2,10},{3,11},{4,12},{5,13},{6,14},{7,15},{8,0},{9,1},... | collective-permute-start | bytes 393224 | tf_op jit(solution)/shard_map/ppermute | solution.py:369
  26.7 13.7 %collective-permute-start.4 = (bf16[2,256,128]{2,1,0:T(8,128)(2,1)S(1)}, bf16[2,256,128]{2,1,0:T(8,128)(2,1)S(1)}, u32[]{:S(2)}, u32[]{:S(2)}) collective-permute-start(bf16[2,256,128]{2,1,0:T(8,128)(2,1)S(1)} %get-tuple-element.131), channel_id=1, source_target_pairs={{0,10},{1,11},{2,8},{3,9},{4,14},{5,15},{6,12},{7,13},{8,2},{9,3},... | collective-permute-start | bytes 393224 | tf_op jit(solution)/shard_map/ppermute | solution.py:369
  28.0 12.4 %collective-permute-start.5 = (bf16[2,256,128]{2,1,0:T(8,128)(2,1)S(1)}, bf16[2,256,128]{2,1,0:T(8,128)(2,1)S(1)}, u32[]{:S(2)}, u32[]{:S(2)}) collective-permute-start(bf16[2,256,128]{2,1,0:T(8,128)(2,1)S(1)} %get-tuple-element.127), channel_id=1, source_target_pairs={{0,2},{1,3},{2,0},{3,1},{4,6},{5,7},{6,4},{7,5},{8,10},{9,11},{10,... | collective-permute-start | bytes 393224 | tf_op jit(solution)/shard_map/ppermute | solution.py:369
  28.3 12.1 %collective-permute-start.6 = (bf16[2,256,128]{2,1,0:T(8,128)(2,1)S(1)}, bf16[2,256,128]{2,1,0:T(8,128)(2,1)S(1)}, u32[]{:S(2)}, u32[]{:S(2)}) collective-permute-start(bf16[2,256,128]{2,1,0:T(8,128)(2,1)S(1)} %get-tuple-element.128), channel_id=1, source_target_pairs={{0,4},{1,5},{2,6},{3,7},{4,0},{5,1},{6,2},{7,3},{8,12},{9,13},{10,... | collective-permute-start | bytes 393224 | tf_op jit(solution)/shard_map/ppermute | solution.py:369
  30.1 11.8 %collective-permute-start.7 = (bf16[2,256,128]{2,1,0:T(8,128)(2,1)S(1)}, bf16[2,256,128]{2,1,0:T(8,128)(2,1)S(1)}, u32[]{:S(2)}, u32[]{:S(2)}) collective-permute-start(bf16[2,256,128]{2,1,0:T(8,128)(2,1)S(1)} %get-tuple-element.129), channel_id=1, source_target_pairs={{0,6},{1,7},{2,4},{3,5},{4,2},{5,3},{6,0},{7,1},{8,14},{9,15},{10,... | collective-permute-start | bytes 393224 | tf_op jit(solution)/shard_map/ppermute | solution.py:369
  41.9 22.5 %collective-permute-start.27 = (bf16[6,512,512]{2,1,0:T(8,128)(2,1)S(1)}, bf16[6,512,512]{2,1,0:T(8,128)(2,1)S(1)}, u32[]{:S(2)}, u32[]{:S(2)}) collective-permute-start(bf16[6,512,512]{2,1,0:T(8,128)(2,1)S(1)} %get-tuple-element.186), channel_id=1, source_target_pairs={{0,1},{1,0},{2,3},{3,2},{4,5},{5,4},{6,7},{7,6},{8,9},{9,8},{10,11... | collective-permute-start | bytes 9437192 | tf_op jit(solution)/shard_map/ppermute | solution.py:369
  41.9 18.2 %collective-permute-start.26 = (bf16[2,512,512]{2,1,0:T(8,128)(2,1)S(1)}, bf16[2,512,512]{2,1,0:T(8,128)(2,1)S(1)}, u32[]{:S(2)}, u32[]{:S(2)}) collective-permute-start(bf16[2,512,512]{2,1,0:T(8,128)(2,1)S(1)} %get-tuple-element.183), channel_id=1, source_target_pairs={{0,1},{1,0},{2,3},{3,2},{4,5},{5,4},{6,7},{7,6},{8,9},{9,8},{10,11... | collective-permute-start | bytes 3145736 | tf_op jit(solution)/shard_map/ppermute | solution.py:369
  42.4 10.5 %collective-permute-start.8 = (bf16[2,256,128]{2,1,0:T(8,128)(2,1)S(1)}, bf16[2,256,128]{2,1,0:T(8,128)(2,1)S(1)}, u32[]{:S(2)}, u32[]{:S(2)}) collective-permute-start(bf16[2,256,128]{2,1,0:T(8,128)(2,1)S(1)} %get-tuple-element.134), channel_id=1, source_target_pairs={{0,12},{1,13},{2,14},{3,15},{4,8},{5,9},{6,10},{7,11},{8,4},{9,5},... | collective-permute-start | bytes 393224 | tf_op jit(solution)/shard_map/ppermute | solution.py:369
  47.0 8.0 %collective-permute-start.9 = (bf16[2,256,128]{2,1,0:T(8,128)(2,1)S(1)}, bf16[2,256,128]{2,1,0:T(8,128)(2,1)S(1)}, u32[]{:S(2)}, u32[]{:S(2)}) collective-permute-start(bf16[2,256,128]{2,1,0:T(8,128)(2,1)S(1)} %get-tuple-element.135), channel_id=1, source_target_pairs={{0,14},{1,15},{2,12},{3,13},{4,10},{5,11},{6,8},{7,9},{8,6},{9,7},... | collective-permute-start | bytes 393224 | tf_op jit(solution)/shard_map/ppermute | solution.py:369
  61.5 5.9 %collective-permute-start.28 = (bf16[128,512]{1,0:T(8,128)(2,1)S(1)}, bf16[128,512]{1,0:T(8,128)(2,1)S(1)}, u32[]{:S(2)}, u32[]{:S(2)}) collective-permute-start(bf16[128,512]{1,0:T(8,128)(2,1)S(1)} %get-tuple-element.188), channel_id=1, source_target_pairs={{0,4},{1,5},{4,8},{5,9},{8,12},{9,13},{12,14},{13,15},{14,10},{15,... | collective-permute-start | bytes 393224 | tf_op jit(solution)/shard_map/ppermute | solution.py:366
  64.3 5.6 %collective-permute-start.32 = (bf16[128,512]{1,0:T(8,128)(2,1)S(1)}, bf16[128,512]{1,0:T(8,128)(2,1)S(1)}, u32[]{:S(2)}, u32[]{:S(2)}) collective-permute-start(bf16[128,512]{1,0:T(8,128)(2,1)S(1)} %get-tuple-element.192), channel_id=1, source_target_pairs={{0,2},{1,3},{4,0},{5,1},{8,4},{9,5},{12,8},{13,9},{14,12},{15,13},... | collective-permute-start | bytes 393224 | tf_op jit(solution)/shard_map/ppermute | solution.py:366
  72.5 5.3 %collective-permute-start.30 = (bf16[128,512]{1,0:T(8,128)(2,1)S(1)}, bf16[128,512]{1,0:T(8,128)(2,1)S(1)}, u32[]{:S(2)}, u32[]{:S(2)}) collective-permute-start(bf16[128,512]{1,0:T(8,128)(2,1)S(1)} %add_convert_fusion.4), channel_id=1, source_target_pairs={{0,4},{1,5},{4,8},{5,9},{8,12},{9,13},{12,14},{13,15},{14,10},{15,... | collective-permute-start | bytes 393224 | tf_op jit(solution)/shard_map/ppermute | solution.py:366
  75.1 5.3 %collective-permute-start.34 = (bf16[128,512]{1,0:T(8,128)(2,1)S(1)}, bf16[128,512]{1,0:T(8,128)(2,1)S(1)}, u32[]{:S(2)}, u32[]{:S(2)}) collective-permute-start(bf16[128,512]{1,0:T(8,128)(2,1)S(1)} %add_convert_fusion.1), channel_id=1, source_target_pairs={{0,2},{1,3},{4,0},{5,1},{8,4},{9,5},{12,8},{13,9},{14,12},{15,13},... | collective-permute-start | bytes 393224 | tf_op jit(solution)/shard_map/ppermute | solution.py:366
  (12 other events, 51.8 us)

commit v6 on v5

--- a/solution.py
+++ b/solution.py
@@ -13,6 +13,7 @@
 DH = 128
 EPS = 1e-05
 PAD = 16
+BLOCK = 512
 MIB = 1 << 20
 TRANS_B = (((1,), (1,)), ((), ()))
 
@@ -51,13 +52,18 @@
     return chip_at(lax.rem(place_of(chip, chips) + offset + chips, chips), chips)
 
 
-def pack_kernel(tokens, gain, block, sem):
+def pack_kernel(tokens, gain, block, near, sems):
     rows, width = tokens.shape
-    copy = pltpu.make_async_copy(tokens, block.at[pl.ds(0, rows), :], sem)
-    copy.start()
-    wide = gain[...].astype(jnp.float32).reshape(1, width)
+    copies = [
+        pltpu.make_async_copy(gain, near, sems.at[0]),
+        pltpu.make_async_copy(tokens, block.at[pl.ds(0, rows), :], sems.at[1]),
+    ]
+    for copy in copies:
+        copy.start()
+    copies[0].wait()
+    wide = near[...].astype(jnp.float32).reshape(1, width)
     block[rows:, :] = jnp.broadcast_to(wide, (PAD, width)).astype(jnp.bfloat16)
-    copy.wait()
+    copies[1].wait()
 
 
 def pack(tokens, gain):
@@ -65,11 +71,11 @@
     return pl.pallas_call(
         pack_kernel,
         out_shape=pltpu.VMEM((rows + PAD, width), jnp.bfloat16),
-        in_specs=anywhere(1) + in_vmem(1),
+        in_specs=anywhere(2),
         out_specs=in_vmem(1)[0],
-        scratch_shapes=[pltpu.SemaphoreType.DMA],
+        scratch_shapes=[pltpu.VMEM((width,), jnp.bfloat16), pltpu.SemaphoreType.DMA((2,))],
         name="pack",
-    )(tokens, gain)
+    )(in_hbm(tokens), in_hbm(gain))
 
 
 def cut_kernel(chips, cache, *pieces):
@@ -239,17 +245,18 @@
         for head in range(heads):
             start = number * lines + head * rows
             query_all[start : start + rows, :] = query_ref[:, head * DH : (head + 1) * DH]
-    query = query_all[...]
-    keys_own = jnp.concatenate([own_key] * (2 * heads), axis=0)
-    own = jnp.sum(query.astype(jnp.float32) * keys_own, axis=1, keepdims=True) / math.sqrt(DH)
-    lane = lax.broadcasted_iota(jnp.int32, (2 * lines, 128), 1)
-    line = lax.broadcasted_iota(jnp.int32, (2 * lines, 128), 0)
-    total = jnp.where((lane == 0) & (line < lines), 1.0, 0.0)
-    numerator = jnp.concatenate([own_value] * heads + [jnp.zeros((lines, DH), jnp.float32)], axis=0)
-    top, total, numerator = weigh(query, caches, scores, own, total, numerator)
-    top_ref[...] = jnp.broadcast_to(top, top_ref.shape)
-    total_ref[...] = total
-    numerator_ref[...] = numerator
+    lane = lax.broadcasted_iota(jnp.int32, (rows, 128), 1)
+    for start in range(0, 2 * lines, rows):
+        some = slice(start, start + rows)
+        query = query_all[some, :]
+        own = jnp.sum(query.astype(jnp.float32) * own_key, axis=1, keepdims=True) / math.sqrt(DH)
+        mine_here = start < lines
+        total = jnp.where(lane == 0, 1.0, 0.0) if mine_here else jnp.zeros((rows, 128), jnp.float32)
+        numerator = own_value if mine_here else jnp.zeros((rows, DH), jnp.float32)
+        top, total, numerator = weigh(query, caches, scores.at[some, :], own, total, numerator)
+        top_ref[some, :] = jnp.broadcast_to(top, (rows, 128))
+        total_ref[some, :] = total
+        numerator_ref[some, :] = numerator
 
 
 def begin(caches, owns, mine, other):
@@ -273,12 +280,15 @@
 def finish_kernel(count, *refs):
     caches = refs[:count]
     query_all, top_ref, total_ref, numerator_ref, state_ref, sum_ref, scores = refs[count:]
-    top, total, numerator = weigh(
-        query_all[...], caches, scores, top_ref[:, 0:1], total_ref[...], numerator_ref[...]
-    )
-    lane = lax.broadcasted_iota(jnp.int32, total.shape, 1)
-    state_ref[...] = jnp.where(lane < 64, top, jnp.sum(total, axis=1, keepdims=True))
-    sum_ref[...] = numerator
+    lines = query_all.shape[0]
+    for start in range(0, lines, BLOCK):
+        some = slice(start, start + BLOCK)
+        top, total, numerator = weigh(
+            query_all[some, :], caches, scores.at[some, :], top_ref[some, 0:1], total_ref[some, :], numerator_ref[some, :]
+        )
+        lane = lax.broadcasted_iota(jnp.int32, total.shape, 1)
+        state_ref[some, :] = jnp.where(lane < 64, top, jnp.sum(total, axis=1, keepdims=True))
+        sum_ref[some, :] = numerator
 
 
 def finish(caches, state):

time: 83.9 us -> 82.8 us (0.987)
  Pallas kernels: 24.1 us -> 23 us
where the time goes in v6:
time: 82.8 us; the launch traced here: 82.6 us
  starting transfers between devices  34 us (41%)
  waiting for transfers between devices  24.5 us (30%)
  Pallas kernels  23 us (28%)
  other arithmetic  0.86 us (1%)
    ppermute x14, starting transfers between devices, around(): return lax.ppermute(value, 'seq', pairs)  19.5 us
    ppermute x14, waiting for transfers between devices, around(): return lax.ppermute(value, 'seq', pairs)  17.2 us
    ppermute x21, starting transfers between devices, swap(): return lax.ppermute(value, 'seq', [(i, i ^ bits) for i in range(size)])  14.4 us
    ppermute x21, waiting for transfers between devices, swap(): return lax.ppermute(value, 'seq', [(i, i ^ bits) for i in range(size)])  7.31 us
    pallas_call x1, Pallas kernels, project(): pl.pallas_call(functools.partial(project_kernel, offsets, chips, rows), o...  4.92 us
    pallas_call x2, Pallas kernels, half(): pl.pallas_call(functools.partial(half_kernel, groups, chips, width), out_...  4.55 us
    pallas_call x2, Pallas kernels, fetch(): pl.pallas_call(functools.partial(fetch_kernel, start, size), out_shape=pl...  4.39 us
    pallas_call x1, Pallas kernels, begin(): pl.pallas_call(functools.partial(begin_kernel, count, len(owns), heads),...  3.62 us
  transfers between devices with their start and end apart: 35, of which 15 were waited for; matrix products, arithmetic and copies ran while one was open for 0% of the time, Pallas kernels for 27%

profile of v6, /device:TPU:0, one launch (start us, length us, event | category | flops | bytes accessed | tf_op | source)
XLA Modules:
  0.0 82.6 jit_solution(4696827943561286649)
XLA Ops:
  1.0 3.1 %collective-permute-start = (bf16[144,512]{1,0:T(8,128)(2,1)S(1)}, bf16[144,512]{1,0:T(8,128)(2,1)S(1)}, u32[]{:S(2)}, u32[]{:S(2)}) collective-permute-start(bf16[144,512]{1,0:T(8,128)(2,1)S(1)} %pack.1.refs_0_), channel_id=1, source_target_pairs={{0,4},{1,5},{4,8},{5,9},{8,12},{9,13},{12,14},{13,15},{14,10},{15,... | collective-permute-start | bytes 442376 | tf_op jit(solution)/shard_map/ppermute | solution.py:376
  4.0 2.2 %fetch.2.refs_16_ = bf16[256,8192]{1,0:T(8,128)(2,1)S(1)} custom-call(bf16[512,8192]{1,0:T(8,128)(2,1)} %source.1), custom_call_target="tpu_custom_call" | custom-call | bytes 8388608 | tf_op jit(solution)/shard_map/fetch/pallas_call | solution.py:140
  7.8 1.8 %collective-permute-start.1 = (bf16[144,512]{1,0:T(8,128)(2,1)S(1)}, bf16[144,512]{1,0:T(8,128)(2,1)S(1)}, u32[]{:S(2)}, u32[]{:S(2)}) collective-permute-start(bf16[144,512]{1,0:T(8,128)(2,1)S(1)} %collective-permute-done.refs_2_), channel_id=1, source_target_pairs={{0,4},{1,5},{4,8},{5,9},{8,12},{9,13},{12,14},{13,15},{14,10},{15,... | collective-permute-start | bytes 442376 | tf_op jit(solution)/shard_map/ppermute | solution.py:376
  9.9 2.2 %fetch.3.refs_17_ = bf16[256,8192]{1,0:T(8,128)(2,1)S(1)} custom-call(bf16[512,8192]{1,0:T(8,128)(2,1)} %source.1), custom_call_target="tpu_custom_call" | custom-call | bytes 8388608 | tf_op jit(solution)/shard_map/fetch/pallas_call | solution.py:140
  13.0 1.8 %collective-permute-start.2 = (bf16[144,512]{1,0:T(8,128)(2,1)S(1)}, bf16[144,512]{1,0:T(8,128)(2,1)S(1)}, u32[]{:S(2)}, u32[]{:S(2)}) collective-permute-start(bf16[144,512]{1,0:T(8,128)(2,1)S(1)} %collective-permute-done.1.refs_6_), channel_id=1, source_target_pairs={{0,4},{1,5},{4,8},{5,9},{8,12},{9,13},{12,14},{13,15},{14,10},{15,... | collective-permute-start | bytes 442376 | tf_op jit(solution)/shard_map/ppermute | solution.py:376
  15.3 2.0 %collective-permute-done.15.refs_8_ = bf16[144,512]{1,0:T(8,128)(2,1)S(1)} collective-permute-done((bf16[144,512]{1,0:T(8,128)(2,1)S(1)}, bf16[144,512]{1,0:T(8,128)(2,1)S(1)}, u32[]{:S(2)}, u32[]{:S(2)}) %collective-permute-start.15) | collective-permute-done | bytes 147488 | tf_op jit(solution)/shard_map/ppermute | solution.py:376
  18.1 1.8 %collective-permute-start.20 = (bf16[144,512]{1,0:T(8,128)(2,1)S(1)}, bf16[144,512]{1,0:T(8,128)(2,1)S(1)}, u32[]{:S(2)}, u32[]{:S(2)}) collective-permute-start(bf16[144,512]{1,0:T(8,128)(2,1)S(1)} %collective-permute-done.2.refs_10_), channel_id=1, source_target_pairs={{0,4},{1,5},{4,8},{5,9},{8,12},{9,13},{12,14},{13,15},{14,10},{15,... | collective-permute-start | bytes 442376 | tf_op jit(solution)/shard_map/ppermute | solution.py:376
  20.5 2.0 %collective-permute-done.18.refs_12_ = bf16[144,512]{1,0:T(8,128)(2,1)S(1)} collective-permute-done((bf16[144,512]{1,0:T(8,128)(2,1)S(1)}, bf16[144,512]{1,0:T(8,128)(2,1)S(1)}, u32[]{:S(2)}, u32[]{:S(2)}) %collective-permute-start.18) | collective-permute-done | bytes 147488 | tf_op jit(solution)/shard_map/ppermute | solution.py:376
  23.3 2.8 %collective-permute-start.3 = (bf16[2,256,128]{2,1,0:T(8,128)(2,1)S(1)}, bf16[2,256,128]{2,1,0:T(8,128)(2,1)S(1)}, u32[]{:S(2)}, u32[]{:S(2)}) collective-permute-start(bf16[2,256,128]{2,1,0:T(8,128)(2,1)S(1)} %get-tuple-element.130), channel_id=1, source_target_pairs={{0,8},{1,9},{2,10},{3,11},{4,12},{5,13},{6,14},{7,15},{8,0},{9,1},... | collective-permute-start | bytes 393224 | tf_op jit(solution)/shard_map/ppermute | solution.py:379
  30.9 4.9 %project.1 = (bf16[128,512]{1,0:T(8,128)(2,1)S(1)}, bf16[128,128]{1,0:T(8,128)(2,1)S(1)}) custom-call(bf16[144,512]{1,0:T(8,128)(2,1)S(1)} %pack.1.refs_0_, bf16[144,512]{1,0:T(8,128)(2,1)S(1)} %collective-permute-done.10.refs_1_, bf16[144,512]{1,0:T(8,128)(2,1)S(1)} %collective-permute-done.refs_2_, bf16[144,512]{1,0:T(8,128)(2,1)S(1)} %collective-permute-done.11.refs_3_, ...), custom_call_target="tpu_custom_call" | custom-call | tf_op jit(solution)/shard_map/project/pallas_call | solution.py:193
  35.8 2.3 %half.2 = (bf16[2,512,512]{2,1,0:T(8,128)(2,1)S(1)}, bf16[6,512,512]{2,1,0:T(8,128)(2,1)S(1)}) custom-call(bf16[512,8192]{1,0:T(8,128)(2,1)} %w_out.1), custom_call_target="tpu_custom_call" | custom-call | tf_op jit(solution)/shard_map/half/pallas_call | solution.py:122
  41.8 4.6 %collective-permute-start.8 = (bf16[2,256,128]{2,1,0:T(8,128)(2,1)S(1)}, bf16[2,256,128]{2,1,0:T(8,128)(2,1)S(1)}, u32[]{:S(2)}, u32[]{:S(2)}) collective-permute-start(bf16[2,256,128]{2,1,0:T(8,128)(2,1)S(1)} %get-tuple-element.134), channel_id=1, source_target_pairs={{0,12},{1,13},{2,14},{3,15},{4,8},{5,9},{6,10},{7,11},{8,4},{9,5},... | collective-permute-start | bytes 393224 | tf_op jit(solution)/shard_map/ppermute | solution.py:379
  46.4 3.6 %begin.1 = (bf16[1024,128]{1,0:T(8,128)(2,1)S(1)}, f32[1024,128]{1,0:T(8,128)S(1)}, f32[1024,128]{1,0:T(8,128)S(1)}, f32[1024,128]{1,0:T(8,128)S(1)}) custom-call(bf16[2,256,128]{2,1,0:T(8,128)(2,1)S(1)} %get-tuple-element.144.refs_0_, bf16[2,256,128]{2,1,0:T(8,128)(2,1)S(1)} %collective-permute-done.3.refs_1_, ...), custom_call_target="tpu_custom_call" | custom-call | flops 1 | bytes 1 | tf_op jit(solution)/shard_map/begin/pallas_call | solution.py:267
  50.0 2.3 %half.3 = (bf16[2,512,512]{2,1,0:T(8,128)(2,1)S(1)}, bf16[6,512,512]{2,1,0:T(8,128)(2,1)S(1)}) custom-call(bf16[512,8192]{1,0:T(8,128)(2,1)} %w_out.1), custom_call_target="tpu_custom_call" | custom-call | tf_op jit(solution)/shard_map/half/pallas_call | solution.py:122
  52.3 2.1 %collective-permute-done.9.refs_1_ = bf16[2,256,128]{2,1,0:T(8,128)(2,1)S(1)} collective-permute-done((bf16[2,256,128]{2,1,0:T(8,128)(2,1)S(1)}, bf16[2,256,128]{2,1,0:T(8,128)(2,1)S(1)}, u32[]{:S(2)}, u32[]{:S(2)}) %collective-permute-start.9) | collective-permute-done | bytes 131104 | tf_op jit(solution)/shard_map/ppermute | solution.py:379
  54.4 2.0 %finish.1 = (f32[1024,128]{1,0:T(8,128)S(1)}, f32[1024,128]{1,0:T(8,128)S(1)}) custom-call(bf16[2,256,128]{2,1,0:T(8,128)(2,1)S(1)} %collective-permute-done.8.refs_0_, bf16[2,256,128]{2,1,0:T(8,128)(2,1)S(1)} %collective-permute-done.9.refs_1_, bf16[1024,128]{1,0:T(8,128)(2,1)S(1)} %get-tuple-element.176.refs_2_, ...), custom_call_target="tpu_custom_call" | custom-call | tf_op jit(solution)/shard_map/finish/pallas_call | solution.py:298
  60.4 2.9 %collective-permute-start.28 = (bf16[128,512]{1,0:T(8,128)(2,1)S(1)}, bf16[128,512]{1,0:T(8,128)(2,1)S(1)}, u32[]{:S(2)}, u32[]{:S(2)}) collective-permute-start(bf16[128,512]{1,0:T(8,128)(2,1)S(1)} %get-tuple-element.188), channel_id=1, source_target_pairs={{0,4},{1,5},{4,8},{5,9},{8,12},{9,13},{12,14},{13,15},{14,10},{15,... | collective-permute-start | bytes 393224 | tf_op jit(solution)/shard_map/ppermute | solution.py:376
  64.3 2.1 %collective-permute-done.28 = bf16[128,512]{1,0:T(8,128)(2,1)S(1)} collective-permute-done((bf16[128,512]{1,0:T(8,128)(2,1)S(1)}, bf16[128,512]{1,0:T(8,128)(2,1)S(1)}, u32[]{:S(2)}, u32[]{:S(2)}) %collective-permute-start.28) | collective-permute-done | bytes 131104 | tf_op jit(solution)/shard_map/ppermute | solution.py:376
  66.4 2.5 %collective-permute-start.29 = (bf16[128,512]{1,0:T(8,128)(2,1)S(1)}, bf16[128,512]{1,0:T(8,128)(2,1)S(1)}, u32[]{:S(2)}, u32[]{:S(2)}) collective-permute-start(bf16[128,512]{1,0:T(8,128)(2,1)S(1)} %add_convert_fusion.5), channel_id=1, source_target_pairs={{0,4},{1,5},{4,8},{5,9},{8,12},{9,13},{12,14},{13,15},{14,10},{15,... | collective-permute-start | bytes 393224 | tf_op jit(solution)/shard_map/ppermute | solution.py:376
  69.0 2.4 %collective-permute-done.29 = bf16[128,512]{1,0:T(8,128)(2,1)S(1)} collective-permute-done((bf16[128,512]{1,0:T(8,128)(2,1)S(1)}, bf16[128,512]{1,0:T(8,128)(2,1)S(1)}, u32[]{:S(2)}, u32[]{:S(2)}) %collective-permute-start.29) | collective-permute-done | bytes 131104 | tf_op jit(solution)/shard_map/ppermute | solution.py:376
  71.5 2.5 %collective-permute-start.30 = (bf16[128,512]{1,0:T(8,128)(2,1)S(1)}, bf16[128,512]{1,0:T(8,128)(2,1)S(1)}, u32[]{:S(2)}, u32[]{:S(2)}) collective-permute-start(bf16[128,512]{1,0:T(8,128)(2,1)S(1)} %add_convert_fusion.4), channel_id=1, source_target_pairs={{0,4},{1,5},{4,8},{5,9},{8,12},{9,13},{12,14},{13,15},{14,10},{15,... | collective-permute-start | bytes 393224 | tf_op jit(solution)/shard_map/ppermute | solution.py:376
  74.1 2.7 %collective-permute-done.30 = bf16[128,512]{1,0:T(8,128)(2,1)S(1)} collective-permute-done((bf16[128,512]{1,0:T(8,128)(2,1)S(1)}, bf16[128,512]{1,0:T(8,128)(2,1)S(1)}, u32[]{:S(2)}, u32[]{:S(2)}) %collective-permute-start.30) | collective-permute-done | bytes 131104 | tf_op jit(solution)/shard_map/ppermute | solution.py:376
  76.8 2.5 %collective-permute-start.31 = (bf16[128,512]{1,0:T(8,128)(2,1)S(1)}, bf16[128,512]{1,0:T(8,128)(2,1)S(1)}, u32[]{:S(2)}, u32[]{:S(2)}) collective-permute-start(bf16[128,512]{1,0:T(8,128)(2,1)S(1)} %add_convert_fusion.3), channel_id=1, source_target_pairs={{0,4},{1,5},{4,8},{5,9},{8,12},{9,13},{12,14},{13,15},{14,10},{15,... | collective-permute-start | bytes 393224 | tf_op jit(solution)/shard_map/ppermute | solution.py:376
  79.3 2.5 %collective-permute-done.31 = bf16[128,512]{1,0:T(8,128)(2,1)S(1)} collective-permute-done((bf16[128,512]{1,0:T(8,128)(2,1)S(1)}, bf16[128,512]{1,0:T(8,128)(2,1)S(1)}, u32[]{:S(2)}, u32[]{:S(2)}) %collective-permute-start.31) | collective-permute-done | bytes 131104 | tf_op jit(solution)/shard_map/ppermute | solution.py:376
  (65 shorter events, 20.9 us)
Async XLA Ops:
  1.0 6.9 %collective-permute-start = (bf16[144,512]{1,0:T(8,128)(2,1)S(1)}, bf16[144,512]{1,0:T(8,128)(2,1)S(1)}, u32[]{:S(2)}, u32[]{:S(2)}) collective-permute-start(bf16[144,512]{1,0:T(8,128)(2,1)S(1)} %pack.1.refs_0_), channel_id=1, source_target_pairs={{0,4},{1,5},{4,8},{5,9},{8,12},{9,13},{12,14},{13,15},{14,10},{15,... | collective-permute-start | bytes 442376 | tf_op jit(solution)/shard_map/ppermute | solution.py:376
  4.0 8.1 %collective-permute-start.12 = (bf16[144,512]{1,0:T(8,128)(2,1)S(1)}, bf16[144,512]{1,0:T(8,128)(2,1)S(1)}, u32[]{:S(2)}, u32[]{:S(2)}) collective-permute-start(bf16[144,512]{1,0:T(8,128)(2,1)S(1)} %pack.1.refs_0_), channel_id=1, source_target_pairs={{0,2},{1,3},{4,0},{5,1},{8,4},{9,5},{12,8},{13,9},{14,12},{15,13},... | collective-permute-start | bytes 442376 | tf_op jit(solution)/shard_map/ppermute | solution.py:376
  7.8 5.1 %collective-permute-start.1 = (bf16[144,512]{1,0:T(8,128)(2,1)S(1)}, bf16[144,512]{1,0:T(8,128)(2,1)S(1)}, u32[]{:S(2)}, u32[]{:S(2)}) collective-permute-start(bf16[144,512]{1,0:T(8,128)(2,1)S(1)} %collective-permute-done.refs_2_), channel_id=1, source_target_pairs={{0,4},{1,5},{4,8},{5,9},{8,12},{9,13},{12,14},{13,15},{14,10},{15,... | collective-permute-start | bytes 442376 | tf_op jit(solution)/shard_map/ppermute | solution.py:376
  12.1 5.2 %collective-permute-start.15 = (bf16[144,512]{1,0:T(8,128)(2,1)S(1)}, bf16[144,512]{1,0:T(8,128)(2,1)S(1)}, u32[]{:S(2)}, u32[]{:S(2)}) collective-permute-start(bf16[144,512]{1,0:T(8,128)(2,1)S(1)} %collective-permute-done.12.refs_4_), channel_id=1, source_target_pairs={{0,2},{1,3},{4,0},{5,1},{8,4},{9,5},{12,8},{13,9},{14,12},{15,13},... | collective-permute-start | bytes 442376 | tf_op jit(solution)/shard_map/ppermute | solution.py:376
  14.8 5.1 %collective-permute-start.10 = (bf16[144,512]{1,0:T(8,128)(2,1)S(1)}, bf16[144,512]{1,0:T(8,128)(2,1)S(1)}, u32[]{:S(2)}, u32[]{:S(2)}) collective-permute-start(bf16[144,512]{1,0:T(8,128)(2,1)S(1)} %pack.1.refs_0_), channel_id=1, source_target_pairs={{0,1},{1,0},{2,3},{3,2},{4,5},{5,4},{6,7},{7,6},{8,9},{9,8},{10,11... | collective-permute-start | bytes 442376 | tf_op jit(solution)/shard_map/ppermute | solution.py:379
  14.8 5.1 %collective-permute-start.11 = (bf16[144,512]{1,0:T(8,128)(2,1)S(1)}, bf16[144,512]{1,0:T(8,128)(2,1)S(1)}, u32[]{:S(2)}, u32[]{:S(2)}) collective-permute-start(bf16[144,512]{1,0:T(8,128)(2,1)S(1)} %collective-permute-done.refs_2_), channel_id=1, source_target_pairs={{0,1},{1,0},{2,3},{3,2},{4,5},{5,4},{6,7},{7,6},{8,9},{9,8},{10,11... | collective-permute-start | bytes 442376 | tf_op jit(solution)/shard_map/ppermute | solution.py:379
  15.3 5.2 %collective-permute-start.13 = (bf16[144,512]{1,0:T(8,128)(2,1)S(1)}, bf16[144,512]{1,0:T(8,128)(2,1)S(1)}, u32[]{:S(2)}, u32[]{:S(2)}) collective-permute-start(bf16[144,512]{1,0:T(8,128)(2,1)S(1)} %collective-permute-done.12.refs_4_), channel_id=1, source_target_pairs={{0,1},{1,0},{2,3},{3,2},{4,5},{5,4},{6,7},{7,6},{8,9},{9,8},{10,11... | collective-permute-start | bytes 442376 | tf_op jit(solution)/shard_map/ppermute | solution.py:379
  19.9 6.2 %collective-permute-start.16 = (bf16[144,512]{1,0:T(8,128)(2,1)S(1)}, bf16[144,512]{1,0:T(8,128)(2,1)S(1)}, u32[]{:S(2)}, u32[]{:S(2)}) collective-permute-start(bf16[144,512]{1,0:T(8,128)(2,1)S(1)} %collective-permute-done.15.refs_8_), channel_id=1, source_target_pairs={{0,1},{1,0},{2,3},{3,2},{4,5},{5,4},{6,7},{7,6},{8,9},{9,8},{10,11... | collective-permute-start | bytes 442376 | tf_op jit(solution)/shard_map/ppermute | solution.py:379
  20.4 6.9 %collective-permute-start.17 = (bf16[144,512]{1,0:T(8,128)(2,1)S(1)}, bf16[144,512]{1,0:T(8,128)(2,1)S(1)}, u32[]{:S(2)}, u32[]{:S(2)}) collective-permute-start(bf16[144,512]{1,0:T(8,128)(2,1)S(1)} %collective-permute-done.2.refs_10_), channel_id=1, source_target_pairs={{0,1},{1,0},{2,3},{3,2},{4,5},{5,4},{6,7},{7,6},{8,9},{9,8},{10,11... | collective-permute-start | bytes 442376 | tf_op jit(solution)/shard_map/ppermute | solution.py:379
  22.5 5.2 %collective-permute-start.19 = (bf16[144,512]{1,0:T(8,128)(2,1)S(1)}, bf16[144,512]{1,0:T(8,128)(2,1)S(1)}, u32[]{:S(2)}, u32[]{:S(2)}) collective-permute-start(bf16[144,512]{1,0:T(8,128)(2,1)S(1)} %collective-permute-done.18.refs_12_), channel_id=1, source_target_pairs={{0,1},{1,0},{2,3},{3,2},{4,5},{5,4},{6,7},{7,6},{8,9},{9,8},{10,11... | collective-permute-start | bytes 442376 | tf_op jit(solution)/shard_map/ppermute | solution.py:379
  23.3 6.2 %collective-permute-start.21 = (bf16[144,512]{1,0:T(8,128)(2,1)S(1)}, bf16[144,512]{1,0:T(8,128)(2,1)S(1)}, u32[]{:S(2)}, u32[]{:S(2)}) collective-permute-start(bf16[144,512]{1,0:T(8,128)(2,1)S(1)} %collective-permute-done.20.refs_14_), channel_id=1, source_target_pairs={{0,1},{1,0},{2,3},{3,2},{4,5},{5,4},{6,7},{7,6},{8,9},{9,8},{10,11... | collective-permute-start | bytes 442376 | tf_op jit(solution)/shard_map/ppermute | solution.py:379
  23.3 14.8 %collective-permute-start.3 = (bf16[2,256,128]{2,1,0:T(8,128)(2,1)S(1)}, bf16[2,256,128]{2,1,0:T(8,128)(2,1)S(1)}, u32[]{:S(2)}, u32[]{:S(2)}) collective-permute-start(bf16[2,256,128]{2,1,0:T(8,128)(2,1)S(1)} %get-tuple-element.130), channel_id=1, source_target_pairs={{0,8},{1,9},{2,10},{3,11},{4,12},{5,13},{6,14},{7,15},{8,0},{9,1},... | collective-permute-start | bytes 393224 | tf_op jit(solution)/shard_map/ppermute | solution.py:379
  26.1 13.7 %collective-permute-start.4 = (bf16[2,256,128]{2,1,0:T(8,128)(2,1)S(1)}, bf16[2,256,128]{2,1,0:T(8,128)(2,1)S(1)}, u32[]{:S(2)}, u32[]{:S(2)}) collective-permute-start(bf16[2,256,128]{2,1,0:T(8,128)(2,1)S(1)} %get-tuple-element.131), channel_id=1, source_target_pairs={{0,10},{1,11},{2,8},{3,9},{4,14},{5,15},{6,12},{7,13},{8,2},{9,3},... | collective-permute-start | bytes 393224 | tf_op jit(solution)/shard_map/ppermute | solution.py:379
  27.4 12.4 %collective-permute-start.5 = (bf16[2,256,128]{2,1,0:T(8,128)(2,1)S(1)}, bf16[2,256,128]{2,1,0:T(8,128)(2,1)S(1)}, u32[]{:S(2)}, u32[]{:S(2)}) collective-permute-start(bf16[2,256,128]{2,1,0:T(8,128)(2,1)S(1)} %get-tuple-element.127), channel_id=1, source_target_pairs={{0,2},{1,3},{2,0},{3,1},{4,6},{5,7},{6,4},{7,5},{8,10},{9,11},{10,... | collective-permute-start | bytes 393224 | tf_op jit(solution)/shard_map/ppermute | solution.py:379
  27.7 12.1 %collective-permute-start.6 = (bf16[2,256,128]{2,1,0:T(8,128)(2,1)S(1)}, bf16[2,256,128]{2,1,0:T(8,128)(2,1)S(1)}, u32[]{:S(2)}, u32[]{:S(2)}) collective-permute-start(bf16[2,256,128]{2,1,0:T(8,128)(2,1)S(1)} %get-tuple-element.128), channel_id=1, source_target_pairs={{0,4},{1,5},{2,6},{3,7},{4,0},{5,1},{6,2},{7,3},{8,12},{9,13},{10,... | collective-permute-start | bytes 393224 | tf_op jit(solution)/shard_map/ppermute | solution.py:379
  29.5 11.8 %collective-permute-start.7 = (bf16[2,256,128]{2,1,0:T(8,128)(2,1)S(1)}, bf16[2,256,128]{2,1,0:T(8,128)(2,1)S(1)}, u32[]{:S(2)}, u32[]{:S(2)}) collective-permute-start(bf16[2,256,128]{2,1,0:T(8,128)(2,1)S(1)} %get-tuple-element.129), channel_id=1, source_target_pairs={{0,6},{1,7},{2,4},{3,5},{4,2},{5,3},{6,0},{7,1},{8,14},{9,15},{10,... | collective-permute-start | bytes 393224 | tf_op jit(solution)/shard_map/ppermute | solution.py:379
  41.2 22.1 %collective-permute-start.27 = (bf16[6,512,512]{2,1,0:T(8,128)(2,1)S(1)}, bf16[6,512,512]{2,1,0:T(8,128)(2,1)S(1)}, u32[]{:S(2)}, u32[]{:S(2)}) collective-permute-start(bf16[6,512,512]{2,1,0:T(8,128)(2,1)S(1)} %get-tuple-element.186), channel_id=1, source_target_pairs={{0,1},{1,0},{2,3},{3,2},{4,5},{5,4},{6,7},{7,6},{8,9},{9,8},{10,11... | collective-permute-start | bytes 9437192 | tf_op jit(solution)/shard_map/ppermute | solution.py:379
  41.3 17.8 %collective-permute-start.26 = (bf16[2,512,512]{2,1,0:T(8,128)(2,1)S(1)}, bf16[2,512,512]{2,1,0:T(8,128)(2,1)S(1)}, u32[]{:S(2)}, u32[]{:S(2)}) collective-permute-start(bf16[2,512,512]{2,1,0:T(8,128)(2,1)S(1)} %get-tuple-element.183), channel_id=1, source_target_pairs={{0,1},{1,0},{2,3},{3,2},{4,5},{5,4},{6,7},{7,6},{8,9},{9,8},{10,11... | collective-permute-start | bytes 3145736 | tf_op jit(solution)/shard_map/ppermute | solution.py:379
  41.8 10.5 %collective-permute-start.8 = (bf16[2,256,128]{2,1,0:T(8,128)(2,1)S(1)}, bf16[2,256,128]{2,1,0:T(8,128)(2,1)S(1)}, u32[]{:S(2)}, u32[]{:S(2)}) collective-permute-start(bf16[2,256,128]{2,1,0:T(8,128)(2,1)S(1)} %get-tuple-element.134), channel_id=1, source_target_pairs={{0,12},{1,13},{2,14},{3,15},{4,8},{5,9},{6,10},{7,11},{8,4},{9,5},... | collective-permute-start | bytes 393224 | tf_op jit(solution)/shard_map/ppermute | solution.py:379
  46.4 8.0 %collective-permute-start.9 = (bf16[2,256,128]{2,1,0:T(8,128)(2,1)S(1)}, bf16[2,256,128]{2,1,0:T(8,128)(2,1)S(1)}, u32[]{:S(2)}, u32[]{:S(2)}) collective-permute-start(bf16[2,256,128]{2,1,0:T(8,128)(2,1)S(1)} %get-tuple-element.135), channel_id=1, source_target_pairs={{0,14},{1,15},{2,12},{3,13},{4,10},{5,11},{6,8},{7,9},{8,6},{9,7},... | collective-permute-start | bytes 393224 | tf_op jit(solution)/shard_map/ppermute | solution.py:379
  60.4 5.9 %collective-permute-start.28 = (bf16[128,512]{1,0:T(8,128)(2,1)S(1)}, bf16[128,512]{1,0:T(8,128)(2,1)S(1)}, u32[]{:S(2)}, u32[]{:S(2)}) collective-permute-start(bf16[128,512]{1,0:T(8,128)(2,1)S(1)} %get-tuple-element.188), channel_id=1, source_target_pairs={{0,4},{1,5},{4,8},{5,9},{8,12},{9,13},{12,14},{13,15},{14,10},{15,... | collective-permute-start | bytes 393224 | tf_op jit(solution)/shard_map/ppermute | solution.py:376
  63.3 5.6 %collective-permute-start.32 = (bf16[128,512]{1,0:T(8,128)(2,1)S(1)}, bf16[128,512]{1,0:T(8,128)(2,1)S(1)}, u32[]{:S(2)}, u32[]{:S(2)}) collective-permute-start(bf16[128,512]{1,0:T(8,128)(2,1)S(1)} %get-tuple-element.192), channel_id=1, source_target_pairs={{0,2},{1,3},{4,0},{5,1},{8,4},{9,5},{12,8},{13,9},{14,12},{15,13},... | collective-permute-start | bytes 393224 | tf_op jit(solution)/shard_map/ppermute | solution.py:376
  71.5 5.3 %collective-permute-start.30 = (bf16[128,512]{1,0:T(8,128)(2,1)S(1)}, bf16[128,512]{1,0:T(8,128)(2,1)S(1)}, u32[]{:S(2)}, u32[]{:S(2)}) collective-permute-start(bf16[128,512]{1,0:T(8,128)(2,1)S(1)} %add_convert_fusion.4), channel_id=1, source_target_pairs={{0,4},{1,5},{4,8},{5,9},{8,12},{9,13},{12,14},{13,15},{14,10},{15,... | collective-permute-start | bytes 393224 | tf_op jit(solution)/shard_map/ppermute | solution.py:376
  74.0 5.3 %collective-permute-start.34 = (bf16[128,512]{1,0:T(8,128)(2,1)S(1)}, bf16[128,512]{1,0:T(8,128)(2,1)S(1)}, u32[]{:S(2)}, u32[]{:S(2)}) collective-permute-start(bf16[128,512]{1,0:T(8,128)(2,1)S(1)} %add_convert_fusion.1), channel_id=1, source_target_pairs={{0,2},{1,3},{4,0},{5,1},{8,4},{9,5},{12,8},{13,9},{14,12},{15,13},... | collective-permute-start | bytes 393224 | tf_op jit(solution)/shard_map/ppermute | solution.py:376
  (12 other events, 51.8 us)

commit v7 on v6

--- a/solution.py
+++ b/solution.py
@@ -326,7 +326,7 @@
         scale, far_scale = jnp.exp(top - peak), jnp.exp(far_top - peak)
         denominator = state[near_lines, 64:65] * scale + far_state[far_lines, 64:65] * far_scale
         numerator = sums[near_lines, :] * scale + far_sums[far_lines, :] * far_scale
-        result = (numerator / denominator).astype(jnp.bfloat16)
+        result = (numerator * (1.0 / denominator)).astype(jnp.bfloat16)
         for head in range(heads):
             attention_ref[number, :, head * DH : (head + 1) * DH] = result[head * rows : (head + 1) * rows, :]
         parts.append(attention_ref[number])
@@ -414,8 +414,8 @@
             take(left, step)
 
     soon = (chips - reach) // 2
-    sooner = [*range(reach, reach + soon), *range(1, reach)]
-    later = [step for step in range(1, chips) if step not in sooner]
+    sooner = [*range(reach, reach + soon), *reversed(range(1, reach))]
+    later = [*reversed(range(reach + soon, chips))]
     close = [swap(pieces[step], 2 * step) for step in sooner]
     pieces, close = lax.optimization_barrier((pieces, close))
     far_parts = [swap(pieces[step], 2 * step) for step in later]

time: 82.8 us -> 82.1 us (level)
    ppermute x21, waiting for transfers between devices: 7.31 us -> 6.17 us  [swap(): return lax.ppermute(value, 'seq', [(i, i ^ bits) for i in range(size)])]
  transfers between devices with their start and end apart: 35 -> 35, of which waited for: 15 -> 19; matrix products, arithmetic and copies ran while one was open for 0% -> 0% of each run, Pallas kernels for 27% -> 27%
where the time goes in v7:
time: 82.1 us; the launch traced here: 81.6 us
  starting transfers between devices  33.8 us (41%)
  waiting for transfers between devices  23.7 us (29%)
  Pallas kernels  22.9 us (28%)
  other arithmetic  0.86 us (1%)
    ppermute x14, starting transfers between devices, around(): return lax.ppermute(value, 'seq', pairs)  19.3 us
    ppermute x14, waiting for transfers between devices, around(): return lax.ppermute(value, 'seq', pairs)  17.6 us
    ppermute x21, starting transfers between devices, swap(): return lax.ppermute(value, 'seq', [(i, i ^ bits) for i in range(size)])  14.5 us
    ppermute x21, waiting for transfers between devices, swap(): return lax.ppermute(value, 'seq', [(i, i ^ bits) for i in range(size)])  6.17 us
    pallas_call x1, Pallas kernels, project(): pl.pallas_call(functools.partial(project_kernel, offsets, chips, rows), o...  4.92 us
    pallas_call x2, Pallas kernels, half(): pl.pallas_call(functools.partial(half_kernel, groups, chips, width), out_...  4.55 us
    pallas_call x2, Pallas kernels, fetch(): pl.pallas_call(functools.partial(fetch_kernel, start, size), out_shape=pl...  4.39 us
    pallas_call x1, Pallas kernels, begin(): pl.pallas_call(functools.partial(begin_kernel, count, len(owns), heads),...  3.62 us
  transfers between devices with their start and end apart: 35, of which 19 were waited for; matrix products, arithmetic and copies ran while one was open for 0% of the time, Pallas kernels for 27%

profile of v7, /device:TPU:0, one launch (start us, length us, event | category | flops | bytes accessed | tf_op | source)
XLA Modules:
  0.0 81.6 jit_solution(9288092029077324938)
XLA Ops:
  1.0 3.1 %collective-permute-start = (bf16[144,512]{1,0:T(8,128)(2,1)S(1)}, bf16[144,512]{1,0:T(8,128)(2,1)S(1)}, u32[]{:S(2)}, u32[]{:S(2)}) collective-permute-start(bf16[144,512]{1,0:T(8,128)(2,1)S(1)} %pack.1.refs_0_), channel_id=1, source_target_pairs={{0,4},{1,5},{4,8},{5,9},{8,12},{9,13},{12,14},{13,15},{14,10},{15,... | collective-permute-start | bytes 442376 | tf_op jit(solution)/shard_map/ppermute | solution.py:376
  4.0 2.2 %fetch.2.refs_16_ = bf16[256,8192]{1,0:T(8,128)(2,1)S(1)} custom-call(bf16[512,8192]{1,0:T(8,128)(2,1)} %source.1), custom_call_target="tpu_custom_call" | custom-call | bytes 8388608 | tf_op jit(solution)/shard_map/fetch/pallas_call | solution.py:140
  7.8 1.8 %collective-permute-start.1 = (bf16[144,512]{1,0:T(8,128)(2,1)S(1)}, bf16[144,512]{1,0:T(8,128)(2,1)S(1)}, u32[]{:S(2)}, u32[]{:S(2)}) collective-permute-start(bf16[144,512]{1,0:T(8,128)(2,1)S(1)} %collective-permute-done.refs_2_), channel_id=1, source_target_pairs={{0,4},{1,5},{4,8},{5,9},{8,12},{9,13},{12,14},{13,15},{14,10},{15,... | collective-permute-start | bytes 442376 | tf_op jit(solution)/shard_map/ppermute | solution.py:376
  9.9 2.2 %fetch.3.refs_17_ = bf16[256,8192]{1,0:T(8,128)(2,1)S(1)} custom-call(bf16[512,8192]{1,0:T(8,128)(2,1)} %source.1), custom_call_target="tpu_custom_call" | custom-call | bytes 8388608 | tf_op jit(solution)/shard_map/fetch/pallas_call | solution.py:140
  13.0 1.8 %collective-permute-start.2 = (bf16[144,512]{1,0:T(8,128)(2,1)S(1)}, bf16[144,512]{1,0:T(8,128)(2,1)S(1)}, u32[]{:S(2)}, u32[]{:S(2)}) collective-permute-start(bf16[144,512]{1,0:T(8,128)(2,1)S(1)} %collective-permute-done.1.refs_6_), channel_id=1, source_target_pairs={{0,4},{1,5},{4,8},{5,9},{8,12},{9,13},{12,14},{13,15},{14,10},{15,... | collective-permute-start | bytes 442376 | tf_op jit(solution)/shard_map/ppermute | solution.py:376
  15.3 2.0 %collective-permute-done.15.refs_8_ = bf16[144,512]{1,0:T(8,128)(2,1)S(1)} collective-permute-done((bf16[144,512]{1,0:T(8,128)(2,1)S(1)}, bf16[144,512]{1,0:T(8,128)(2,1)S(1)}, u32[]{:S(2)}, u32[]{:S(2)}) %collective-permute-start.15) | collective-permute-done | bytes 147488 | tf_op jit(solution)/shard_map/ppermute | solution.py:376
  18.1 1.8 %collective-permute-start.20 = (bf16[144,512]{1,0:T(8,128)(2,1)S(1)}, bf16[144,512]{1,0:T(8,128)(2,1)S(1)}, u32[]{:S(2)}, u32[]{:S(2)}) collective-permute-start(bf16[144,512]{1,0:T(8,128)(2,1)S(1)} %collective-permute-done.2.refs_10_), channel_id=1, source_target_pairs={{0,4},{1,5},{4,8},{5,9},{8,12},{9,13},{12,14},{13,15},{14,10},{15,... | collective-permute-start | bytes 442376 | tf_op jit(solution)/shard_map/ppermute | solution.py:376
  20.5 2.0 %collective-permute-done.18.refs_12_ = bf16[144,512]{1,0:T(8,128)(2,1)S(1)} collective-permute-done((bf16[144,512]{1,0:T(8,128)(2,1)S(1)}, bf16[144,512]{1,0:T(8,128)(2,1)S(1)}, u32[]{:S(2)}, u32[]{:S(2)}) %collective-permute-start.18) | collective-permute-done | bytes 147488 | tf_op jit(solution)/shard_map/ppermute | solution.py:376
  23.3 2.8 %collective-permute-start.3 = (bf16[2,256,128]{2,1,0:T(8,128)(2,1)S(1)}, bf16[2,256,128]{2,1,0:T(8,128)(2,1)S(1)}, u32[]{:S(2)}, u32[]{:S(2)}) collective-permute-start(bf16[2,256,128]{2,1,0:T(8,128)(2,1)S(1)} %get-tuple-element.130), channel_id=1, source_target_pairs={{0,8},{1,9},{2,10},{3,11},{4,12},{5,13},{6,14},{7,15},{8,0},{9,1},... | collective-permute-start | bytes 393224 | tf_op jit(solution)/shard_map/ppermute | solution.py:379
  29.1 1.7 %collective-permute-start.7 = (bf16[2,256,128]{2,1,0:T(8,128)(2,1)S(1)}, bf16[2,256,128]{2,1,0:T(8,128)(2,1)S(1)}, u32[]{:S(2)}, u32[]{:S(2)}) collective-permute-start(bf16[2,256,128]{2,1,0:T(8,128)(2,1)S(1)} %get-tuple-element.127), channel_id=1, source_target_pairs={{0,2},{1,3},{2,0},{3,1},{4,6},{5,7},{6,4},{7,5},{8,10},{9,11},{10,... | collective-permute-start | bytes 393224 | tf_op jit(solution)/shard_map/ppermute | solution.py:379
  30.9 4.9 %project.1 = (bf16[128,512]{1,0:T(8,128)(2,1)S(1)}, bf16[128,128]{1,0:T(8,128)(2,1)S(1)}) custom-call(bf16[144,512]{1,0:T(8,128)(2,1)S(1)} %pack.1.refs_0_, bf16[144,512]{1,0:T(8,128)(2,1)S(1)} %collective-permute-done.10.refs_1_, bf16[144,512]{1,0:T(8,128)(2,1)S(1)} %collective-permute-done.refs_2_, bf16[144,512]{1,0:T(8,128)(2,1)S(1)} %collective-permute-done.11.refs_3_, ...), custom_call_target="tpu_custom_call" | custom-call | tf_op jit(solution)/shard_map/project/pallas_call | solution.py:193
  35.8 2.3 %half.2 = (bf16[2,512,512]{2,1,0:T(8,128)(2,1)S(1)}, bf16[6,512,512]{2,1,0:T(8,128)(2,1)S(1)}) custom-call(bf16[512,8192]{1,0:T(8,128)(2,1)} %w_out.1), custom_call_target="tpu_custom_call" | custom-call | tf_op jit(solution)/shard_map/half/pallas_call | solution.py:122
  41.5 4.6 %collective-permute-start.8 = (bf16[2,256,128]{2,1,0:T(8,128)(2,1)S(1)}, bf16[2,256,128]{2,1,0:T(8,128)(2,1)S(1)}, u32[]{:S(2)}, u32[]{:S(2)}) collective-permute-start(bf16[2,256,128]{2,1,0:T(8,128)(2,1)S(1)} %get-tuple-element.134), channel_id=1, source_target_pairs={{0,14},{1,15},{2,12},{3,13},{4,10},{5,11},{6,8},{7,9},{8,6},{9,7},... | collective-permute-start | bytes 393224 | tf_op jit(solution)/shard_map/ppermute | solution.py:379
  46.1 3.6 %begin.1 = (bf16[1024,128]{1,0:T(8,128)(2,1)S(1)}, f32[1024,128]{1,0:T(8,128)S(1)}, f32[1024,128]{1,0:T(8,128)S(1)}, f32[1024,128]{1,0:T(8,128)S(1)}) custom-call(bf16[2,256,128]{2,1,0:T(8,128)(2,1)S(1)} %get-tuple-element.144.refs_0_, bf16[2,256,128]{2,1,0:T(8,128)(2,1)S(1)} %collective-permute-done.3.refs_1_, ...), custom_call_target="tpu_custom_call" | custom-call | flops 1 | bytes 1 | tf_op jit(solution)/shard_map/begin/pallas_call | solution.py:267
  49.8 2.3 %half.3 = (bf16[2,512,512]{2,1,0:T(8,128)(2,1)S(1)}, bf16[6,512,512]{2,1,0:T(8,128)(2,1)S(1)}) custom-call(bf16[512,8192]{1,0:T(8,128)(2,1)} %w_out.1), custom_call_target="tpu_custom_call" | custom-call | tf_op jit(solution)/shard_map/half/pallas_call | solution.py:122
  53.2 2.0 %finish.1 = (f32[1024,128]{1,0:T(8,128)S(1)}, f32[1024,128]{1,0:T(8,128)S(1)}) custom-call(bf16[2,256,128]{2,1,0:T(8,128)(2,1)S(1)} %collective-permute-done.8.refs_0_, bf16[2,256,128]{2,1,0:T(8,128)(2,1)S(1)} %collective-permute-done.9.refs_1_, bf16[1024,128]{1,0:T(8,128)(2,1)S(1)} %get-tuple-element.176.refs_2_, ...), custom_call_target="tpu_custom_call" | custom-call | tf_op jit(solution)/shard_map/finish/pallas_call | solution.py:298
  59.2 3.0 %collective-permute-start.28 = (bf16[128,512]{1,0:T(8,128)(2,1)S(1)}, bf16[128,512]{1,0:T(8,128)(2,1)S(1)}, u32[]{:S(2)}, u32[]{:S(2)}) collective-permute-start(bf16[128,512]{1,0:T(8,128)(2,1)S(1)} %get-tuple-element.188), channel_id=1, source_target_pairs={{0,4},{1,5},{4,8},{5,9},{8,12},{9,13},{12,14},{13,15},{14,10},{15,... | collective-permute-start | bytes 393224 | tf_op jit(solution)/shard_map/ppermute | solution.py:376
  63.3 2.1 %collective-permute-done.28 = bf16[128,512]{1,0:T(8,128)(2,1)S(1)} collective-permute-done((bf16[128,512]{1,0:T(8,128)(2,1)S(1)}, bf16[128,512]{1,0:T(8,128)(2,1)S(1)}, u32[]{:S(2)}, u32[]{:S(2)}) %collective-permute-start.28) | collective-permute-done | bytes 131104 | tf_op jit(solution)/shard_map/ppermute | solution.py:376
  65.3 2.5 %collective-permute-start.29 = (bf16[128,512]{1,0:T(8,128)(2,1)S(1)}, bf16[128,512]{1,0:T(8,128)(2,1)S(1)}, u32[]{:S(2)}, u32[]{:S(2)}) collective-permute-start(bf16[128,512]{1,0:T(8,128)(2,1)S(1)} %add_convert_fusion.5), channel_id=1, source_target_pairs={{0,4},{1,5},{4,8},{5,9},{8,12},{9,13},{12,14},{13,15},{14,10},{15,... | collective-permute-start | bytes 393224 | tf_op jit(solution)/shard_map/ppermute | solution.py:376
  68.4 2.4 %collective-permute-done.29 = bf16[128,512]{1,0:T(8,128)(2,1)S(1)} collective-permute-done((bf16[128,512]{1,0:T(8,128)(2,1)S(1)}, bf16[128,512]{1,0:T(8,128)(2,1)S(1)}, u32[]{:S(2)}, u32[]{:S(2)}) %collective-permute-start.29) | collective-permute-done | bytes 131104 | tf_op jit(solution)/shard_map/ppermute | solution.py:376
  70.8 2.2 %collective-permute-start.30 = (bf16[128,512]{1,0:T(8,128)(2,1)S(1)}, bf16[128,512]{1,0:T(8,128)(2,1)S(1)}, u32[]{:S(2)}, u32[]{:S(2)}) collective-permute-start(bf16[128,512]{1,0:T(8,128)(2,1)S(1)} %add_convert_fusion.4), channel_id=1, source_target_pairs={{0,4},{1,5},{4,8},{5,9},{8,12},{9,13},{12,14},{13,15},{14,10},{15,... | collective-permute-start | bytes 393224 | tf_op jit(solution)/shard_map/ppermute | solution.py:376
  73.5 2.3 %collective-permute-done.30 = bf16[128,512]{1,0:T(8,128)(2,1)S(1)} collective-permute-done((bf16[128,512]{1,0:T(8,128)(2,1)S(1)}, bf16[128,512]{1,0:T(8,128)(2,1)S(1)}, u32[]{:S(2)}, u32[]{:S(2)}) %collective-permute-start.30) | collective-permute-done | bytes 131104 | tf_op jit(solution)/shard_map/ppermute | solution.py:376
  75.8 2.5 %collective-permute-start.31 = (bf16[128,512]{1,0:T(8,128)(2,1)S(1)}, bf16[128,512]{1,0:T(8,128)(2,1)S(1)}, u32[]{:S(2)}, u32[]{:S(2)}) collective-permute-start(bf16[128,512]{1,0:T(8,128)(2,1)S(1)} %add_convert_fusion.3), channel_id=1, source_target_pairs={{0,4},{1,5},{4,8},{5,9},{8,12},{9,13},{12,14},{13,15},{14,10},{15,... | collective-permute-start | bytes 393224 | tf_op jit(solution)/shard_map/ppermute | solution.py:376
  78.5 2.4 %collective-permute-done.31 = bf16[128,512]{1,0:T(8,128)(2,1)S(1)} collective-permute-done((bf16[128,512]{1,0:T(8,128)(2,1)S(1)}, bf16[128,512]{1,0:T(8,128)(2,1)S(1)}, u32[]{:S(2)}, u32[]{:S(2)}) %collective-permute-start.31) | collective-permute-done | bytes 131104 | tf_op jit(solution)/shard_map/ppermute | solution.py:376
  (65 shorter events, 21.0 us)
Async XLA Ops:
  1.0 6.9 %collective-permute-start = (bf16[144,512]{1,0:T(8,128)(2,1)S(1)}, bf16[144,512]{1,0:T(8,128)(2,1)S(1)}, u32[]{:S(2)}, u32[]{:S(2)}) collective-permute-start(bf16[144,512]{1,0:T(8,128)(2,1)S(1)} %pack.1.refs_0_), channel_id=1, source_target_pairs={{0,4},{1,5},{4,8},{5,9},{8,12},{9,13},{12,14},{13,15},{14,10},{15,... | collective-permute-start | bytes 442376 | tf_op jit(solution)/shard_map/ppermute | solution.py:376
  4.0 8.1 %collective-permute-start.12 = (bf16[144,512]{1,0:T(8,128)(2,1)S(1)}, bf16[144,512]{1,0:T(8,128)(2,1)S(1)}, u32[]{:S(2)}, u32[]{:S(2)}) collective-permute-start(bf16[144,512]{1,0:T(8,128)(2,1)S(1)} %pack.1.refs_0_), channel_id=1, source_target_pairs={{0,2},{1,3},{4,0},{5,1},{8,4},{9,5},{12,8},{13,9},{14,12},{15,13},... | collective-permute-start | bytes 442376 | tf_op jit(solution)/shard_map/ppermute | solution.py:376
  7.8 5.1 %collective-permute-start.1 = (bf16[144,512]{1,0:T(8,128)(2,1)S(1)}, bf16[144,512]{1,0:T(8,128)(2,1)S(1)}, u32[]{:S(2)}, u32[]{:S(2)}) collective-permute-start(bf16[144,512]{1,0:T(8,128)(2,1)S(1)} %collective-permute-done.refs_2_), channel_id=1, source_target_pairs={{0,4},{1,5},{4,8},{5,9},{8,12},{9,13},{12,14},{13,15},{14,10},{15,... | collective-permute-start | bytes 442376 | tf_op jit(solution)/shard_map/ppermute | solution.py:376
  12.1 5.2 %collective-permute-start.15 = (bf16[144,512]{1,0:T(8,128)(2,1)S(1)}, bf16[144,512]{1,0:T(8,128)(2,1)S(1)}, u32[]{:S(2)}, u32[]{:S(2)}) collective-permute-start(bf16[144,512]{1,0:T(8,128)(2,1)S(1)} %collective-permute-done.12.refs_4_), channel_id=1, source_target_pairs={{0,2},{1,3},{4,0},{5,1},{8,4},{9,5},{12,8},{13,9},{14,12},{15,13},... | collective-permute-start | bytes 442376 | tf_op jit(solution)/shard_map/ppermute | solution.py:376
  13.0 5.1 %collective-permute-start.2 = (bf16[144,512]{1,0:T(8,128)(2,1)S(1)}, bf16[144,512]{1,0:T(8,128)(2,1)S(1)}, u32[]{:S(2)}, u32[]{:S(2)}) collective-permute-start(bf16[144,512]{1,0:T(8,128)(2,1)S(1)} %collective-permute-done.1.refs_6_), channel_id=1, source_target_pairs={{0,4},{1,5},{4,8},{5,9},{8,12},{9,13},{12,14},{13,15},{14,10},{15,... | collective-permute-start | bytes 442376 | tf_op jit(solution)/shard_map/ppermute | solution.py:376
  14.8 5.1 %collective-permute-start.10 = (bf16[144,512]{1,0:T(8,128)(2,1)S(1)}, bf16[144,512]{1,0:T(8,128)(2,1)S(1)}, u32[]{:S(2)}, u32[]{:S(2)}) collective-permute-start(bf16[144,512]{1,0:T(8,128)(2,1)S(1)} %pack.1.refs_0_), channel_id=1, source_target_pairs={{0,1},{1,0},{2,3},{3,2},{4,5},{5,4},{6,7},{7,6},{8,9},{9,8},{10,11... | collective-permute-start | bytes 442376 | tf_op jit(solution)/shard_map/ppermute | solution.py:379
  14.8 5.1 %collective-permute-start.11 = (bf16[144,512]{1,0:T(8,128)(2,1)S(1)}, bf16[144,512]{1,0:T(8,128)(2,1)S(1)}, u32[]{:S(2)}, u32[]{:S(2)}) collective-permute-start(bf16[144,512]{1,0:T(8,128)(2,1)S(1)} %collective-permute-done.refs_2_), channel_id=1, source_target_pairs={{0,1},{1,0},{2,3},{3,2},{4,5},{5,4},{6,7},{7,6},{8,9},{9,8},{10,11... | collective-permute-start | bytes 442376 | tf_op jit(solution)/shard_map/ppermute | solution.py:379
  15.3 5.2 %collective-permute-start.13 = (bf16[144,512]{1,0:T(8,128)(2,1)S(1)}, bf16[144,512]{1,0:T(8,128)(2,1)S(1)}, u32[]{:S(2)}, u32[]{:S(2)}) collective-permute-start(bf16[144,512]{1,0:T(8,128)(2,1)S(1)} %collective-permute-done.12.refs_4_), channel_id=1, source_target_pairs={{0,1},{1,0},{2,3},{3,2},{4,5},{5,4},{6,7},{7,6},{8,9},{9,8},{10,11... | collective-permute-start | bytes 442376 | tf_op jit(solution)/shard_map/ppermute | solution.py:379
  19.9 6.2 %collective-permute-start.16 = (bf16[144,512]{1,0:T(8,128)(2,1)S(1)}, bf16[144,512]{1,0:T(8,128)(2,1)S(1)}, u32[]{:S(2)}, u32[]{:S(2)}) collective-permute-start(bf16[144,512]{1,0:T(8,128)(2,1)S(1)} %collective-permute-done.15.refs_8_), channel_id=1, source_target_pairs={{0,1},{1,0},{2,3},{3,2},{4,5},{5,4},{6,7},{7,6},{8,9},{9,8},{10,11... | collective-permute-start | bytes 442376 | tf_op jit(solution)/shard_map/ppermute | solution.py:379
  20.4 6.9 %collective-permute-start.17 = (bf16[144,512]{1,0:T(8,128)(2,1)S(1)}, bf16[144,512]{1,0:T(8,128)(2,1)S(1)}, u32[]{:S(2)}, u32[]{:S(2)}) collective-permute-start(bf16[144,512]{1,0:T(8,128)(2,1)S(1)} %collective-permute-done.2.refs_10_), channel_id=1, source_target_pairs={{0,1},{1,0},{2,3},{3,2},{4,5},{5,4},{6,7},{7,6},{8,9},{9,8},{10,11... | collective-permute-start | bytes 442376 | tf_op jit(solution)/shard_map/ppermute | solution.py:379
  22.5 6.4 %collective-permute-start.19 = (bf16[144,512]{1,0:T(8,128)(2,1)S(1)}, bf16[144,512]{1,0:T(8,128)(2,1)S(1)}, u32[]{:S(2)}, u32[]{:S(2)}) collective-permute-start(bf16[144,512]{1,0:T(8,128)(2,1)S(1)} %collective-permute-done.18.refs_12_), channel_id=1, source_target_pairs={{0,1},{1,0},{2,3},{3,2},{4,5},{5,4},{6,7},{7,6},{8,9},{9,8},{10,11... | collective-permute-start | bytes 442376 | tf_op jit(solution)/shard_map/ppermute | solution.py:379
  23.3 5.9 %collective-permute-start.21 = (bf16[144,512]{1,0:T(8,128)(2,1)S(1)}, bf16[144,512]{1,0:T(8,128)(2,1)S(1)}, u32[]{:S(2)}, u32[]{:S(2)}) collective-permute-start(bf16[144,512]{1,0:T(8,128)(2,1)S(1)} %collective-permute-done.20.refs_14_), channel_id=1, source_target_pairs={{0,1},{1,0},{2,3},{3,2},{4,5},{5,4},{6,7},{7,6},{8,9},{9,8},{10,11... | collective-permute-start | bytes 442376 | tf_op jit(solution)/shard_map/ppermute | solution.py:379
  23.3 14.8 %collective-permute-start.3 = (bf16[2,256,128]{2,1,0:T(8,128)(2,1)S(1)}, bf16[2,256,128]{2,1,0:T(8,128)(2,1)S(1)}, u32[]{:S(2)}, u32[]{:S(2)}) collective-permute-start(bf16[2,256,128]{2,1,0:T(8,128)(2,1)S(1)} %get-tuple-element.130), channel_id=1, source_target_pairs={{0,8},{1,9},{2,10},{3,11},{4,12},{5,13},{6,14},{7,15},{8,0},{9,1},... | collective-permute-start | bytes 393224 | tf_op jit(solution)/shard_map/ppermute | solution.py:379
  26.1 13.7 %collective-permute-start.4 = (bf16[2,256,128]{2,1,0:T(8,128)(2,1)S(1)}, bf16[2,256,128]{2,1,0:T(8,128)(2,1)S(1)}, u32[]{:S(2)}, u32[]{:S(2)}) collective-permute-start(bf16[2,256,128]{2,1,0:T(8,128)(2,1)S(1)} %get-tuple-element.131), channel_id=1, source_target_pairs={{0,10},{1,11},{2,8},{3,9},{4,14},{5,15},{6,12},{7,13},{8,2},{9,3},... | collective-permute-start | bytes 393224 | tf_op jit(solution)/shard_map/ppermute | solution.py:379
  27.4 12.4 %collective-permute-start.5 = (bf16[2,256,128]{2,1,0:T(8,128)(2,1)S(1)}, bf16[2,256,128]{2,1,0:T(8,128)(2,1)S(1)}, u32[]{:S(2)}, u32[]{:S(2)}) collective-permute-start(bf16[2,256,128]{2,1,0:T(8,128)(2,1)S(1)} %get-tuple-element.129), channel_id=1, source_target_pairs={{0,6},{1,7},{2,4},{3,5},{4,2},{5,3},{6,0},{7,1},{8,14},{9,15},{10,... | collective-permute-start | bytes 393224 | tf_op jit(solution)/shard_map/ppermute | solution.py:379
  28.9 11.1 %collective-permute-start.6 = (bf16[2,256,128]{2,1,0:T(8,128)(2,1)S(1)}, bf16[2,256,128]{2,1,0:T(8,128)(2,1)S(1)}, u32[]{:S(2)}, u32[]{:S(2)}) collective-permute-start(bf16[2,256,128]{2,1,0:T(8,128)(2,1)S(1)} %get-tuple-element.128), channel_id=1, source_target_pairs={{0,4},{1,5},{2,6},{3,7},{4,0},{5,1},{6,2},{7,3},{8,12},{9,13},{10,... | collective-permute-start | bytes 393224 | tf_op jit(solution)/shard_map/ppermute | solution.py:379
  29.1 10.9 %collective-permute-start.7 = (bf16[2,256,128]{2,1,0:T(8,128)(2,1)S(1)}, bf16[2,256,128]{2,1,0:T(8,128)(2,1)S(1)}, u32[]{:S(2)}, u32[]{:S(2)}) collective-permute-start(bf16[2,256,128]{2,1,0:T(8,128)(2,1)S(1)} %get-tuple-element.127), channel_id=1, source_target_pairs={{0,2},{1,3},{2,0},{3,1},{4,6},{5,7},{6,4},{7,5},{8,10},{9,11},{10,... | collective-permute-start | bytes 393224 | tf_op jit(solution)/shard_map/ppermute | solution.py:379
  41.0 21.3 %collective-permute-start.27 = (bf16[6,512,512]{2,1,0:T(8,128)(2,1)S(1)}, bf16[6,512,512]{2,1,0:T(8,128)(2,1)S(1)}, u32[]{:S(2)}, u32[]{:S(2)}) collective-permute-start(bf16[6,512,512]{2,1,0:T(8,128)(2,1)S(1)} %get-tuple-element.186), channel_id=1, source_target_pairs={{0,1},{1,0},{2,3},{3,2},{4,5},{5,4},{6,7},{7,6},{8,9},{9,8},{10,11... | collective-permute-start | bytes 9437192 | tf_op jit(solution)/shard_map/ppermute | solution.py:379
  41.2 16.8 %collective-permute-start.26 = (bf16[2,512,512]{2,1,0:T(8,128)(2,1)S(1)}, bf16[2,512,512]{2,1,0:T(8,128)(2,1)S(1)}, u32[]{:S(2)}, u32[]{:S(2)}) collective-permute-start(bf16[2,512,512]{2,1,0:T(8,128)(2,1)S(1)} %get-tuple-element.183), channel_id=1, source_target_pairs={{0,1},{1,0},{2,3},{3,2},{4,5},{5,4},{6,7},{7,6},{8,9},{9,8},{10,11... | collective-permute-start | bytes 3145736 | tf_op jit(solution)/shard_map/ppermute | solution.py:379
  41.5 10.6 %collective-permute-start.8 = (bf16[2,256,128]{2,1,0:T(8,128)(2,1)S(1)}, bf16[2,256,128]{2,1,0:T(8,128)(2,1)S(1)}, u32[]{:S(2)}, u32[]{:S(2)}) collective-permute-start(bf16[2,256,128]{2,1,0:T(8,128)(2,1)S(1)} %get-tuple-element.134), channel_id=1, source_target_pairs={{0,14},{1,15},{2,12},{3,13},{4,10},{5,11},{6,8},{7,9},{8,6},{9,7},... | collective-permute-start | bytes 393224 | tf_op jit(solution)/shard_map/ppermute | solution.py:379
  46.1 7.1 %collective-permute-start.9 = (bf16[2,256,128]{2,1,0:T(8,128)(2,1)S(1)}, bf16[2,256,128]{2,1,0:T(8,128)(2,1)S(1)}, u32[]{:S(2)}, u32[]{:S(2)}) collective-permute-start(bf16[2,256,128]{2,1,0:T(8,128)(2,1)S(1)} %get-tuple-element.135), channel_id=1, source_target_pairs={{0,12},{1,13},{2,14},{3,15},{4,8},{5,9},{6,10},{7,11},{8,4},{9,5},... | collective-permute-start | bytes 393224 | tf_op jit(solution)/shard_map/ppermute | solution.py:379
  59.2 6.1 %collective-permute-start.28 = (bf16[128,512]{1,0:T(8,128)(2,1)S(1)}, bf16[128,512]{1,0:T(8,128)(2,1)S(1)}, u32[]{:S(2)}, u32[]{:S(2)}) collective-permute-start(bf16[128,512]{1,0:T(8,128)(2,1)S(1)} %get-tuple-element.188), channel_id=1, source_target_pairs={{0,4},{1,5},{4,8},{5,9},{8,12},{9,13},{12,14},{13,15},{14,10},{15,... | collective-permute-start | bytes 393224 | tf_op jit(solution)/shard_map/ppermute | solution.py:376
  62.3 6.0 %collective-permute-start.32 = (bf16[128,512]{1,0:T(8,128)(2,1)S(1)}, bf16[128,512]{1,0:T(8,128)(2,1)S(1)}, u32[]{:S(2)}, u32[]{:S(2)}) collective-permute-start(bf16[128,512]{1,0:T(8,128)(2,1)S(1)} %get-tuple-element.192), channel_id=1, source_target_pairs={{0,2},{1,3},{4,0},{5,1},{8,4},{9,5},{12,8},{13,9},{14,12},{15,13},... | collective-permute-start | bytes 393224 | tf_op jit(solution)/shard_map/ppermute | solution.py:376
  65.3 5.4 %collective-permute-start.29 = (bf16[128,512]{1,0:T(8,128)(2,1)S(1)}, bf16[128,512]{1,0:T(8,128)(2,1)S(1)}, u32[]{:S(2)}, u32[]{:S(2)}) collective-permute-start(bf16[128,512]{1,0:T(8,128)(2,1)S(1)} %add_convert_fusion.5), channel_id=1, source_target_pairs={{0,4},{1,5},{4,8},{5,9},{8,12},{9,13},{12,14},{13,15},{14,10},{15,... | collective-permute-start | bytes 393224 | tf_op jit(solution)/shard_map/ppermute | solution.py:376
  (12 other events, 51.2 us)

commit v8 on v7

--- a/solution.py
+++ b/solution.py
@@ -13,7 +13,6 @@
 DH = 128
 EPS = 1e-05
 PAD = 16
-BLOCK = 512
 MIB = 1 << 20
 TRANS_B = (((1,), (1,)), ((), ()))
 
@@ -277,31 +276,31 @@
     )(*caches, *owns, mine, other)
 
 
-def finish_kernel(count, *refs):
+def finish_kernel(count, number, *refs):
     caches = refs[:count]
-    query_all, top_ref, total_ref, numerator_ref, state_ref, sum_ref, scores = refs[count:]
-    lines = query_all.shape[0]
-    for start in range(0, lines, BLOCK):
-        some = slice(start, start + BLOCK)
-        top, total, numerator = weigh(
-            query_all[some, :], caches, scores.at[some, :], top_ref[some, 0:1], total_ref[some, :], numerator_ref[some, :]
-        )
-        lane = lax.broadcasted_iota(jnp.int32, total.shape, 1)
-        state_ref[some, :] = jnp.where(lane < 64, top, jnp.sum(total, axis=1, keepdims=True))
-        sum_ref[some, :] = numerator
-
-
-def finish(caches, state):
+    query_all, top_ref, total_ref, numerator_ref, out_ref, scores = refs[count:]
+    lines = query_all.shape[0] // 2
+    some = slice(number * lines, (number + 1) * lines)
+    top, total, numerator = weigh(
+        query_all[some, :], caches, scores, top_ref[some, 0:1], total_ref[some, :], numerator_ref[some, :]
+    )
+    lane = lax.broadcasted_iota(jnp.int32, total.shape, 1)
+    out_ref[:, :DH] = numerator
+    out_ref[:, DH:] = jnp.where(lane < 64, top, jnp.sum(total, axis=1, keepdims=True))
+
+
+def finish(caches, state, number):
     count = len(caches)
-    lines = state[0].shape[0]
+    lines = state[0].shape[0] // 2
     positions = count * caches[0].shape[1]
     return pl.pallas_call(
-        functools.partial(finish_kernel, count),
-        out_shape=[jax.ShapeDtypeStruct((lines, 128), jnp.float32)] * 2,
+        functools.partial(finish_kernel, count, number),
+        out_shape=jax.ShapeDtypeStruct((lines, DH + 128), jnp.float32),
         in_specs=in_vmem(count + 4),
-        out_specs=in_vmem(2),
+        out_specs=in_vmem(1)[0],
         scratch_shapes=[pltpu.VMEM((lines, positions), jnp.float32)],
         compiler_params=params(24),
+        cost_estimate=cost(8 * lines * positions * DH, 8 * lines * positions),
         name="finish",
     )(*caches, *state)
 
@@ -313,19 +312,18 @@
 
 
 def merge_kernel(rows, *refs):
-    state, sums, far_state, far_sums, mine, other = refs[:6]
-    attention_ref, outs = refs[6], refs[7:]
-    lines = state.shape[0] // 2
-    heads = lines // rows
+    states, far_states = refs[:2], refs[2:4]
+    mine, other, attention_ref = refs[4:7]
+    outs = refs[7:]
+    heads = states[0].shape[0] // rows
     parts = []
     for number in range(2):
-        near_lines = slice(number * lines, (number + 1) * lines)
-        far_lines = slice((1 - number) * lines, (2 - number) * lines)
-        top, far_top = state[near_lines, 0:1], far_state[far_lines, 0:1]
+        state, far_state = states[number], far_states[1 - number]
+        top, far_top = state[:, DH : DH + 1], far_state[:, DH : DH + 1]
         peak = jnp.maximum(top, far_top)
         scale, far_scale = jnp.exp(top - peak), jnp.exp(far_top - peak)
-        denominator = state[near_lines, 64:65] * scale + far_state[far_lines, 64:65] * far_scale
-        numerator = sums[near_lines, :] * scale + far_sums[far_lines, :] * far_scale
+        denominator = state[:, DH + 64 : DH + 65] * scale + far_state[:, DH + 64 : DH + 65] * far_scale
+        numerator = state[:, :DH] * scale + far_state[:, :DH] * far_scale
         result = (numerator * (1.0 / denominator)).astype(jnp.bfloat16)
         for head in range(heads):
             attention_ref[number, :, head * DH : (head + 1) * DH] = result[head * rows : (head + 1) * rows, :]
@@ -334,7 +332,7 @@
         out[...] = output_term(parts, (mine[number], other[number])).astype(out.dtype)
 
 
-def merge(state, sums, far_state, far_sums, mine, other, rows):
+def merge(states, far_states, mine, other, rows):
     count, depth, width = mine.shape
     return pl.pallas_call(
         functools.partial(merge_kernel, rows),
@@ -344,7 +342,7 @@
         out_specs=in_vmem(1 + count),
         compiler_params=params(16),
         name="merge",
-    )(state, sums, far_state, far_sums, mine, other)
+    )(*states, *far_states, mine, other)
 
 
 def rest_kernel(attention, mine, other, *outs):
@@ -442,9 +440,10 @@
     w_out, state = lax.optimization_barrier((w_out, state))
     mine_first, mine_others = half(w_out, chips, (True, first), (True, others))
     state, mine_first, mine_others = lax.optimization_barrier((state, mine_first, mine_others))
-    state, sums = finish(far_parts, state)
-
-    attention, *terms = merge(state, sums, swap(state, 1), swap(sums, 1), mine_first, other_first, rows)
+    ends = [finish(far_parts, state, number) for number in range(2)]
+    swapped = [swap(end, 1) for end in ends]
+
+    attention, *terms = merge(ends, swapped, mine_first, other_first, rows)
     terms = dict(zip(first, terms))
     terms.update(zip(others, rest(attention, mine_others, other_others)))
     right = left = None

time: 82.1 us -> 81.9 us (level)
    ppermute x14, waiting for transfers between devices: 17.6 us -> 18.4 us  [around(): return lax.ppermute(value, 'seq', pairs)]
    pallas_call x1 -> x2, Pallas kernels: 1.96 us -> 2.16 us  [finish(): pl.pallas_call(functools.partial(finish_kernel, count, number), out_shape...]
where the time goes in v8:
time: 81.9 us; the launch traced here: 81.6 us
  starting transfers between devices  33.5 us (41%)
  waiting for transfers between devices  24 us (29%)
  Pallas kernels  23.1 us (28%)
  other arithmetic  0.84 us (1%)
    ppermute x14, starting transfers between devices, around(): return lax.ppermute(value, 'seq', pairs)  18.9 us
    ppermute x14, waiting for transfers between devices, around(): return lax.ppermute(value, 'seq', pairs)  18.4 us
    ppermute x21, starting transfers between devices, swap(): return lax.ppermute(value, 'seq', [(i, i ^ bits) for i in range(size)])  14.5 us
    ppermute x21, waiting for transfers between devices, swap(): return lax.ppermute(value, 'seq', [(i, i ^ bits) for i in range(size)])  5.56 us
    pallas_call x1, Pallas kernels, project(): pl.pallas_call(functools.partial(project_kernel, offsets, chips, rows), o...  4.92 us
    pallas_call x2, Pallas kernels, half(): pl.pallas_call(functools.partial(half_kernel, groups, chips, width), out_...  4.55 us
    pallas_call x2, Pallas kernels, fetch(): pl.pallas_call(functools.partial(fetch_kernel, start, size), out_shape=pl...  4.39 us
    pallas_call x1, Pallas kernels, begin(): pl.pallas_call(functools.partial(begin_kernel, count, len(owns), heads),...  3.62 us
  transfers between devices with their start and end apart: 35, of which 19 were waited for; matrix products, arithmetic and copies ran while one was open for 0% of the time, Pallas kernels for 27%

profile of v8, /device:TPU:0, one launch (start us, length us, event | category | flops | bytes accessed | tf_op | source)
XLA Modules:
  0.0 81.6 jit_solution(5701043089494616896)
XLA Ops:
  1.0 3.1 %collective-permute-start = (bf16[144,512]{1,0:T(8,128)(2,1)S(1)}, bf16[144,512]{1,0:T(8,128)(2,1)S(1)}, u32[]{:S(2)}, u32[]{:S(2)}) collective-permute-start(bf16[144,512]{1,0:T(8,128)(2,1)S(1)} %pack.1.refs_0_), channel_id=1, source_target_pairs={{0,4},{1,5},{4,8},{5,9},{8,12},{9,13},{12,14},{13,15},{14,10},{15,... | collective-permute-start | bytes 442376 | tf_op jit(solution)/shard_map/ppermute | solution.py:374
  4.0 2.2 %fetch.2.refs_16_ = bf16[256,8192]{1,0:T(8,128)(2,1)S(1)} custom-call(bf16[512,8192]{1,0:T(8,128)(2,1)} %source.1), custom_call_target="tpu_custom_call" | custom-call | bytes 8388608 | tf_op jit(solution)/shard_map/fetch/pallas_call | solution.py:139
  7.8 1.8 %collective-permute-start.1 = (bf16[144,512]{1,0:T(8,128)(2,1)S(1)}, bf16[144,512]{1,0:T(8,128)(2,1)S(1)}, u32[]{:S(2)}, u32[]{:S(2)}) collective-permute-start(bf16[144,512]{1,0:T(8,128)(2,1)S(1)} %collective-permute-done.refs_2_), channel_id=1, source_target_pairs={{0,4},{1,5},{4,8},{5,9},{8,12},{9,13},{12,14},{13,15},{14,10},{15,... | collective-permute-start | bytes 442376 | tf_op jit(solution)/shard_map/ppermute | solution.py:374
  9.9 2.2 %fetch.3.refs_17_ = bf16[256,8192]{1,0:T(8,128)(2,1)S(1)} custom-call(bf16[512,8192]{1,0:T(8,128)(2,1)} %source.1), custom_call_target="tpu_custom_call" | custom-call | bytes 8388608 | tf_op jit(solution)/shard_map/fetch/pallas_call | solution.py:139
  13.0 1.8 %collective-permute-start.2 = (bf16[144,512]{1,0:T(8,128)(2,1)S(1)}, bf16[144,512]{1,0:T(8,128)(2,1)S(1)}, u32[]{:S(2)}, u32[]{:S(2)}) collective-permute-start(bf16[144,512]{1,0:T(8,128)(2,1)S(1)} %collective-permute-done.1.refs_6_), channel_id=1, source_target_pairs={{0,4},{1,5},{4,8},{5,9},{8,12},{9,13},{12,14},{13,15},{14,10},{15,... | collective-permute-start | bytes 442376 | tf_op jit(solution)/shard_map/ppermute | solution.py:374
  15.3 2.0 %collective-permute-done.15.refs_8_ = bf16[144,512]{1,0:T(8,128)(2,1)S(1)} collective-permute-done((bf16[144,512]{1,0:T(8,128)(2,1)S(1)}, bf16[144,512]{1,0:T(8,128)(2,1)S(1)}, u32[]{:S(2)}, u32[]{:S(2)}) %collective-permute-start.15) | collective-permute-done | bytes 147488 | tf_op jit(solution)/shard_map/ppermute | solution.py:374
  18.1 1.8 %collective-permute-start.20 = (bf16[144,512]{1,0:T(8,128)(2,1)S(1)}, bf16[144,512]{1,0:T(8,128)(2,1)S(1)}, u32[]{:S(2)}, u32[]{:S(2)}) collective-permute-start(bf16[144,512]{1,0:T(8,128)(2,1)S(1)} %collective-permute-done.2.refs_10_), channel_id=1, source_target_pairs={{0,4},{1,5},{4,8},{5,9},{8,12},{9,13},{12,14},{13,15},{14,10},{15,... | collective-permute-start | bytes 442376 | tf_op jit(solution)/shard_map/ppermute | solution.py:374
  20.5 2.0 %collective-permute-done.18.refs_12_ = bf16[144,512]{1,0:T(8,128)(2,1)S(1)} collective-permute-done((bf16[144,512]{1,0:T(8,128)(2,1)S(1)}, bf16[144,512]{1,0:T(8,128)(2,1)S(1)}, u32[]{:S(2)}, u32[]{:S(2)}) %collective-permute-start.18) | collective-permute-done | bytes 147488 | tf_op jit(solution)/shard_map/ppermute | solution.py:374
  23.3 2.8 %collective-permute-start.3 = (bf16[2,256,128]{2,1,0:T(8,128)(2,1)S(1)}, bf16[2,256,128]{2,1,0:T(8,128)(2,1)S(1)}, u32[]{:S(2)}, u32[]{:S(2)}) collective-permute-start(bf16[2,256,128]{2,1,0:T(8,128)(2,1)S(1)} %get-tuple-element.128), channel_id=1, source_target_pairs={{0,8},{1,9},{2,10},{3,11},{4,12},{5,13},{6,14},{7,15},{8,0},{9,1},... | collective-permute-start | bytes 393224 | tf_op jit(solution)/shard_map/ppermute | solution.py:377
  29.1 1.7 %collective-permute-start.7 = (bf16[2,256,128]{2,1,0:T(8,128)(2,1)S(1)}, bf16[2,256,128]{2,1,0:T(8,128)(2,1)S(1)}, u32[]{:S(2)}, u32[]{:S(2)}) collective-permute-start(bf16[2,256,128]{2,1,0:T(8,128)(2,1)S(1)} %get-tuple-element.125), channel_id=1, source_target_pairs={{0,2},{1,3},{2,0},{3,1},{4,6},{5,7},{6,4},{7,5},{8,10},{9,11},{10,... | collective-permute-start | bytes 393224 | tf_op jit(solution)/shard_map/ppermute | solution.py:377
  30.9 4.9 %project.1 = (bf16[128,512]{1,0:T(8,128)(2,1)S(1)}, bf16[128,128]{1,0:T(8,128)(2,1)S(1)}) custom-call(bf16[144,512]{1,0:T(8,128)(2,1)S(1)} %pack.1.refs_0_, bf16[144,512]{1,0:T(8,128)(2,1)S(1)} %collective-permute-done.10.refs_1_, bf16[144,512]{1,0:T(8,128)(2,1)S(1)} %collective-permute-done.refs_2_, bf16[144,512]{1,0:T(8,128)(2,1)S(1)} %collective-permute-done.11.refs_3_, ...), custom_call_target="tpu_custom_call" | custom-call | tf_op jit(solution)/shard_map/project/pallas_call | solution.py:192
  35.8 2.3 %half.2 = (bf16[2,512,512]{2,1,0:T(8,128)(2,1)S(1)}, bf16[6,512,512]{2,1,0:T(8,128)(2,1)S(1)}) custom-call(bf16[512,8192]{1,0:T(8,128)(2,1)} %w_out.1), custom_call_target="tpu_custom_call" | custom-call | tf_op jit(solution)/shard_map/half/pallas_call | solution.py:121
  38.2 1.6 %collective-permute-done.4.refs_2_ = bf16[2,256,128]{2,1,0:T(8,128)(2,1)S(1)} collective-permute-done((bf16[2,256,128]{2,1,0:T(8,128)(2,1)S(1)}, bf16[2,256,128]{2,1,0:T(8,128)(2,1)S(1)}, u32[]{:S(2)}, u32[]{:S(2)}) %collective-permute-start.4) | collective-permute-done | bytes 131104 | tf_op jit(solution)/shard_map/ppermute | solution.py:377
  41.5 4.6 %collective-permute-start.8 = (bf16[2,256,128]{2,1,0:T(8,128)(2,1)S(1)}, bf16[2,256,128]{2,1,0:T(8,128)(2,1)S(1)}, u32[]{:S(2)}, u32[]{:S(2)}) collective-permute-start(bf16[2,256,128]{2,1,0:T(8,128)(2,1)S(1)} %get-tuple-element.132), channel_id=1, source_target_pairs={{0,14},{1,15},{2,12},{3,13},{4,10},{5,11},{6,8},{7,9},{8,6},{9,7},... | collective-permute-start | bytes 393224 | tf_op jit(solution)/shard_map/ppermute | solution.py:377
  46.1 3.6 %begin.1 = (bf16[1024,128]{1,0:T(8,128)(2,1)S(1)}, f32[1024,128]{1,0:T(8,128)S(1)}, f32[1024,128]{1,0:T(8,128)S(1)}, f32[1024,128]{1,0:T(8,128)S(1)}) custom-call(bf16[2,256,128]{2,1,0:T(8,128)(2,1)S(1)} %get-tuple-element.142.refs_0_, bf16[2,256,128]{2,1,0:T(8,128)(2,1)S(1)} %collective-permute-done.3.refs_1_, ...), custom_call_target="tpu_custom_call" | custom-call | flops 1 | bytes 1 | tf_op jit(solution)/shard_map/begin/pallas_call | solution.py:266
  49.8 2.3 %half.3 = (bf16[2,512,512]{2,1,0:T(8,128)(2,1)S(1)}, bf16[6,512,512]{2,1,0:T(8,128)(2,1)S(1)}) custom-call(bf16[512,8192]{1,0:T(8,128)(2,1)} %w_out.1), custom_call_target="tpu_custom_call" | custom-call | tf_op jit(solution)/shard_map/half/pallas_call | solution.py:121
  58.9 3.0 %collective-permute-start.28 = (bf16[128,512]{1,0:T(8,128)(2,1)S(1)}, bf16[128,512]{1,0:T(8,128)(2,1)S(1)}, u32[]{:S(2)}, u32[]{:S(2)}) collective-permute-start(bf16[128,512]{1,0:T(8,128)(2,1)S(1)} %get-tuple-element.184), channel_id=1, source_target_pairs={{0,4},{1,5},{4,8},{5,9},{8,12},{9,13},{12,14},{13,15},{14,10},{15,... | collective-permute-start | bytes 393224 | tf_op jit(solution)/shard_map/ppermute | solution.py:374
  62.9 2.3 %collective-permute-done.28 = bf16[128,512]{1,0:T(8,128)(2,1)S(1)} collective-permute-done((bf16[128,512]{1,0:T(8,128)(2,1)S(1)}, bf16[128,512]{1,0:T(8,128)(2,1)S(1)}, u32[]{:S(2)}, u32[]{:S(2)}) %collective-permute-start.28) | collective-permute-done | bytes 131104 | tf_op jit(solution)/shard_map/ppermute | solution.py:374
  65.2 2.5 %collective-permute-start.29 = (bf16[128,512]{1,0:T(8,128)(2,1)S(1)}, bf16[128,512]{1,0:T(8,128)(2,1)S(1)}, u32[]{:S(2)}, u32[]{:S(2)}) collective-permute-start(bf16[128,512]{1,0:T(8,128)(2,1)S(1)} %add_convert_fusion.5), channel_id=1, source_target_pairs={{0,4},{1,5},{4,8},{5,9},{8,12},{9,13},{12,14},{13,15},{14,10},{15,... | collective-permute-start | bytes 393224 | tf_op jit(solution)/shard_map/ppermute | solution.py:374
  68.2 2.5 %collective-permute-done.29 = bf16[128,512]{1,0:T(8,128)(2,1)S(1)} collective-permute-done((bf16[128,512]{1,0:T(8,128)(2,1)S(1)}, bf16[128,512]{1,0:T(8,128)(2,1)S(1)}, u32[]{:S(2)}, u32[]{:S(2)}) %collective-permute-start.29) | collective-permute-done | bytes 131104 | tf_op jit(solution)/shard_map/ppermute | solution.py:374
  70.8 2.0 %collective-permute-start.30 = (bf16[128,512]{1,0:T(8,128)(2,1)S(1)}, bf16[128,512]{1,0:T(8,128)(2,1)S(1)}, u32[]{:S(2)}, u32[]{:S(2)}) collective-permute-start(bf16[128,512]{1,0:T(8,128)(2,1)S(1)} %add_convert_fusion.4), channel_id=1, source_target_pairs={{0,4},{1,5},{4,8},{5,9},{8,12},{9,13},{12,14},{13,15},{14,10},{15,... | collective-permute-start | bytes 393224 | tf_op jit(solution)/shard_map/ppermute | solution.py:374
  73.6 2.3 %collective-permute-done.30 = bf16[128,512]{1,0:T(8,128)(2,1)S(1)} collective-permute-done((bf16[128,512]{1,0:T(8,128)(2,1)S(1)}, bf16[128,512]{1,0:T(8,128)(2,1)S(1)}, u32[]{:S(2)}, u32[]{:S(2)}) %collective-permute-start.30) | collective-permute-done | bytes 131104 | tf_op jit(solution)/shard_map/ppermute | solution.py:374
  75.9 2.0 %collective-permute-start.31 = (bf16[128,512]{1,0:T(8,128)(2,1)S(1)}, bf16[128,512]{1,0:T(8,128)(2,1)S(1)}, u32[]{:S(2)}, u32[]{:S(2)}) collective-permute-start(bf16[128,512]{1,0:T(8,128)(2,1)S(1)} %add_convert_fusion.3), channel_id=1, source_target_pairs={{0,4},{1,5},{4,8},{5,9},{8,12},{9,13},{12,14},{13,15},{14,10},{15,... | collective-permute-start | bytes 393224 | tf_op jit(solution)/shard_map/ppermute | solution.py:374
  78.3 2.6 %collective-permute-done.31 = bf16[128,512]{1,0:T(8,128)(2,1)S(1)} collective-permute-done((bf16[128,512]{1,0:T(8,128)(2,1)S(1)}, bf16[128,512]{1,0:T(8,128)(2,1)S(1)}, u32[]{:S(2)}, u32[]{:S(2)}) %collective-permute-start.31) | collective-permute-done | bytes 131104 | tf_op jit(solution)/shard_map/ppermute | solution.py:374
  (66 shorter events, 21.4 us)
Async XLA Ops:
  1.0 6.9 %collective-permute-start = (bf16[144,512]{1,0:T(8,128)(2,1)S(1)}, bf16[144,512]{1,0:T(8,128)(2,1)S(1)}, u32[]{:S(2)}, u32[]{:S(2)}) collective-permute-start(bf16[144,512]{1,0:T(8,128)(2,1)S(1)} %pack.1.refs_0_), channel_id=1, source_target_pairs={{0,4},{1,5},{4,8},{5,9},{8,12},{9,13},{12,14},{13,15},{14,10},{15,... | collective-permute-start | bytes 442376 | tf_op jit(solution)/shard_map/ppermute | solution.py:374
  4.0 8.1 %collective-permute-start.12 = (bf16[144,512]{1,0:T(8,128)(2,1)S(1)}, bf16[144,512]{1,0:T(8,128)(2,1)S(1)}, u32[]{:S(2)}, u32[]{:S(2)}) collective-permute-start(bf16[144,512]{1,0:T(8,128)(2,1)S(1)} %pack.1.refs_0_), channel_id=1, source_target_pairs={{0,2},{1,3},{4,0},{5,1},{8,4},{9,5},{12,8},{13,9},{14,12},{15,13},... | collective-permute-start | bytes 442376 | tf_op jit(solution)/shard_map/ppermute | solution.py:374
  12.1 5.2 %collective-permute-start.15 = (bf16[144,512]{1,0:T(8,128)(2,1)S(1)}, bf16[144,512]{1,0:T(8,128)(2,1)S(1)}, u32[]{:S(2)}, u32[]{:S(2)}) collective-permute-start(bf16[144,512]{1,0:T(8,128)(2,1)S(1)} %collective-permute-done.12.refs_4_), channel_id=1, source_target_pairs={{0,2},{1,3},{4,0},{5,1},{8,4},{9,5},{12,8},{13,9},{14,12},{15,13},... | collective-permute-start | bytes 442376 | tf_op jit(solution)/shard_map/ppermute | solution.py:374
  13.0 5.1 %collective-permute-start.2 = (bf16[144,512]{1,0:T(8,128)(2,1)S(1)}, bf16[144,512]{1,0:T(8,128)(2,1)S(1)}, u32[]{:S(2)}, u32[]{:S(2)}) collective-permute-start(bf16[144,512]{1,0:T(8,128)(2,1)S(1)} %collective-permute-done.1.refs_6_), channel_id=1, source_target_pairs={{0,4},{1,5},{4,8},{5,9},{8,12},{9,13},{12,14},{13,15},{14,10},{15,... | collective-permute-start | bytes 442376 | tf_op jit(solution)/shard_map/ppermute | solution.py:374
  14.8 5.1 %collective-permute-start.10 = (bf16[144,512]{1,0:T(8,128)(2,1)S(1)}, bf16[144,512]{1,0:T(8,128)(2,1)S(1)}, u32[]{:S(2)}, u32[]{:S(2)}) collective-permute-start(bf16[144,512]{1,0:T(8,128)(2,1)S(1)} %pack.1.refs_0_), channel_id=1, source_target_pairs={{0,1},{1,0},{2,3},{3,2},{4,5},{5,4},{6,7},{7,6},{8,9},{9,8},{10,11... | collective-permute-start | bytes 442376 | tf_op jit(solution)/shard_map/ppermute | solution.py:377
  14.8 5.1 %collective-permute-start.11 = (bf16[144,512]{1,0:T(8,128)(2,1)S(1)}, bf16[144,512]{1,0:T(8,128)(2,1)S(1)}, u32[]{:S(2)}, u32[]{:S(2)}) collective-permute-start(bf16[144,512]{1,0:T(8,128)(2,1)S(1)} %collective-permute-done.refs_2_), channel_id=1, source_target_pairs={{0,1},{1,0},{2,3},{3,2},{4,5},{5,4},{6,7},{7,6},{8,9},{9,8},{10,11... | collective-permute-start | bytes 442376 | tf_op jit(solution)/shard_map/ppermute | solution.py:377
  15.3 5.2 %collective-permute-start.13 = (bf16[144,512]{1,0:T(8,128)(2,1)S(1)}, bf16[144,512]{1,0:T(8,128)(2,1)S(1)}, u32[]{:S(2)}, u32[]{:S(2)}) collective-permute-start(bf16[144,512]{1,0:T(8,128)(2,1)S(1)} %collective-permute-done.12.refs_4_), channel_id=1, source_target_pairs={{0,1},{1,0},{2,3},{3,2},{4,5},{5,4},{6,7},{7,6},{8,9},{9,8},{10,11... | collective-permute-start | bytes 442376 | tf_op jit(solution)/shard_map/ppermute | solution.py:377
  18.1 5.1 %collective-permute-start.20 = (bf16[144,512]{1,0:T(8,128)(2,1)S(1)}, bf16[144,512]{1,0:T(8,128)(2,1)S(1)}, u32[]{:S(2)}, u32[]{:S(2)}) collective-permute-start(bf16[144,512]{1,0:T(8,128)(2,1)S(1)} %collective-permute-done.2.refs_10_), channel_id=1, source_target_pairs={{0,4},{1,5},{4,8},{5,9},{8,12},{9,13},{12,14},{13,15},{14,10},{15,... | collective-permute-start | bytes 442376 | tf_op jit(solution)/shard_map/ppermute | solution.py:374
  19.9 6.2 %collective-permute-start.16 = (bf16[144,512]{1,0:T(8,128)(2,1)S(1)}, bf16[144,512]{1,0:T(8,128)(2,1)S(1)}, u32[]{:S(2)}, u32[]{:S(2)}) collective-permute-start(bf16[144,512]{1,0:T(8,128)(2,1)S(1)} %collective-permute-done.15.refs_8_), channel_id=1, source_target_pairs={{0,1},{1,0},{2,3},{3,2},{4,5},{5,4},{6,7},{7,6},{8,9},{9,8},{10,11... | collective-permute-start | bytes 442376 | tf_op jit(solution)/shard_map/ppermute | solution.py:377
  20.4 6.9 %collective-permute-start.17 = (bf16[144,512]{1,0:T(8,128)(2,1)S(1)}, bf16[144,512]{1,0:T(8,128)(2,1)S(1)}, u32[]{:S(2)}, u32[]{:S(2)}) collective-permute-start(bf16[144,512]{1,0:T(8,128)(2,1)S(1)} %collective-permute-done.2.refs_10_), channel_id=1, source_target_pairs={{0,1},{1,0},{2,3},{3,2},{4,5},{5,4},{6,7},{7,6},{8,9},{9,8},{10,11... | collective-permute-start | bytes 442376 | tf_op jit(solution)/shard_map/ppermute | solution.py:377
  22.5 6.4 %collective-permute-start.19 = (bf16[144,512]{1,0:T(8,128)(2,1)S(1)}, bf16[144,512]{1,0:T(8,128)(2,1)S(1)}, u32[]{:S(2)}, u32[]{:S(2)}) collective-permute-start(bf16[144,512]{1,0:T(8,128)(2,1)S(1)} %collective-permute-done.18.refs_12_), channel_id=1, source_target_pairs={{0,1},{1,0},{2,3},{3,2},{4,5},{5,4},{6,7},{7,6},{8,9},{9,8},{10,11... | collective-permute-start | bytes 442376 | tf_op jit(solution)/shard_map/ppermute | solution.py:377
  23.3 5.9 %collective-permute-start.21 = (bf16[144,512]{1,0:T(8,128)(2,1)S(1)}, bf16[144,512]{1,0:T(8,128)(2,1)S(1)}, u32[]{:S(2)}, u32[]{:S(2)}) collective-permute-start(bf16[144,512]{1,0:T(8,128)(2,1)S(1)} %collective-permute-done.20.refs_14_), channel_id=1, source_target_pairs={{0,1},{1,0},{2,3},{3,2},{4,5},{5,4},{6,7},{7,6},{8,9},{9,8},{10,11... | collective-permute-start | bytes 442376 | tf_op jit(solution)/shard_map/ppermute | solution.py:377
  23.3 14.8 %collective-permute-start.3 = (bf16[2,256,128]{2,1,0:T(8,128)(2,1)S(1)}, bf16[2,256,128]{2,1,0:T(8,128)(2,1)S(1)}, u32[]{:S(2)}, u32[]{:S(2)}) collective-permute-start(bf16[2,256,128]{2,1,0:T(8,128)(2,1)S(1)} %get-tuple-element.128), channel_id=1, source_target_pairs={{0,8},{1,9},{2,10},{3,11},{4,12},{5,13},{6,14},{7,15},{8,0},{9,1},... | collective-permute-start | bytes 393224 | tf_op jit(solution)/shard_map/ppermute | solution.py:377
  26.1 13.7 %collective-permute-start.4 = (bf16[2,256,128]{2,1,0:T(8,128)(2,1)S(1)}, bf16[2,256,128]{2,1,0:T(8,128)(2,1)S(1)}, u32[]{:S(2)}, u32[]{:S(2)}) collective-permute-start(bf16[2,256,128]{2,1,0:T(8,128)(2,1)S(1)} %get-tuple-element.129), channel_id=1, source_target_pairs={{0,10},{1,11},{2,8},{3,9},{4,14},{5,15},{6,12},{7,13},{8,2},{9,3},... | collective-permute-start | bytes 393224 | tf_op jit(solution)/shard_map/ppermute | solution.py:377
  27.4 12.4 %collective-permute-start.5 = (bf16[2,256,128]{2,1,0:T(8,128)(2,1)S(1)}, bf16[2,256,128]{2,1,0:T(8,128)(2,1)S(1)}, u32[]{:S(2)}, u32[]{:S(2)}) collective-permute-start(bf16[2,256,128]{2,1,0:T(8,128)(2,1)S(1)} %get-tuple-element.127), channel_id=1, source_target_pairs={{0,6},{1,7},{2,4},{3,5},{4,2},{5,3},{6,0},{7,1},{8,14},{9,15},{10,... | collective-permute-start | bytes 393224 | tf_op jit(solution)/shard_map/ppermute | solution.py:377
  28.9 11.1 %collective-permute-start.6 = (bf16[2,256,128]{2,1,0:T(8,128)(2,1)S(1)}, bf16[2,256,128]{2,1,0:T(8,128)(2,1)S(1)}, u32[]{:S(2)}, u32[]{:S(2)}) collective-permute-start(bf16[2,256,128]{2,1,0:T(8,128)(2,1)S(1)} %get-tuple-element.126), channel_id=1, source_target_pairs={{0,4},{1,5},{2,6},{3,7},{4,0},{5,1},{6,2},{7,3},{8,12},{9,13},{10,... | collective-permute-start | bytes 393224 | tf_op jit(solution)/shard_map/ppermute | solution.py:377
  29.1 10.9 %collective-permute-start.7 = (bf16[2,256,128]{2,1,0:T(8,128)(2,1)S(1)}, bf16[2,256,128]{2,1,0:T(8,128)(2,1)S(1)}, u32[]{:S(2)}, u32[]{:S(2)}) collective-permute-start(bf16[2,256,128]{2,1,0:T(8,128)(2,1)S(1)} %get-tuple-element.125), channel_id=1, source_target_pairs={{0,2},{1,3},{2,0},{3,1},{4,6},{5,7},{6,4},{7,5},{8,10},{9,11},{10,... | collective-permute-start | bytes 393224 | tf_op jit(solution)/shard_map/ppermute | solution.py:377
  41.0 20.9 %collective-permute-start.27 = (bf16[6,512,512]{2,1,0:T(8,128)(2,1)S(1)}, bf16[6,512,512]{2,1,0:T(8,128)(2,1)S(1)}, u32[]{:S(2)}, u32[]{:S(2)}) collective-permute-start(bf16[6,512,512]{2,1,0:T(8,128)(2,1)S(1)} %get-tuple-element.182), channel_id=1, source_target_pairs={{0,1},{1,0},{2,3},{3,2},{4,5},{5,4},{6,7},{7,6},{8,9},{9,8},{10,11... | collective-permute-start | bytes 9437192 | tf_op jit(solution)/shard_map/ppermute | solution.py:377
  41.2 16.4 %collective-permute-start.26 = (bf16[2,512,512]{2,1,0:T(8,128)(2,1)S(1)}, bf16[2,512,512]{2,1,0:T(8,128)(2,1)S(1)}, u32[]{:S(2)}, u32[]{:S(2)}) collective-permute-start(bf16[2,512,512]{2,1,0:T(8,128)(2,1)S(1)} %get-tuple-element.179), channel_id=1, source_target_pairs={{0,1},{1,0},{2,3},{3,2},{4,5},{5,4},{6,7},{7,6},{8,9},{9,8},{10,11... | collective-permute-start | bytes 3145736 | tf_op jit(solution)/shard_map/ppermute | solution.py:377
  41.5 10.6 %collective-permute-start.8 = (bf16[2,256,128]{2,1,0:T(8,128)(2,1)S(1)}, bf16[2,256,128]{2,1,0:T(8,128)(2,1)S(1)}, u32[]{:S(2)}, u32[]{:S(2)}) collective-permute-start(bf16[2,256,128]{2,1,0:T(8,128)(2,1)S(1)} %get-tuple-element.132), channel_id=1, source_target_pairs={{0,14},{1,15},{2,12},{3,13},{4,10},{5,11},{6,8},{7,9},{8,6},{9,7},... | collective-permute-start | bytes 393224 | tf_op jit(solution)/shard_map/ppermute | solution.py:377
  46.1 7.1 %collective-permute-start.9 = (bf16[2,256,128]{2,1,0:T(8,128)(2,1)S(1)}, bf16[2,256,128]{2,1,0:T(8,128)(2,1)S(1)}, u32[]{:S(2)}, u32[]{:S(2)}) collective-permute-start(bf16[2,256,128]{2,1,0:T(8,128)(2,1)S(1)} %get-tuple-element.133), channel_id=1, source_target_pairs={{0,12},{1,13},{2,14},{3,15},{4,8},{5,9},{6,10},{7,11},{8,4},{9,5},... | collective-permute-start | bytes 393224 | tf_op jit(solution)/shard_map/ppermute | solution.py:377
  58.9 6.3 %collective-permute-start.28 = (bf16[128,512]{1,0:T(8,128)(2,1)S(1)}, bf16[128,512]{1,0:T(8,128)(2,1)S(1)}, u32[]{:S(2)}, u32[]{:S(2)}) collective-permute-start(bf16[128,512]{1,0:T(8,128)(2,1)S(1)} %get-tuple-element.184), channel_id=1, source_target_pairs={{0,4},{1,5},{4,8},{5,9},{8,12},{9,13},{12,14},{13,15},{14,10},{15,... | collective-permute-start | bytes 393224 | tf_op jit(solution)/shard_map/ppermute | solution.py:374
  61.9 6.2 %collective-permute-start.32 = (bf16[128,512]{1,0:T(8,128)(2,1)S(1)}, bf16[128,512]{1,0:T(8,128)(2,1)S(1)}, u32[]{:S(2)}, u32[]{:S(2)}) collective-permute-start(bf16[128,512]{1,0:T(8,128)(2,1)S(1)} %get-tuple-element.188), channel_id=1, source_target_pairs={{0,2},{1,3},{4,0},{5,1},{8,4},{9,5},{12,8},{13,9},{14,12},{15,13},... | collective-permute-start | bytes 393224 | tf_op jit(solution)/shard_map/ppermute | solution.py:374
  65.2 5.6 %collective-permute-start.29 = (bf16[128,512]{1,0:T(8,128)(2,1)S(1)}, bf16[128,512]{1,0:T(8,128)(2,1)S(1)}, u32[]{:S(2)}, u32[]{:S(2)}) collective-permute-start(bf16[128,512]{1,0:T(8,128)(2,1)S(1)} %add_convert_fusion.5), channel_id=1, source_target_pairs={{0,4},{1,5},{4,8},{5,9},{8,12},{9,13},{12,14},{13,15},{14,10},{15,... | collective-permute-start | bytes 393224 | tf_op jit(solution)/shard_map/ppermute | solution.py:374
  (12 other events, 50.7 us)

commit v9 on v8

--- a/solution.py
+++ b/solution.py
@@ -434,7 +434,9 @@
 
     send_first, send_others = sends
     other_first = swap(send_first, 1)
-    send_others, owns, other_query, close = lax.optimization_barrier((send_others, owns, other_query, close))
+    send_others, owns, other_query, close[:-1] = lax.optimization_barrier(
+        (send_others, owns, other_query, close[:-1])
+    )
     other_others = swap(send_others, 1)
     state = begin([pieces[0], *close], owns, query, other_query)
     w_out, state = lax.optimization_barrier((w_out, state))

time: 81.9 us -> 81.9 us (level)
  no operation moved by 1% of the time
where the time goes in v9:
time: 81.9 us; the launch traced here: 81.6 us
  starting transfers between devices  33.5 us (41%)
  waiting for transfers between devices  24 us (29%)
  Pallas kernels  23.1 us (28%)
  other arithmetic  0.84 us (1%)
    ppermute x14, starting transfers between devices, around(): return lax.ppermute(value, 'seq', pairs)  18.9 us
    ppermute x14, waiting for transfers between devices, around(): return lax.ppermute(value, 'seq', pairs)  18.4 us
    ppermute x21, starting transfers between devices, swap(): return lax.ppermute(value, 'seq', [(i, i ^ bits) for i in range(size)])  14.5 us
    ppermute x21, waiting for transfers between devices, swap(): return lax.ppermute(value, 'seq', [(i, i ^ bits) for i in range(size)])  5.56 us
    pallas_call x1, Pallas kernels, project(): pl.pallas_call(functools.partial(project_kernel, offsets, chips, rows), o...  4.92 us
    pallas_call x2, Pallas kernels, half(): pl.pallas_call(functools.partial(half_kernel, groups, chips, width), out_...  4.55 us
    pallas_call x2, Pallas kernels, fetch(): pl.pallas_call(functools.partial(fetch_kernel, start, size), out_shape=pl...  4.39 us
    pallas_call x1, Pallas kernels, begin(): pl.pallas_call(functools.partial(begin_kernel, count, len(owns), heads),...  3.62 us
  transfers between devices with their start and end apart: 35, of which 19 were waited for; matrix products, arithmetic and copies ran while one was open for 0% of the time, Pallas kernels for 27%

profile of v9, /device:TPU:0, one launch (start us, length us, event | category | flops | bytes accessed | tf_op | source)
XLA Modules:
  0.0 81.6 jit_solution(5701043089494616896)
XLA Ops:
  1.0 3.1 %collective-permute-start = (bf16[144,512]{1,0:T(8,128)(2,1)S(1)}, bf16[144,512]{1,0:T(8,128)(2,1)S(1)}, u32[]{:S(2)}, u32[]{:S(2)}) collective-permute-start(bf16[144,512]{1,0:T(8,128)(2,1)S(1)} %pack.1.refs_0_), channel_id=1, source_target_pairs={{0,4},{1,5},{4,8},{5,9},{8,12},{9,13},{12,14},{13,15},{14,10},{15,... | collective-permute-start | bytes 442376 | tf_op jit(solution)/shard_map/ppermute | solution.py:374
  4.0 2.2 %fetch.2.refs_16_ = bf16[256,8192]{1,0:T(8,128)(2,1)S(1)} custom-call(bf16[512,8192]{1,0:T(8,128)(2,1)} %source.1), custom_call_target="tpu_custom_call" | custom-call | bytes 8388608 | tf_op jit(solution)/shard_map/fetch/pallas_call | solution.py:139
  7.8 1.8 %collective-permute-start.1 = (bf16[144,512]{1,0:T(8,128)(2,1)S(1)}, bf16[144,512]{1,0:T(8,128)(2,1)S(1)}, u32[]{:S(2)}, u32[]{:S(2)}) collective-permute-start(bf16[144,512]{1,0:T(8,128)(2,1)S(1)} %collective-permute-done.refs_2_), channel_id=1, source_target_pairs={{0,4},{1,5},{4,8},{5,9},{8,12},{9,13},{12,14},{13,15},{14,10},{15,... | collective-permute-start | bytes 442376 | tf_op jit(solution)/shard_map/ppermute | solution.py:374
  9.9 2.2 %fetch.3.refs_17_ = bf16[256,8192]{1,0:T(8,128)(2,1)S(1)} custom-call(bf16[512,8192]{1,0:T(8,128)(2,1)} %source.1), custom_call_target="tpu_custom_call" | custom-call | bytes 8388608 | tf_op jit(solution)/shard_map/fetch/pallas_call | solution.py:139
  13.0 1.8 %collective-permute-start.2 = (bf16[144,512]{1,0:T(8,128)(2,1)S(1)}, bf16[144,512]{1,0:T(8,128)(2,1)S(1)}, u32[]{:S(2)}, u32[]{:S(2)}) collective-permute-start(bf16[144,512]{1,0:T(8,128)(2,1)S(1)} %collective-permute-done.1.refs_6_), channel_id=1, source_target_pairs={{0,4},{1,5},{4,8},{5,9},{8,12},{9,13},{12,14},{13,15},{14,10},{15,... | collective-permute-start | bytes 442376 | tf_op jit(solution)/shard_map/ppermute | solution.py:374
  15.3 2.0 %collective-permute-done.15.refs_8_ = bf16[144,512]{1,0:T(8,128)(2,1)S(1)} collective-permute-done((bf16[144,512]{1,0:T(8,128)(2,1)S(1)}, bf16[144,512]{1,0:T(8,128)(2,1)S(1)}, u32[]{:S(2)}, u32[]{:S(2)}) %collective-permute-start.15) | collective-permute-done | bytes 147488 | tf_op jit(solution)/shard_map/ppermute | solution.py:374
  18.1 1.8 %collective-permute-start.20 = (bf16[144,512]{1,0:T(8,128)(2,1)S(1)}, bf16[144,512]{1,0:T(8,128)(2,1)S(1)}, u32[]{:S(2)}, u32[]{:S(2)}) collective-permute-start(bf16[144,512]{1,0:T(8,128)(2,1)S(1)} %collective-permute-done.2.refs_10_), channel_id=1, source_target_pairs={{0,4},{1,5},{4,8},{5,9},{8,12},{9,13},{12,14},{13,15},{14,10},{15,... | collective-permute-start | bytes 442376 | tf_op jit(solution)/shard_map/ppermute | solution.py:374
  20.5 2.0 %collective-permute-done.18.refs_12_ = bf16[144,512]{1,0:T(8,128)(2,1)S(1)} collective-permute-done((bf16[144,512]{1,0:T(8,128)(2,1)S(1)}, bf16[144,512]{1,0:T(8,128)(2,1)S(1)}, u32[]{:S(2)}, u32[]{:S(2)}) %collective-permute-start.18) | collective-permute-done | bytes 147488 | tf_op jit(solution)/shard_map/ppermute | solution.py:374
  23.3 2.8 %collective-permute-start.3 = (bf16[2,256,128]{2,1,0:T(8,128)(2,1)S(1)}, bf16[2,256,128]{2,1,0:T(8,128)(2,1)S(1)}, u32[]{:S(2)}, u32[]{:S(2)}) collective-permute-start(bf16[2,256,128]{2,1,0:T(8,128)(2,1)S(1)} %get-tuple-element.127), channel_id=1, source_target_pairs={{0,8},{1,9},{2,10},{3,11},{4,12},{5,13},{6,14},{7,15},{8,0},{9,1},... | collective-permute-start | bytes 393224 | tf_op jit(solution)/shard_map/ppermute | solution.py:377
  29.1 1.7 %collective-permute-start.7 = (bf16[2,256,128]{2,1,0:T(8,128)(2,1)S(1)}, bf16[2,256,128]{2,1,0:T(8,128)(2,1)S(1)}, u32[]{:S(2)}, u32[]{:S(2)}) collective-permute-start(bf16[2,256,128]{2,1,0:T(8,128)(2,1)S(1)} %get-tuple-element.124), channel_id=1, source_target_pairs={{0,2},{1,3},{2,0},{3,1},{4,6},{5,7},{6,4},{7,5},{8,10},{9,11},{10,... | collective-permute-start | bytes 393224 | tf_op jit(solution)/shard_map/ppermute | solution.py:377
  30.9 4.9 %project.1 = (bf16[128,512]{1,0:T(8,128)(2,1)S(1)}, bf16[128,128]{1,0:T(8,128)(2,1)S(1)}) custom-call(bf16[144,512]{1,0:T(8,128)(2,1)S(1)} %pack.1.refs_0_, bf16[144,512]{1,0:T(8,128)(2,1)S(1)} %collective-permute-done.10.refs_1_, bf16[144,512]{1,0:T(8,128)(2,1)S(1)} %collective-permute-done.refs_2_, bf16[144,512]{1,0:T(8,128)(2,1)S(1)} %collective-permute-done.11.refs_3_, ...), custom_call_target="tpu_custom_call" | custom-call | tf_op jit(solution)/shard_map/project/pallas_call | solution.py:192
  35.8 2.3 %half.2 = (bf16[2,512,512]{2,1,0:T(8,128)(2,1)S(1)}, bf16[6,512,512]{2,1,0:T(8,128)(2,1)S(1)}) custom-call(bf16[512,8192]{1,0:T(8,128)(2,1)} %w_out.1), custom_call_target="tpu_custom_call" | custom-call | tf_op jit(solution)/shard_map/half/pallas_call | solution.py:121
  38.2 1.6 %collective-permute-done.4.refs_2_ = bf16[2,256,128]{2,1,0:T(8,128)(2,1)S(1)} collective-permute-done((bf16[2,256,128]{2,1,0:T(8,128)(2,1)S(1)}, bf16[2,256,128]{2,1,0:T(8,128)(2,1)S(1)}, u32[]{:S(2)}, u32[]{:S(2)}) %collective-permute-start.4) | collective-permute-done | bytes 131104 | tf_op jit(solution)/shard_map/ppermute | solution.py:377
  41.5 4.6 %collective-permute-start.8 = (bf16[2,256,128]{2,1,0:T(8,128)(2,1)S(1)}, bf16[2,256,128]{2,1,0:T(8,128)(2,1)S(1)}, u32[]{:S(2)}, u32[]{:S(2)}) collective-permute-start(bf16[2,256,128]{2,1,0:T(8,128)(2,1)S(1)} %get-tuple-element.131), channel_id=1, source_target_pairs={{0,14},{1,15},{2,12},{3,13},{4,10},{5,11},{6,8},{7,9},{8,6},{9,7},... | collective-permute-start | bytes 393224 | tf_op jit(solution)/shard_map/ppermute | solution.py:377
  46.1 3.6 %begin.1 = (bf16[1024,128]{1,0:T(8,128)(2,1)S(1)}, f32[1024,128]{1,0:T(8,128)S(1)}, f32[1024,128]{1,0:T(8,128)S(1)}, f32[1024,128]{1,0:T(8,128)S(1)}) custom-call(bf16[2,256,128]{2,1,0:T(8,128)(2,1)S(1)} %get-tuple-element.141.refs_0_, bf16[2,256,128]{2,1,0:T(8,128)(2,1)S(1)} %collective-permute-done.3.refs_1_, ...), custom_call_target="tpu_custom_call" | custom-call | flops 1 | bytes 1 | tf_op jit(solution)/shard_map/begin/pallas_call | solution.py:266
  49.8 2.3 %half.3 = (bf16[2,512,512]{2,1,0:T(8,128)(2,1)S(1)}, bf16[6,512,512]{2,1,0:T(8,128)(2,1)S(1)}) custom-call(bf16[512,8192]{1,0:T(8,128)(2,1)} %w_out.1), custom_call_target="tpu_custom_call" | custom-call | tf_op jit(solution)/shard_map/half/pallas_call | solution.py:121
  58.9 3.0 %collective-permute-start.28 = (bf16[128,512]{1,0:T(8,128)(2,1)S(1)}, bf16[128,512]{1,0:T(8,128)(2,1)S(1)}, u32[]{:S(2)}, u32[]{:S(2)}) collective-permute-start(bf16[128,512]{1,0:T(8,128)(2,1)S(1)} %get-tuple-element.182), channel_id=1, source_target_pairs={{0,4},{1,5},{4,8},{5,9},{8,12},{9,13},{12,14},{13,15},{14,10},{15,... | collective-permute-start | bytes 393224 | tf_op jit(solution)/shard_map/ppermute | solution.py:374
  62.9 2.3 %collective-permute-done.28 = bf16[128,512]{1,0:T(8,128)(2,1)S(1)} collective-permute-done((bf16[128,512]{1,0:T(8,128)(2,1)S(1)}, bf16[128,512]{1,0:T(8,128)(2,1)S(1)}, u32[]{:S(2)}, u32[]{:S(2)}) %collective-permute-start.28) | collective-permute-done | bytes 131104 | tf_op jit(solution)/shard_map/ppermute | solution.py:374
  65.2 2.5 %collective-permute-start.29 = (bf16[128,512]{1,0:T(8,128)(2,1)S(1)}, bf16[128,512]{1,0:T(8,128)(2,1)S(1)}, u32[]{:S(2)}, u32[]{:S(2)}) collective-permute-start(bf16[128,512]{1,0:T(8,128)(2,1)S(1)} %add_convert_fusion.5), channel_id=1, source_target_pairs={{0,4},{1,5},{4,8},{5,9},{8,12},{9,13},{12,14},{13,15},{14,10},{15,... | collective-permute-start | bytes 393224 | tf_op jit(solution)/shard_map/ppermute | solution.py:374
  68.2 2.5 %collective-permute-done.29 = bf16[128,512]{1,0:T(8,128)(2,1)S(1)} collective-permute-done((bf16[128,512]{1,0:T(8,128)(2,1)S(1)}, bf16[128,512]{1,0:T(8,128)(2,1)S(1)}, u32[]{:S(2)}, u32[]{:S(2)}) %collective-permute-start.29) | collective-permute-done | bytes 131104 | tf_op jit(solution)/shard_map/ppermute | solution.py:374
  70.8 2.0 %collective-permute-start.30 = (bf16[128,512]{1,0:T(8,128)(2,1)S(1)}, bf16[128,512]{1,0:T(8,128)(2,1)S(1)}, u32[]{:S(2)}, u32[]{:S(2)}) collective-permute-start(bf16[128,512]{1,0:T(8,128)(2,1)S(1)} %add_convert_fusion.4), channel_id=1, source_target_pairs={{0,4},{1,5},{4,8},{5,9},{8,12},{9,13},{12,14},{13,15},{14,10},{15,... | collective-permute-start | bytes 393224 | tf_op jit(solution)/shard_map/ppermute | solution.py:374
  73.6 2.3 %collective-permute-done.30 = bf16[128,512]{1,0:T(8,128)(2,1)S(1)} collective-permute-done((bf16[128,512]{1,0:T(8,128)(2,1)S(1)}, bf16[128,512]{1,0:T(8,128)(2,1)S(1)}, u32[]{:S(2)}, u32[]{:S(2)}) %collective-permute-start.30) | collective-permute-done | bytes 131104 | tf_op jit(solution)/shard_map/ppermute | solution.py:374
  75.9 2.0 %collective-permute-start.31 = (bf16[128,512]{1,0:T(8,128)(2,1)S(1)}, bf16[128,512]{1,0:T(8,128)(2,1)S(1)}, u32[]{:S(2)}, u32[]{:S(2)}) collective-permute-start(bf16[128,512]{1,0:T(8,128)(2,1)S(1)} %add_convert_fusion.3), channel_id=1, source_target_pairs={{0,4},{1,5},{4,8},{5,9},{8,12},{9,13},{12,14},{13,15},{14,10},{15,... | collective-permute-start | bytes 393224 | tf_op jit(solution)/shard_map/ppermute | solution.py:374
  78.3 2.6 %collective-permute-done.31 = bf16[128,512]{1,0:T(8,128)(2,1)S(1)} collective-permute-done((bf16[128,512]{1,0:T(8,128)(2,1)S(1)}, bf16[128,512]{1,0:T(8,128)(2,1)S(1)}, u32[]{:S(2)}, u32[]{:S(2)}) %collective-permute-start.31) | collective-permute-done | bytes 131104 | tf_op jit(solution)/shard_map/ppermute | solution.py:374
  (66 shorter events, 21.4 us)
Async XLA Ops:
  1.0 6.9 %collective-permute-start = (bf16[144,512]{1,0:T(8,128)(2,1)S(1)}, bf16[144,512]{1,0:T(8,128)(2,1)S(1)}, u32[]{:S(2)}, u32[]{:S(2)}) collective-permute-start(bf16[144,512]{1,0:T(8,128)(2,1)S(1)} %pack.1.refs_0_), channel_id=1, source_target_pairs={{0,4},{1,5},{4,8},{5,9},{8,12},{9,13},{12,14},{13,15},{14,10},{15,... | collective-permute-start | bytes 442376 | tf_op jit(solution)/shard_map/ppermute | solution.py:374
  4.0 8.1 %collective-permute-start.12 = (bf16[144,512]{1,0:T(8,128)(2,1)S(1)}, bf16[144,512]{1,0:T(8,128)(2,1)S(1)}, u32[]{:S(2)}, u32[]{:S(2)}) collective-permute-start(bf16[144,512]{1,0:T(8,128)(2,1)S(1)} %pack.1.refs_0_), channel_id=1, source_target_pairs={{0,2},{1,3},{4,0},{5,1},{8,4},{9,5},{12,8},{13,9},{14,12},{15,13},... | collective-permute-start | bytes 442376 | tf_op jit(solution)/shard_map/ppermute | solution.py:374
  12.1 5.2 %collective-permute-start.15 = (bf16[144,512]{1,0:T(8,128)(2,1)S(1)}, bf16[144,512]{1,0:T(8,128)(2,1)S(1)}, u32[]{:S(2)}, u32[]{:S(2)}) collective-permute-start(bf16[144,512]{1,0:T(8,128)(2,1)S(1)} %collective-permute-done.12.refs_4_), channel_id=1, source_target_pairs={{0,2},{1,3},{4,0},{5,1},{8,4},{9,5},{12,8},{13,9},{14,12},{15,13},... | collective-permute-start | bytes 442376 | tf_op jit(solution)/shard_map/ppermute | solution.py:374
  13.0 5.1 %collective-permute-start.2 = (bf16[144,512]{1,0:T(8,128)(2,1)S(1)}, bf16[144,512]{1,0:T(8,128)(2,1)S(1)}, u32[]{:S(2)}, u32[]{:S(2)}) collective-permute-start(bf16[144,512]{1,0:T(8,128)(2,1)S(1)} %collective-permute-done.1.refs_6_), channel_id=1, source_target_pairs={{0,4},{1,5},{4,8},{5,9},{8,12},{9,13},{12,14},{13,15},{14,10},{15,... | collective-permute-start | bytes 442376 | tf_op jit(solution)/shard_map/ppermute | solution.py:374
  14.8 5.1 %collective-permute-start.10 = (bf16[144,512]{1,0:T(8,128)(2,1)S(1)}, bf16[144,512]{1,0:T(8,128)(2,1)S(1)}, u32[]{:S(2)}, u32[]{:S(2)}) collective-permute-start(bf16[144,512]{1,0:T(8,128)(2,1)S(1)} %pack.1.refs_0_), channel_id=1, source_target_pairs={{0,1},{1,0},{2,3},{3,2},{4,5},{5,4},{6,7},{7,6},{8,9},{9,8},{10,11... | collective-permute-start | bytes 442376 | tf_op jit(solution)/shard_map/ppermute | solution.py:377
  14.8 5.1 %collective-permute-start.11 = (bf16[144,512]{1,0:T(8,128)(2,1)S(1)}, bf16[144,512]{1,0:T(8,128)(2,1)S(1)}, u32[]{:S(2)}, u32[]{:S(2)}) collective-permute-start(bf16[144,512]{1,0:T(8,128)(2,1)S(1)} %collective-permute-done.refs_2_), channel_id=1, source_target_pairs={{0,1},{1,0},{2,3},{3,2},{4,5},{5,4},{6,7},{7,6},{8,9},{9,8},{10,11... | collective-permute-start | bytes 442376 | tf_op jit(solution)/shard_map/ppermute | solution.py:377
  15.3 5.2 %collective-permute-start.13 = (bf16[144,512]{1,0:T(8,128)(2,1)S(1)}, bf16[144,512]{1,0:T(8,128)(2,1)S(1)}, u32[]{:S(2)}, u32[]{:S(2)}) collective-permute-start(bf16[144,512]{1,0:T(8,128)(2,1)S(1)} %collective-permute-done.12.refs_4_), channel_id=1, source_target_pairs={{0,1},{1,0},{2,3},{3,2},{4,5},{5,4},{6,7},{7,6},{8,9},{9,8},{10,11... | collective-permute-start | bytes 442376 | tf_op jit(solution)/shard_map/ppermute | solution.py:377
  18.1 5.1 %collective-permute-start.20 = (bf16[144,512]{1,0:T(8,128)(2,1)S(1)}, bf16[144,512]{1,0:T(8,128)(2,1)S(1)}, u32[]{:S(2)}, u32[]{:S(2)}) collective-permute-start(bf16[144,512]{1,0:T(8,128)(2,1)S(1)} %collective-permute-done.2.refs_10_), channel_id=1, source_target_pairs={{0,4},{1,5},{4,8},{5,9},{8,12},{9,13},{12,14},{13,15},{14,10},{15,... | collective-permute-start | bytes 442376 | tf_op jit(solution)/shard_map/ppermute | solution.py:374
  19.9 6.2 %collective-permute-start.16 = (bf16[144,512]{1,0:T(8,128)(2,1)S(1)}, bf16[144,512]{1,0:T(8,128)(2,1)S(1)}, u32[]{:S(2)}, u32[]{:S(2)}) collective-permute-start(bf16[144,512]{1,0:T(8,128)(2,1)S(1)} %collective-permute-done.15.refs_8_), channel_id=1, source_target_pairs={{0,1},{1,0},{2,3},{3,2},{4,5},{5,4},{6,7},{7,6},{8,9},{9,8},{10,11... | collective-permute-start | bytes 442376 | tf_op jit(solution)/shard_map/ppermute | solution.py:377
  20.4 6.9 %collective-permute-start.17 = (bf16[144,512]{1,0:T(8,128)(2,1)S(1)}, bf16[144,512]{1,0:T(8,128)(2,1)S(1)}, u32[]{:S(2)}, u32[]{:S(2)}) collective-permute-start(bf16[144,512]{1,0:T(8,128)(2,1)S(1)} %collective-permute-done.2.refs_10_), channel_id=1, source_target_pairs={{0,1},{1,0},{2,3},{3,2},{4,5},{5,4},{6,7},{7,6},{8,9},{9,8},{10,11... | collective-permute-start | bytes 442376 | tf_op jit(solution)/shard_map/ppermute | solution.py:377
  22.5 6.4 %collective-permute-start.19 = (bf16[144,512]{1,0:T(8,128)(2,1)S(1)}, bf16[144,512]{1,0:T(8,128)(2,1)S(1)}, u32[]{:S(2)}, u32[]{:S(2)}) collective-permute-start(bf16[144,512]{1,0:T(8,128)(2,1)S(1)} %collective-permute-done.18.refs_12_), channel_id=1, source_target_pairs={{0,1},{1,0},{2,3},{3,2},{4,5},{5,4},{6,7},{7,6},{8,9},{9,8},{10,11... | collective-permute-start | bytes 442376 | tf_op jit(solution)/shard_map/ppermute | solution.py:377
  23.3 5.9 %collective-permute-start.21 = (bf16[144,512]{1,0:T(8,128)(2,1)S(1)}, bf16[144,512]{1,0:T(8,128)(2,1)S(1)}, u32[]{:S(2)}, u32[]{:S(2)}) collective-permute-start(bf16[144,512]{1,0:T(8,128)(2,1)S(1)} %collective-permute-done.20.refs_14_), channel_id=1, source_target_pairs={{0,1},{1,0},{2,3},{3,2},{4,5},{5,4},{6,7},{7,6},{8,9},{9,8},{10,11... | collective-permute-start | bytes 442376 | tf_op jit(solution)/shard_map/ppermute | solution.py:377
  23.3 14.8 %collective-permute-start.3 = (bf16[2,256,128]{2,1,0:T(8,128)(2,1)S(1)}, bf16[2,256,128]{2,1,0:T(8,128)(2,1)S(1)}, u32[]{:S(2)}, u32[]{:S(2)}) collective-permute-start(bf16[2,256,128]{2,1,0:T(8,128)(2,1)S(1)} %get-tuple-element.127), channel_id=1, source_target_pairs={{0,8},{1,9},{2,10},{3,11},{4,12},{5,13},{6,14},{7,15},{8,0},{9,1},... | collective-permute-start | bytes 393224 | tf_op jit(solution)/shard_map/ppermute | solution.py:377
  26.1 13.7 %collective-permute-start.4 = (bf16[2,256,128]{2,1,0:T(8,128)(2,1)S(1)}, bf16[2,256,128]{2,1,0:T(8,128)(2,1)S(1)}, u32[]{:S(2)}, u32[]{:S(2)}) collective-permute-start(bf16[2,256,128]{2,1,0:T(8,128)(2,1)S(1)} %get-tuple-element.128), channel_id=1, source_target_pairs={{0,10},{1,11},{2,8},{3,9},{4,14},{5,15},{6,12},{7,13},{8,2},{9,3},... | collective-permute-start | bytes 393224 | tf_op jit(solution)/shard_map/ppermute | solution.py:377
  27.4 12.4 %collective-permute-start.5 = (bf16[2,256,128]{2,1,0:T(8,128)(2,1)S(1)}, bf16[2,256,128]{2,1,0:T(8,128)(2,1)S(1)}, u32[]{:S(2)}, u32[]{:S(2)}) collective-permute-start(bf16[2,256,128]{2,1,0:T(8,128)(2,1)S(1)} %get-tuple-element.126), channel_id=1, source_target_pairs={{0,6},{1,7},{2,4},{3,5},{4,2},{5,3},{6,0},{7,1},{8,14},{9,15},{10,... | collective-permute-start | bytes 393224 | tf_op jit(solution)/shard_map/ppermute | solution.py:377
  28.9 11.1 %collective-permute-start.6 = (bf16[2,256,128]{2,1,0:T(8,128)(2,1)S(1)}, bf16[2,256,128]{2,1,0:T(8,128)(2,1)S(1)}, u32[]{:S(2)}, u32[]{:S(2)}) collective-permute-start(bf16[2,256,128]{2,1,0:T(8,128)(2,1)S(1)} %get-tuple-element.125), channel_id=1, source_target_pairs={{0,4},{1,5},{2,6},{3,7},{4,0},{5,1},{6,2},{7,3},{8,12},{9,13},{10,... | collective-permute-start | bytes 393224 | tf_op jit(solution)/shard_map/ppermute | solution.py:377
  29.1 10.9 %collective-permute-start.7 = (bf16[2,256,128]{2,1,0:T(8,128)(2,1)S(1)}, bf16[2,256,128]{2,1,0:T(8,128)(2,1)S(1)}, u32[]{:S(2)}, u32[]{:S(2)}) collective-permute-start(bf16[2,256,128]{2,1,0:T(8,128)(2,1)S(1)} %get-tuple-element.124), channel_id=1, source_target_pairs={{0,2},{1,3},{2,0},{3,1},{4,6},{5,7},{6,4},{7,5},{8,10},{9,11},{10,... | collective-permute-start | bytes 393224 | tf_op jit(solution)/shard_map/ppermute | solution.py:377
  41.0 20.9 %collective-permute-start.27 = (bf16[6,512,512]{2,1,0:T(8,128)(2,1)S(1)}, bf16[6,512,512]{2,1,0:T(8,128)(2,1)S(1)}, u32[]{:S(2)}, u32[]{:S(2)}) collective-permute-start(bf16[6,512,512]{2,1,0:T(8,128)(2,1)S(1)} %get-tuple-element.180), channel_id=1, source_target_pairs={{0,1},{1,0},{2,3},{3,2},{4,5},{5,4},{6,7},{7,6},{8,9},{9,8},{10,11... | collective-permute-start | bytes 9437192 | tf_op jit(solution)/shard_map/ppermute | solution.py:377
  41.2 16.4 %collective-permute-start.26 = (bf16[2,512,512]{2,1,0:T(8,128)(2,1)S(1)}, bf16[2,512,512]{2,1,0:T(8,128)(2,1)S(1)}, u32[]{:S(2)}, u32[]{:S(2)}) collective-permute-start(bf16[2,512,512]{2,1,0:T(8,128)(2,1)S(1)} %get-tuple-element.177), channel_id=1, source_target_pairs={{0,1},{1,0},{2,3},{3,2},{4,5},{5,4},{6,7},{7,6},{8,9},{9,8},{10,11... | collective-permute-start | bytes 3145736 | tf_op jit(solution)/shard_map/ppermute | solution.py:377
  41.5 10.6 %collective-permute-start.8 = (bf16[2,256,128]{2,1,0:T(8,128)(2,1)S(1)}, bf16[2,256,128]{2,1,0:T(8,128)(2,1)S(1)}, u32[]{:S(2)}, u32[]{:S(2)}) collective-permute-start(bf16[2,256,128]{2,1,0:T(8,128)(2,1)S(1)} %get-tuple-element.131), channel_id=1, source_target_pairs={{0,14},{1,15},{2,12},{3,13},{4,10},{5,11},{6,8},{7,9},{8,6},{9,7},... | collective-permute-start | bytes 393224 | tf_op jit(solution)/shard_map/ppermute | solution.py:377
  46.1 7.1 %collective-permute-start.9 = (bf16[2,256,128]{2,1,0:T(8,128)(2,1)S(1)}, bf16[2,256,128]{2,1,0:T(8,128)(2,1)S(1)}, u32[]{:S(2)}, u32[]{:S(2)}) collective-permute-start(bf16[2,256,128]{2,1,0:T(8,128)(2,1)S(1)} %get-tuple-element.132), channel_id=1, source_target_pairs={{0,12},{1,13},{2,14},{3,15},{4,8},{5,9},{6,10},{7,11},{8,4},{9,5},... | collective-permute-start | bytes 393224 | tf_op jit(solution)/shard_map/ppermute | solution.py:377
  58.9 6.3 %collective-permute-start.28 = (bf16[128,512]{1,0:T(8,128)(2,1)S(1)}, bf16[128,512]{1,0:T(8,128)(2,1)S(1)}, u32[]{:S(2)}, u32[]{:S(2)}) collective-permute-start(bf16[128,512]{1,0:T(8,128)(2,1)S(1)} %get-tuple-element.182), channel_id=1, source_target_pairs={{0,4},{1,5},{4,8},{5,9},{8,12},{9,13},{12,14},{13,15},{14,10},{15,... | collective-permute-start | bytes 393224 | tf_op jit(solution)/shard_map/ppermute | solution.py:374
  61.9 6.2 %collective-permute-start.32 = (bf16[128,512]{1,0:T(8,128)(2,1)S(1)}, bf16[128,512]{1,0:T(8,128)(2,1)S(1)}, u32[]{:S(2)}, u32[]{:S(2)}) collective-permute-start(bf16[128,512]{1,0:T(8,128)(2,1)S(1)} %get-tuple-element.186), channel_id=1, source_target_pairs={{0,2},{1,3},{4,0},{5,1},{8,4},{9,5},{12,8},{13,9},{14,12},{15,13},... | collective-permute-start | bytes 393224 | tf_op jit(solution)/shard_map/ppermute | solution.py:374
  65.2 5.6 %collective-permute-start.29 = (bf16[128,512]{1,0:T(8,128)(2,1)S(1)}, bf16[128,512]{1,0:T(8,128)(2,1)S(1)}, u32[]{:S(2)}, u32[]{:S(2)}) collective-permute-start(bf16[128,512]{1,0:T(8,128)(2,1)S(1)} %add_convert_fusion.5), channel_id=1, source_target_pairs={{0,4},{1,5},{4,8},{5,9},{8,12},{9,13},{12,14},{13,15},{14,10},{15,... | collective-permute-start | bytes 393224 | tf_op jit(solution)/shard_map/ppermute | solution.py:374
  (12 other events, 50.7 us)
